TPU v7x, 128 devices: a whole 4x4x4 slice. The times are simulated.
128 devices in a mesh: dp: 16 (over y, z), ulysses: 8 (over x, core).
Axes of the slice: x: 4, y: 4, z: 4, core: 2. Of those that a mesh axis runs over, the one named last changes fastest.
Arguments:
- query_vectors: bfloat16 [32768, 3072], P(('dp', 'ulysses')), may hold values from -20 to 20
- key_vectors: bfloat16 [32768, 3072], P(('dp', 'ulysses')), may hold values from -20 to 20
- value_vectors: bfloat16 [32768, 3072], P(('dp', 'ulysses')), may hold values from -6 to 6
- query_tangent: bfloat16 [32768, 3072], P(('dp', 'ulysses')), may hold values from -6 to 6
- key_tangent: bfloat16 [32768, 3072], P(('dp', 'ulysses')), may hold values from -6 to 6
- value_tangent: bfloat16 [32768, 3072], P(('dp', 'ulysses')), may hold values from -6 to 6
- out_weight: bfloat16 [3072, 3072], P(('dp', 'ulysses')), may hold values from -0.3125 to 0.3125
- frame_counts: int32 [32], replicated, may hold values from 1 to 8, as said below
- token_offsets: int32 [32], replicated, may hold values from 0 to 1024
- video_group: int32 [32], replicated, may hold values from 0 to 15
Outputs:
- block_out: bfloat16 [32768, 3072], P(('dp', 'ulysses'))
- block_tangent: bfloat16 [32768, 3072], P(('dp', 'ulysses'))
Inputs may be any that keep to these rules, and one draw needn't show every extreme that they name: `frame_counts`: each data group holds exactly two videos packed from its first slot: one at offset 0, the other starting where that one ends; a video has 128 tokens a frame, and one video has exactly 8 frames.
All inputs are finite; a program needn't handle non-finite values.
Results may differ from a plain program's by a relative error of at most 0.0057.
Values may be sent and summed in bfloat16 or wider, within the bound.
No kernel may reach another device: no remote copies, remote signals or barrier semaphores. Data moves between devices by JAX's collectives and lax.ppermute only.
A program may use at most 128 MiB of HBM per device.

v0:
```python
import math

import jax
import jax.numpy as jnp
from jax import lax
from jax.sharding import PartitionSpec as P

HEAD_DIM = 128
FRAME_TOKENS = 128


masked_value = -1e30


def segment_ids(frame_counts, token_offsets, video_group, group_index, seq_length):
    position = jnp.arange(seq_length, dtype=jnp.int32)[:, None]
    starts = token_offsets[None, :]
    member = (
        (video_group[None, :] == group_index)
        & (position >= starts)
        & (position < starts + FRAME_TOKENS * frame_counts[None, :])
    )
    video_labels = jnp.arange(1, frame_counts.shape[0] + 1, dtype=jnp.int32)[None, :]
    return jnp.sum(jnp.where(member, video_labels, 0), axis=1)


def block_attention(
    query_rows,
    keys_head,
    values_head,
    tquery_rows,
    tkeys_head,
    tvalues_head,
    row_labels,
    key_labels,
):
    scale_factor = 1.0 / math.sqrt(query_rows.shape[-1])
    scores = jnp.dot(query_rows, keys_head.T, preferred_element_type=jnp.float32) * scale_factor
    tangent_scores = (
        jnp.dot(tquery_rows, keys_head.T, preferred_element_type=jnp.float32)
        + jnp.dot(query_rows, tkeys_head.T, preferred_element_type=jnp.float32)
    ) * scale_factor
    allowed = (row_labels[:, None] == key_labels[None, :]) & (row_labels[:, None] > 0)
    scores = jnp.where(allowed, scores, masked_value)
    row_max = jnp.max(scores, axis=1, keepdims=True)
    weights = jnp.exp(scores - row_max)
    probabilities = weights / jnp.sum(weights, axis=1, keepdims=True)
    probs_low = probabilities.astype(jnp.bfloat16)
    primal_out = jnp.dot(probs_low, values_head, preferred_element_type=jnp.float32)
    mean_tangent = jnp.sum(probabilities * tangent_scores, axis=1, keepdims=True)
    tangent_probs = (probabilities * (tangent_scores - mean_tangent)).astype(jnp.bfloat16)
    tangent_out = jnp.dot(tangent_probs, values_head, preferred_element_type=jnp.float32) + jnp.dot(
        probs_low, tvalues_head, preferred_element_type=jnp.float32
    )
    valid_rows = (row_labels > 0)[:, None]
    return (
        jnp.where(valid_rows, primal_out, 0.0).astype(jnp.bfloat16),
        jnp.where(valid_rows, tangent_out, 0.0).astype(jnp.bfloat16),
    )


def head_attention(
    queries_head, keys_head, values_head, tqueries_head, tkeys_head, tvalues_head, token_labels
):
    seq_length = queries_head.shape[0]
    block_rows = min(512, seq_length)
    block_count = seq_length // block_rows
    query_blocks = queries_head.reshape(block_count, block_rows, -1)
    tquery_blocks = tqueries_head.reshape(block_count, block_rows, -1)
    label_blocks = token_labels.reshape(block_count, block_rows)

    def one_block(block_items):
        return block_attention(
            block_items[0],
            keys_head,
            values_head,
            block_items[1],
            tkeys_head,
            tvalues_head,
            block_items[2],
            token_labels,
        )

    primal, tangent = lax.map(one_block, (query_blocks, tquery_blocks, label_blocks))
    return (primal.reshape(seq_length, -1), tangent.reshape(seq_length, -1))


def shards(
    query_vectors,
    key_vectors,
    value_vectors,
    query_tangent,
    key_tangent,
    value_tangent,
    out_weight,
    frame_counts,
    token_offsets,
    video_group,
):
    primal_moved = (
        lax.all_to_all(query_vectors, "ulysses", split_axis=1, concat_axis=0, tiled=True),
        lax.all_to_all(key_vectors, "ulysses", split_axis=1, concat_axis=0, tiled=True),
        lax.all_to_all(value_vectors, "ulysses", split_axis=1, concat_axis=0, tiled=True),
    )
    tangent_moved = (
        lax.all_to_all(query_tangent, "ulysses", split_axis=1, concat_axis=0, tiled=True),
        lax.all_to_all(key_tangent, "ulysses", split_axis=1, concat_axis=0, tiled=True),
        lax.all_to_all(value_tangent, "ulysses", split_axis=1, concat_axis=0, tiled=True),
    )
    exchanged = tuple(primal_moved) + tuple(tangent_moved)
    seq_length = exchanged[0].shape[0]
    token_labels = segment_ids(
        frame_counts, token_offsets, video_group, lax.axis_index("dp"), seq_length
    )
    local_heads = exchanged[0].shape[1] // HEAD_DIM
    primal_parts = []
    tangent_parts = []
    for head_number in range(local_heads):
        head_slices = [
            tensor[:, head_number * HEAD_DIM : (head_number + 1) * HEAD_DIM] for tensor in exchanged
        ]
        primal_head, tangent_head = head_attention(*head_slices, token_labels)
        primal_parts.append(primal_head)
        tangent_parts.append(tangent_head)
    primal_heads = jnp.concatenate(primal_parts, axis=1)
    tangent_heads = jnp.concatenate(tangent_parts, axis=1)
    primal_seq, tangent_seq = (
        lax.all_to_all(primal_heads, "ulysses", split_axis=0, concat_axis=1, tiled=True),
        lax.all_to_all(tangent_heads, "ulysses", split_axis=0, concat_axis=1, tiled=True),
    )
    weight_piece = lax.all_gather(out_weight, ("dp", "ulysses"), axis=0, tiled=True)
    return (
        jnp.dot(primal_seq, weight_piece, preferred_element_type=jnp.float32).astype(jnp.bfloat16),
        jnp.dot(tangent_seq, weight_piece, preferred_element_type=jnp.float32).astype(jnp.bfloat16),
    )


def solution(mesh):
    return jax.shard_map(
        shards,
        mesh=mesh,
        in_specs=(
            P(("dp", "ulysses"), None),
            P(("dp", "ulysses"), None),
            P(("dp", "ulysses"), None),
            P(("dp", "ulysses"), None),
            P(("dp", "ulysses"), None),
            P(("dp", "ulysses"), None),
            P(("dp", "ulysses"), None),
            P(),
            P(),
            P(),
        ),
        out_specs=(P(("dp", "ulysses"), None), P(("dp", "ulysses"), None)),
        check_vma=False,
    )
```

profile of v0, /device:TPU:19, one launch (start us, length us, event | category | flops | bytes accessed | tf_op | source)
XLA Modules:
  0.0 397.8 jit_solution(6926787394954710784)
XLA Ops:
  10.4 5.1 %all-to-all-start = ((bf16[256,8,384]{2,0,1:T(8,128)(2,1)}), bf16[256,8,384]{2,0,1:T(8,128)(2,1)S(1)}, u32[]{:S(2)}, u32[]{:S(2)}) async-start(bf16[256,8,384]{2,0,1:T(8,128)(2,1)} %copy.49), calls=%async_computation | async-start | bytes 3145728 | tf_op jit(solution)/shard_map/all_to_all | solution.py:101
  18.9 16.3 %all-to-all-done = bf16[256,8,384]{2,0,1:T(8,128)(2,1)S(1)} async-done(((bf16[256,8,384]{2,0,1:T(8,128)(2,1)}), bf16[256,8,384]{2,0,1:T(8,128)(2,1)S(1)}, u32[]{:S(2)}, u32[]{:S(2)}) %all-to-all-start) | async-done | bytes 1572896 | tf_op jit(solution)/shard_map/all_to_all | solution.py:101
  35.2 5.5 %all-to-all-start.3 = ((bf16[256,8,384]{2,0,1:T(8,128)(2,1)}), bf16[256,8,384]{2,0,1:T(8,128)(2,1)S(1)}, u32[]{:S(2)}, u32[]{:S(2)}) async-start(bf16[256,8,384]{2,0,1:T(8,128)(2,1)} %copy.53), calls=%async_computation.3 | async-start | bytes 3145728 | tf_op jit(solution)/shard_map/all_to_all | solution.py:106
  43.4 16.9 %all-to-all-done.3 = bf16[256,8,384]{2,0,1:T(8,128)(2,1)S(1)} async-done(((bf16[256,8,384]{2,0,1:T(8,128)(2,1)}), bf16[256,8,384]{2,0,1:T(8,128)(2,1)S(1)}, u32[]{:S(2)}, u32[]{:S(2)}) %all-to-all-start.3) | async-done | bytes 1572896 | tf_op jit(solution)/shard_map/all_to_all | solution.py:106
  61.5 5.4 %all-to-all-start.1 = ((bf16[256,8,384]{2,0,1:T(8,128)(2,1)}), bf16[256,8,384]{2,0,1:T(8,128)(2,1)S(1)}, u32[]{:S(2)}, u32[]{:S(2)}) async-start(bf16[256,8,384]{2,0,1:T(8,128)(2,1)} %bitcast.218), calls=%async_computation.1 | async-start | bytes 3145728 | tf_op jit(solution)/shard_map/all_to_all | solution.py:102
  69.7 16.9 %all-to-all-done.1 = bf16[256,8,384]{2,0,1:T(8,128)(2,1)S(1)} async-done(((bf16[256,8,384]{2,0,1:T(8,128)(2,1)}), bf16[256,8,384]{2,0,1:T(8,128)(2,1)S(1)}, u32[]{:S(2)}, u32[]{:S(2)}) %all-to-all-start.1) | async-done | bytes 1572896 | tf_op jit(solution)/shard_map/all_to_all | solution.py:102
  86.6 6.3 %all-to-all-start.2 = ((bf16[256,8,384]{2,0,1:T(8,128)(2,1)}), bf16[256,8,384]{2,0,1:T(8,128)(2,1)}, u32[]{:S(2)}, u32[]{:S(2)}) async-start(bf16[256,8,384]{2,0,1:T(8,128)(2,1)} %bitcast.216), calls=%async_computation.2 | async-start | bytes 3145728 | tf_op jit(solution)/shard_map/all_to_all | solution.py:103
  96.4 16.3 %all-to-all-done.2 = bf16[256,8,384]{2,0,1:T(8,128)(2,1)} async-done(((bf16[256,8,384]{2,0,1:T(8,128)(2,1)}), bf16[256,8,384]{2,0,1:T(8,128)(2,1)}, u32[]{:S(2)}, u32[]{:S(2)}) %all-to-all-start.2) | async-done | bytes 1572896 | tf_op jit(solution)/shard_map/all_to_all | solution.py:103
  112.7 6.7 %all-to-all-start.4 = ((bf16[256,8,384]{2,0,1:T(8,128)(2,1)}), bf16[256,8,384]{2,0,1:T(8,128)(2,1)}, u32[]{:S(2)}, u32[]{:S(2)}) async-start(bf16[256,8,384]{2,0,1:T(8,128)(2,1)} %bitcast.214), calls=%async_computation.4 | async-start | bytes 3145728 | tf_op jit(solution)/shard_map/all_to_all | solution.py:107
  119.6 2.8 copy.66
  125.0 19.7 %all-to-all-done.4 = bf16[256,8,384]{2,0,1:T(8,128)(2,1)} async-done(((bf16[256,8,384]{2,0,1:T(8,128)(2,1)}), bf16[256,8,384]{2,0,1:T(8,128)(2,1)}, u32[]{:S(2)}, u32[]{:S(2)}) %all-to-all-start.4) | async-done | bytes 1572896 | tf_op jit(solution)/shard_map/all_to_all | solution.py:107
  144.6 6.9 %all-to-all-start.5 = ((bf16[256,8,384]{2,0,1:T(8,128)(2,1)}), bf16[256,8,384]{2,0,1:T(8,128)(2,1)}, u32[]{:S(2)}, u32[]{:S(2)}) async-start(bf16[256,8,384]{2,0,1:T(8,128)(2,1)} %bitcast.215), calls=%async_computation.5 | async-start | bytes 3145728 | tf_op jit(solution)/shard_map/all_to_all | solution.py:108
  156.1 3.0 fusion.78
  159.1 24.9 %all-to-all-done.5 = bf16[256,8,384]{2,0,1:T(8,128)(2,1)} async-done(((bf16[256,8,384]{2,0,1:T(8,128)(2,1)}), bf16[256,8,384]{2,0,1:T(8,128)(2,1)}, u32[]{:S(2)}, u32[]{:S(2)}) %all-to-all-start.5) | async-done | bytes 1572896 | tf_op jit(solution)/shard_map/all_to_all | solution.py:108
  188.0 43.5 %while.36 = (s32[]{:T(128)}, bf16[4,512,128]{2,1,0:T(8,128)(2,1)}, bf16[4,512,128]{2,1,0:T(8,128)(2,1)}, s32[4,512]{1,0:T(4,128)S(1)}, s32[2048]{0:T(1024)S(1)},...) while((s32[]{:T(128)}, bf16[4,512,128]{2,1,0:T(8,128)(2,1)}, ...), condition=%wide.region_5.6_spmd, body=%wide.region_1.5_spmd.sunk | while | flops 1629813760 | bytes 52595348 | solution.py:84
  192.5 2.8 multiply_reduce_fusion.6
  233.1 43.6 %while.37 = (s32[]{:T(128)}, bf16[4,512,128]{2,1,0:T(8,128)(2,1)}, bf16[4,512,128]{2,1,0:T(8,128)(2,1)}, s32[4,512]{1,0:T(4,128)S(1)}, s32[2048]{0:T(1024)S(1)},...) while((s32[]{:T(128)}, bf16[4,512,128]{2,1,0:T(8,128)(2,1)}, ...), condition=%wide.region_10.11_spmd, body=%wide.region_6.10_spmd.sunk | while | flops 1629813760 | bytes 52595348 | solution.py:84
  276.9 39.0 %while.38 = (s32[]{:T(128)}, bf16[4,512,128]{2,1,0:T(8,128)(2,1)S(1)}, bf16[4,512,128]{2,1,0:T(8,128)(2,1)S(1)}, s32[4,512]{1,0:T(4,128)S(1)}, s32[2048]{0:T(102...) while((s32[]{:T(128)}, ...), condition=%wide.region_15.16_spmd, body=%wide.region_11.15_spmd.sunk | while | flops 1629813760 | bytes 52594332 | solution.py:84
  318.3 6.4 %all-to-all-start.7 = ((bf16[8,256,384]{2,1,0:T(8,128)(2,1)}), bf16[8,256,384]{2,1,0:T(8,128)(2,1)S(1)}, u32[]{:S(2)}, u32[]{:S(2)}) async-start(bf16[8,256,384]{2,1,0:T(8,128)(2,1)} %pad_maximum_fusion.1), calls=%async_computation.7 | async-start | bytes 3145728 | tf_op jit(solution)/shard_map/all_to_all | solution.py:129
  327.2 17.1 %all-to-all-done.7 = bf16[8,256,384]{2,1,0:T(8,128)(2,1)S(1)} async-done(((bf16[8,256,384]{2,1,0:T(8,128)(2,1)}), bf16[8,256,384]{2,1,0:T(8,128)(2,1)S(1)}, u32[]{:S(2)}, u32[]{:S(2)}) %all-to-all-start.7) | async-done | bytes 1572896 | tf_op jit(solution)/shard_map/all_to_all | solution.py:129
  344.3 6.1 %all-to-all-start.6 = ((bf16[8,256,384]{2,1,0:T(8,128)(2,1)}), bf16[8,256,384]{2,1,0:T(8,128)(2,1)}, u32[]{:S(2)}, u32[]{:S(2)}) async-start(bf16[8,256,384]{2,1,0:T(8,128)(2,1)} %pad_maximum_fusion), calls=%async_computation.6 | async-start | bytes 3145728 | tf_op jit(solution)/shard_map/all_to_all | solution.py:128
  351.2 19.0 %all-to-all-done.6 = bf16[8,256,384]{2,1,0:T(8,128)(2,1)} async-done(((bf16[8,256,384]{2,1,0:T(8,128)(2,1)}), bf16[8,256,384]{2,1,0:T(8,128)(2,1)}, u32[]{:S(2)}, u32[]{:S(2)}) %all-to-all-start.6) | async-done | bytes 1572896 | tf_op jit(solution)/shard_map/all_to_all | solution.py:128
  372.0 12.9 %convolution_convert_fusion = bf16[256,3072]{1,0:T(8,128)(2,1)} fusion(bf16[256,3072]{0,1:T(8,128)(2,1)S(1)} %bitcast.209, bf16[3072,3072]{1,0:T(8,128)(2,1)} %all-gather.2.cloned.1.call-done), kind=kOutput, calls=%fused_computation.96 | convolution fusion | flops 4832624640 | bytes 22020096 | tf_op jit(solution)/shard_map/dot_general | solution.py:134
  384.8 6.1 %convolution_convert_fusion.1 = bf16[256,3072]{1,0:T(8,128)(2,1)} fusion(bf16[256,3072]{0,1:T(8,128)(2,1)S(1)} %bitcast.210, bf16[3072,3072]{1,0:T(8,128)(2,1)S(1)} %copy-done), kind=kOutput, calls=%fused_computation.97 | convolution fusion | flops 4832624640 | bytes 22020096 | tf_op jit(solution)/shard_map/dot_general | solution.py:133
  (182 shorter events, 159.7 us)
Async XLA Ops:
  10.4 24.8 %all-to-all-start = ((bf16[256,8,384]{2,0,1:T(8,128)(2,1)}), bf16[256,8,384]{2,0,1:T(8,128)(2,1)S(1)}, u32[]{:S(2)}, u32[]{:S(2)}) async-start(bf16[256,8,384]{2,0,1:T(8,128)(2,1)} %copy.49), calls=%async_computation | async-start | bytes 3145728 | tf_op jit(solution)/shard_map/all_to_all | solution.py:101
  35.2 25.1 %all-to-all-start.3 = ((bf16[256,8,384]{2,0,1:T(8,128)(2,1)}), bf16[256,8,384]{2,0,1:T(8,128)(2,1)S(1)}, u32[]{:S(2)}, u32[]{:S(2)}) async-start(bf16[256,8,384]{2,0,1:T(8,128)(2,1)} %copy.53), calls=%async_computation.3 | async-start | bytes 3145728 | tf_op jit(solution)/shard_map/all_to_all | solution.py:106
  61.5 25.1 %all-to-all-start.1 = ((bf16[256,8,384]{2,0,1:T(8,128)(2,1)}), bf16[256,8,384]{2,0,1:T(8,128)(2,1)S(1)}, u32[]{:S(2)}, u32[]{:S(2)}) async-start(bf16[256,8,384]{2,0,1:T(8,128)(2,1)} %bitcast.218), calls=%async_computation.1 | async-start | bytes 3145728 | tf_op jit(solution)/shard_map/all_to_all | solution.py:102
  86.6 26.0 %copy-start.4 = (bf16[256,8,384]{2,0,1:T(8,128)(2,1)}, bf16[256,8,384]{2,0,1:T(8,128)(2,1)S(1)}, u32[]{:S(2)}) copy-start(bf16[256,8,384]{2,0,1:T(8,128)(2,1)S(1)} %all-to-all-done.1) | copy-start | bytes 4718596
  86.6 32.7 %copy-start.13 = (s32[32]{0:T(128)S(1)}, s32[32]{0:T(128)}, u32[]{:S(2)}) copy-start(s32[32]{0:T(128)} %param.25) | copy-start | bytes 388
  86.6 32.7 %copy-start.11 = (s32[32]{0:T(128)S(1)}, s32[32]{0:T(128)}, u32[]{:S(2)}) copy-start(s32[32]{0:T(128)} %param.24) | copy-start | bytes 388
  86.6 32.7 %copy-start.12 = (s32[32]{0:T(128)S(1)}, s32[32]{0:T(128)}, u32[]{:S(2)}) copy-start(s32[32]{0:T(128)} %param.23) | copy-start | bytes 388
  86.6 26.0 %all-to-all-start.2 = ((bf16[256,8,384]{2,0,1:T(8,128)(2,1)}), bf16[256,8,384]{2,0,1:T(8,128)(2,1)}, u32[]{:S(2)}, u32[]{:S(2)}) async-start(bf16[256,8,384]{2,0,1:T(8,128)(2,1)} %bitcast.216), calls=%async_computation.2 | async-start | bytes 3145728 | tf_op jit(solution)/shard_map/all_to_all | solution.py:103
  92.9 279.0 %all-gather.2.cloned.1.call-start = ((), (), s32[]{:S(2)}) async-start(), calls=%async_computation.8 | async-start | bytes 19021824 | tf_op jit(solution)/shard_map/all_gather | solution.py:131
  112.7 32.0 %all-to-all-start.4 = ((bf16[256,8,384]{2,0,1:T(8,128)(2,1)}), bf16[256,8,384]{2,0,1:T(8,128)(2,1)}, u32[]{:S(2)}, u32[]{:S(2)}) async-start(bf16[256,8,384]{2,0,1:T(8,128)(2,1)} %bitcast.214), calls=%async_computation.4 | async-start | bytes 3145728 | tf_op jit(solution)/shard_map/all_to_all | solution.py:107
  119.3 4.4 %copy-start.6 = (bf16[256,8,384]{2,0,1:T(8,128)(2,1)S(1)}, bf16[256,8,384]{2,0,1:T(8,128)(2,1)}, u32[]{:S(2)}) copy-start(bf16[256,8,384]{2,0,1:T(8,128)(2,1)} %copy-done.5) | copy-start | bytes 4718596
  144.6 39.3 %all-to-all-start.5 = ((bf16[256,8,384]{2,0,1:T(8,128)(2,1)}), bf16[256,8,384]{2,0,1:T(8,128)(2,1)}, u32[]{:S(2)}, u32[]{:S(2)}) async-start(bf16[256,8,384]{2,0,1:T(8,128)(2,1)} %bitcast.215), calls=%async_computation.5 | async-start | bytes 3145728 | tf_op jit(solution)/shard_map/all_to_all | solution.py:108
  190.1 2.3 copy-start.10
  201.0 2.3 copy-start.10
  211.9 2.3 copy-start.10
  233.1 43.7 %copy-start.1 = (bf16[2048,128]{1,0:T(8,128)(2,1)S(1)}, bf16[2048,128]{1,0:T(8,128)(2,1)}, u32[]{:S(2)}) copy-start(bf16[2048,128]{1,0:T(8,128)(2,1)} %get-tuple-element.521) | copy-start | bytes 1572868
  233.1 43.7 %copy-start.2 = (bf16[2048,128]{1,0:T(8,128)(2,1)S(1)}, bf16[2048,128]{1,0:T(8,128)(2,1)}, u32[]{:S(2)}) copy-start(bf16[2048,128]{1,0:T(8,128)(2,1)} %get-tuple-element.520) | copy-start | bytes 1572868
  233.1 43.7 %copy-start.3 = (bf16[2048,128]{1,0:T(8,128)(2,1)S(1)}, bf16[2048,128]{1,0:T(8,128)(2,1)}, u32[]{:S(2)}) copy-start(bf16[2048,128]{1,0:T(8,128)(2,1)} %get-tuple-element.524) | copy-start | bytes 1572868
  235.5 2.3 copy-start.9
  276.9 39.0 %copy-start.7 = (bf16[4,512,128]{2,1,0:T(8,128)(2,1)S(1)}, bf16[4,512,128]{2,1,0:T(8,128)(2,1)}, u32[]{:S(2)}) copy-start(bf16[4,512,128]{2,1,0:T(8,128)(2,1)} %get-tuple-element.179) | copy-start | bytes 1572868
  298.7 2.3 copy-start.8
  318.3 26.0 %all-to-all-start.7 = ((bf16[8,256,384]{2,1,0:T(8,128)(2,1)}), bf16[8,256,384]{2,1,0:T(8,128)(2,1)S(1)}, u32[]{:S(2)}, u32[]{:S(2)}) async-start(bf16[8,256,384]{2,1,0:T(8,128)(2,1)} %pad_maximum_fusion.1), calls=%async_computation.7 | async-start | bytes 3145728 | tf_op jit(solution)/shard_map/all_to_all | solution.py:129
  344.3 25.9 %all-to-all-start.6 = ((bf16[8,256,384]{2,1,0:T(8,128)(2,1)}), bf16[8,256,384]{2,1,0:T(8,128)(2,1)}, u32[]{:S(2)}, u32[]{:S(2)}) async-start(bf16[8,256,384]{2,1,0:T(8,128)(2,1)} %pad_maximum_fusion), calls=%async_computation.6 | async-start | bytes 3145728 | tf_op jit(solution)/shard_map/all_to_all | solution.py:128
  371.9 12.9 %copy-start = (bf16[3072,3072]{1,0:T(8,128)(2,1)S(1)}, bf16[3072,3072]{1,0:T(8,128)(2,1)}, u32[]{:S(2)}) copy-start(bf16[3072,3072]{1,0:T(8,128)(2,1)} %all-gather.2.cloned.1.call-done) | copy-start | bytes 56623108
  (8 other events, 17.5 us)
Sparse Core Ops, SparseCore 0:
  96.8 101.5 all-gather.1
where the time goes:
time: 402 us; the launch traced here: 398 us
  waiting for transfers between devices  148 us (37%)
  matrix products  136 us (34%)
  starting transfers between devices  48.4 us (12%)
  local copies, waits for them, and re-layouts  37.3 us (9%)
  between operations  14.2 us (4%)
  other arithmetic  13.7 us (3%)
    dot_general x12, matrix products, block_attention(): jnp.dot(query_rows, tkeys_head.T, preferred_element_type=jnp.float32)  33 us
    dot_general x12, matrix products, block_attention(): jnp.dot(query_rows, keys_head.T, preferred_element_type=jnp.float32)  26.2 us
    all_to_all x1, waiting for transfers between devices, shards(): lax.all_to_all(value_tangent, 'ulysses', split_axis=1, concat_axis=0, til...  24.9 us
    all_to_all x1, waiting for transfers between devices, shards(): lax.all_to_all(key_tangent, 'ulysses', split_axis=1, concat_axis=0, tiled...  19.7 us
    dot_general x12, matrix products, block_attention(): jnp.dot(tquery_rows, keys_head.T, preferred_element_type=jnp.float32)  19.4 us
    all_to_all x1, waiting for transfers between devices, shards(): lax.all_to_all(primal_heads, 'ulysses', split_axis=0, concat_axis=1, tile...  19 us
    all_to_all x1, waiting for transfers between devices, shards(): lax.all_to_all(tangent_heads, 'ulysses', split_axis=0, concat_axis=1, til...  17.1 us
    all_to_all x1, waiting for transfers between devices, shards(): lax.all_to_all(query_tangent, 'ulysses', split_axis=1, concat_axis=0, til...  16.9 us
  transfers between devices with their start and end apart: 9, of which 8 were waited for; matrix products, arithmetic and copies ran while one was open for 41% of the time, Pallas kernels for 0%

commit v1 on v0

v1 whole, which is shorter than its diff:
```python
import functools
import math

import jax
import jax.numpy as jnp
from jax import lax
from jax.experimental import pallas as pl
from jax.experimental.pallas import tpu as pltpu
from jax.sharding import PartitionSpec as P

HEAD_DIM = 128
FRAME = 128
FRAMES_MOST = 8
LOG2E = 1.4426950408889634


def pack_kernel(q, k, v, dq, dk, dv, out):
    for i, ref in enumerate((q, k, v, dq, dk, dv)):
        out[0, i] = ref[...]


def pack_round(tensors, first, rounds, members):
    rows = tensors[0].shape[0]
    return pl.pallas_call(
        pack_kernel,
        grid=(members,),
        in_specs=[pl.BlockSpec((rows, HEAD_DIM), lambda u: (0, u * rounds + first))] * 6,
        out_specs=pl.BlockSpec((1, 6, rows, HEAD_DIM), lambda u: (u, 0, 0, 0)),
        out_shape=jax.ShapeDtypeStruct((members, 6, rows, HEAD_DIM), jnp.bfloat16),
        name="pack",
    )(*tensors)


def nt_dot(a, b):
    return lax.dot_general(a, b, (((1,), (1,)), ((), ())), preferred_element_type=jnp.float32)


def attend_kernel(info, x, out, qq, kk, vv):
    members, _, rows, _ = x.shape
    per = rows // FRAME
    first_count, second_count = info[0], info[1]
    used = first_count + second_count
    factor = LOG2E / math.sqrt(HEAD_DIM)
    scale = 1.0 / math.sqrt(HEAD_DIM)

    def gather(u, carry):
        at = pl.ds(pl.multiple_of(u * rows, rows), rows)
        qq[at, :HEAD_DIM] = x[u, 3]
        qq[at, HEAD_DIM:] = x[u, 0]
        kk[at, :HEAD_DIM] = x[u, 1]
        kk[at, HEAD_DIM:] = x[u, 4]
        vv[at, :HEAD_DIM] = x[u, 2]
        vv[at, HEAD_DIM:] = x[u, 5]
        return carry

    lax.fori_loop(0, (used + per - 1) // per, gather, 0)

    def store(frame, which, value):
        half = pl.multiple_of(lax.rem(frame, per) * FRAME, FRAME)
        out[lax.div(frame, per), which, pl.ds(half, FRAME), :] = value

    def one_video(start, count):
        keys = pl.ds(pl.multiple_of(start * FRAME, FRAME), count * FRAME)

        def one_frame(i, carry):
            frame = start + i
            at = pl.ds(pl.multiple_of(frame * FRAME, FRAME), FRAME)
            s = nt_dot(qq[at, HEAD_DIM:], kk[keys, :HEAD_DIM]) * factor
            t = nt_dot(qq[at, :], kk[keys, :]) * scale
            e = jnp.exp2(s - jnp.max(s, axis=1, keepdims=True))
            total = 1.0 / jnp.sum(e, axis=1, keepdims=True)
            mean = jnp.sum(e * t, axis=1, keepdims=True) * total
            low = e.astype(jnp.bfloat16)
            turned = (e * (t - mean)).astype(jnp.bfloat16)
            both = jnp.dot(low, vv[keys, :], preferred_element_type=jnp.float32)
            more = jnp.dot(turned, vv[keys, :HEAD_DIM], preferred_element_type=jnp.float32)
            store(frame, 0, (both[:, :HEAD_DIM] * total).astype(jnp.bfloat16))
            store(frame, 1, ((both[:, HEAD_DIM:] + more) * total).astype(jnp.bfloat16))
            return carry

        lax.fori_loop(0, count, one_frame, 0)

    def video(i, carry):
        start = jnp.where(i == 0, 0, first_count)
        count = jnp.where(i == 0, first_count, second_count)
        for n in range(1, FRAMES_MOST + 1):
            pl.when(count == n)(functools.partial(one_video, start, n))
        return carry

    lax.fori_loop(0, 2, video, 0)

    def blank(frame, carry):
        nothing = jnp.zeros((FRAME, HEAD_DIM), jnp.bfloat16)
        store(frame, 0, nothing)
        store(frame, 1, nothing)
        return carry

    lax.fori_loop(used, members * per, blank, 0)


def attend(info, x):
    members, _, rows, _ = x.shape
    tokens = members * rows
    return pl.pallas_call(
        attend_kernel,
        in_specs=[
            pl.BlockSpec(memory_space=pltpu.SMEM),
            pl.BlockSpec(memory_space=pltpu.VMEM),
        ],
        out_specs=pl.BlockSpec(memory_space=pltpu.VMEM),
        out_shape=jax.ShapeDtypeStruct((members, 2, rows, HEAD_DIM), jnp.bfloat16),
        scratch_shapes=[pltpu.VMEM((tokens, 2 * HEAD_DIM), jnp.bfloat16)] * 3,
        compiler_params=pltpu.CompilerParams(vmem_limit_bytes=40 * 2**20),
        cost_estimate=pl.CostEstimate(
            flops=7 * 10**9, bytes_accessed=4 * 2**20, transcendentals=2**21
        ),
        name="attend",
    )(info, x)


def project_kernel(rounds, *refs):
    moved, (w, out, tangent, held) = refs[:rounds], refs[rounds:]
    members, _, rows, _ = moved[0].shape

    @pl.when(pl.program_id(0) == 0)
    def _():
        for r, ref in enumerate(moved):
            for u in range(members):
                head = (u * rounds + r) * HEAD_DIM
                for which in range(2):
                    held[which * rows : (which + 1) * rows, head : head + HEAD_DIM] = ref[u, which]

    product = jnp.dot(held[...], w[...], preferred_element_type=jnp.float32)
    out[...] = product[:rows].astype(jnp.bfloat16)
    tangent[...] = product[rows:].astype(jnp.bfloat16)


def project(moved, w):
    rounds = len(moved)
    members, _, rows, _ = moved[0].shape
    depth, width = w.shape
    tile = 512
    given = pl.BlockSpec((rows, tile), lambda n: (0, n))
    return pl.pallas_call(
        functools.partial(project_kernel, rounds),
        grid=(width // tile,),
        in_specs=[pl.BlockSpec(memory_space=pltpu.VMEM)] * rounds
        + [pl.BlockSpec((depth, tile), lambda n: (0, n))],
        out_specs=[given, given],
        out_shape=[jax.ShapeDtypeStruct((rows, width), jnp.bfloat16)] * 2,
        scratch_shapes=[pltpu.VMEM((2 * rows, depth), jnp.bfloat16)],
        compiler_params=pltpu.CompilerParams(vmem_limit_bytes=40 * 2**20),
        name="project",
    )(*moved, w)


def exchange(x):
    return lax.all_to_all(x, "ulysses", split_axis=0, concat_axis=0, tiled=True)


def shards(q, k, v, dq, dk, dv, out_weight, frame_counts, token_offsets, video_group):
    members = lax.axis_size("ulysses")
    rounds = q.shape[1] // HEAD_DIM // members
    mine = video_group == lax.axis_index("dp")
    info = jnp.stack(
        [
            jnp.sum(jnp.where(mine & (token_offsets == 0), frame_counts, 0)),
            jnp.sum(jnp.where(mine & (token_offsets > 0), frame_counts, 0)),
        ]
    ).astype(jnp.int32)
    weight = lax.all_gather(out_weight, ("dp", "ulysses"), axis=0, tiled=True)
    moved = []
    for r in range(rounds):
        arrived = exchange(pack_round((q, k, v, dq, dk, dv), r, rounds, members))
        moved.append(exchange(attend(info, arrived)))
    return tuple(project(moved, weight))


def solution(mesh):
    split = P(("dp", "ulysses"), None)
    return jax.shard_map(
        shards,
        mesh=mesh,
        in_specs=(split,) * 7 + (P(),) * 3,
        out_specs=(split, split),
        check_vma=False,
    )
```

time: 402 us -> 261 us (0.65)
  matrix products: 136 us -> 0 us
  Pallas kernels: 0 us -> 46.9 us
  local copies, waits for them, and re-layouts: 37.3 us -> 12.6 us
  starting transfers between devices: 48.4 us -> 27.1 us
  blocking collectives: 0 us -> 19.4 us
  waiting for transfers between devices: 148 us -> 136 us
  other arithmetic: 13.7 us -> 2 us
    dot_general x74 -> x0, matrix products: 136 us -> none  [the longest x12 33 us: block_attention(): jnp.dot(query_rows, tkeys_head.T, preferred_element_type=jnp.float32)]
    pallas_call x0 -> x7, Pallas kernels: none -> 46.9 us  [the longest x3 18.6 us: pack_round(): pl.pallas_call(pack_kernel, grid=(members,), in_specs=[pl.BlockSpec((rows...]
    all_to_all x8 -> x5, starting transfers between devices: 48.4 us -> 27 us  [exchange(): return lax.all_to_all(x, 'ulysses', split_axis=0, concat_axis=0, tiled=True)]
    all_to_all x0 -> x1, blocking collectives: none -> 19.4 us  [exchange(): return lax.all_to_all(x, 'ulysses', split_axis=0, concat_axis=0, tiled=True)]
    all_to_all x8 -> x0, local copies, waits for them, and re-layouts: 16.6 us -> none  [the longest x1 2.84 us: shards(): lax.all_to_all(value_tangent, 'ulysses', split_axis=1, concat_axis=0, til...]
    slice x6 -> x0, local copies, waits for them, and re-layouts: 12.4 us -> none  [shards(): tensor[:, head_number * HEAD_DIM:(head_number + 1) * HEAD_DIM]]
    all_to_all x8 -> x5, waiting for transfers between devices: 147 us -> 135 us  [exchange(): return lax.all_to_all(x, 'ulysses', split_axis=0, concat_axis=0, tiled=True)]
    unnamed x24 -> x22, local copies, waits for them, and re-layouts: 4.65 us -> 12.6 us
  transfers between devices with their start and end apart: 9 -> 6, of which waited for: 8 -> 5; matrix products, arithmetic and copies ran while one was open for 41% -> 1% of each run, Pallas kernels for 0% -> 12%
where the time goes in v1:
time: 261 us; the launch traced here: 258 us
  waiting for transfers between devices  136 us (52%)
  Pallas kernels  46.9 us (18%)
  starting transfers between devices  27.1 us (10%)
  blocking collectives  19.4 us (7%)
  between operations  14.1 us (5%)
  local copies, waits for them, and re-layouts  12.6 us (5%)
    all_to_all x5, waiting for transfers between devices, exchange(): return lax.all_to_all(x, 'ulysses', split_axis=0, concat_axis=0, tiled=True)  135 us
    all_to_all x5, starting transfers between devices, exchange(): return lax.all_to_all(x, 'ulysses', split_axis=0, concat_axis=0, tiled=True)  27 us
    all_to_all x1, blocking collectives, exchange(): return lax.all_to_all(x, 'ulysses', split_axis=0, concat_axis=0, tiled=True)  19.4 us
    pallas_call x3, Pallas kernels, pack_round(): pl.pallas_call(pack_kernel, grid=(members,), in_specs=[pl.BlockSpec((rows...  18.6 us
    pallas_call x1, Pallas kernels, project(): pl.pallas_call(functools.partial(project_kernel, rounds), grid=(width //...  14.8 us
    pallas_call x3, Pallas kernels, attend(): pl.pallas_call(attend_kernel, in_specs=[pl.BlockSpec(memory_space=pltpu.S...  13.5 us
    unnamed x22, local copies, waits for them, and re-layouts  12.6 us
  transfers between devices with their start and end apart: 6, of which 5 were waited for; matrix products, arithmetic and copies ran while one was open for 1% of the time, Pallas kernels for 12%

profile of v1, /device:TPU:19, one launch (start us, length us, event | category | flops | bytes accessed | tf_op | source)
XLA Modules:
  0.0 257.8 jit_solution(13603746550404300015)
XLA Ops:
  7.9 6.1 %pack.3 = bf16[8,6,256,128]{3,2,1,0:T(8,128)(2,1)} custom-call(bf16[256,3072]{1,0:T(8,128)(2,1)} %q.5, bf16[256,3072]{1,0:T(8,128)(2,1)} %k.5, bf16[256,3072]{1,0:T(8,128)(2,1)} %v.5, bf16[256,3072]{1,0:T(8,128)(2,1)} %dq.5, bf16[256,3072]{1,0:T(8,128)(2,1)} %dk.5, bf16[256,3072]{1,0:T(8,128)(2,1)} %dv.5), custom_call_target="tpu_custom_call" | custom-call | tf_op jit(solution)/shard_map/pack/pallas_call | solution.py:24
  14.0 5.1 %all-to-all-start = ((bf16[8,6,256,128]{3,2,1,0:T(8,128)(2,1)}), bf16[8,6,256,128]{3,2,1,0:T(8,128)(2,1)S(1)}, u32[]{:S(2)}, u32[]{:S(2)}) async-start(bf16[8,6,256,128]{3,2,1,0:T(8,128)(2,1)} %pack.3), calls=%async_computation | async-start | bytes 6291456 | tf_op jit(solution)/shard_map/all_to_all | solution.py:158
  19.2 6.2 %pack.4 = bf16[8,6,256,128]{3,2,1,0:T(8,128)(2,1)} custom-call(bf16[256,3072]{1,0:T(8,128)(2,1)} %q.5, bf16[256,3072]{1,0:T(8,128)(2,1)} %k.5, bf16[256,3072]{1,0:T(8,128)(2,1)} %v.5, bf16[256,3072]{1,0:T(8,128)(2,1)} %dq.5, bf16[256,3072]{1,0:T(8,128)(2,1)} %dk.5, bf16[256,3072]{1,0:T(8,128)(2,1)} %dv.5), custom_call_target="tpu_custom_call" | custom-call | tf_op jit(solution)/shard_map/pack/pallas_call | solution.py:24
  25.3 38.2 %all-to-all-done.x = bf16[8,6,256,128]{3,2,1,0:T(8,128)(2,1)S(1)} async-done(((bf16[8,6,256,128]{3,2,1,0:T(8,128)(2,1)}), bf16[8,6,256,128]{3,2,1,0:T(8,128)(2,1)S(1)}, u32[]{:S(2)}, u32[]{:S(2)}) %all-to-all-start) | async-done | bytes 3145760 | tf_op jit(solution)/shard_map/all_to_all | solution.py:158
  63.5 1.7 copy-done.4
  65.2 5.5 %all-to-all-start.2 = ((bf16[8,6,256,128]{3,2,1,0:T(8,128)(2,1)}), bf16[8,6,256,128]{3,2,1,0:T(8,128)(2,1)S(1)}, u32[]{:S(2)}, u32[]{:S(2)}) async-start(bf16[8,6,256,128]{3,2,1,0:T(8,128)(2,1)} %pack.4), calls=%async_computation.2 | async-start | bytes 6291456 | tf_op jit(solution)/shard_map/all_to_all | solution.py:158
  70.7 6.4 %pack.5 = bf16[8,6,256,128]{3,2,1,0:T(8,128)(2,1)} custom-call(bf16[256,3072]{1,0:T(8,128)(2,1)} %q.5, bf16[256,3072]{1,0:T(8,128)(2,1)} %k.5, bf16[256,3072]{1,0:T(8,128)(2,1)} %v.5, bf16[256,3072]{1,0:T(8,128)(2,1)} %dq.5, bf16[256,3072]{1,0:T(8,128)(2,1)} %dk.5, bf16[256,3072]{1,0:T(8,128)(2,1)} %dv.5), custom_call_target="tpu_custom_call" | custom-call | tf_op jit(solution)/shard_map/pack/pallas_call | solution.py:24
  77.1 55.4 %all-to-all-done.2.x = bf16[8,6,256,128]{3,2,1,0:T(8,128)(2,1)S(1)} async-done(((bf16[8,6,256,128]{3,2,1,0:T(8,128)(2,1)}), bf16[8,6,256,128]{3,2,1,0:T(8,128)(2,1)S(1)}, u32[]{:S(2)}, u32[]{:S(2)}) %all-to-all-start.2) | async-done | bytes 3145760 | tf_op jit(solution)/shard_map/all_to_all | solution.py:158
  132.5 1.7 copy-done.2
  134.2 5.5 %all-to-all-start.4 = ((bf16[8,6,256,128]{3,2,1,0:T(8,128)(2,1)}), bf16[8,6,256,128]{3,2,1,0:T(8,128)(2,1)S(1)}, u32[]{:S(2)}, u32[]{:S(2)}) async-start(bf16[8,6,256,128]{3,2,1,0:T(8,128)(2,1)} %pack.5), calls=%async_computation.4 | async-start | bytes 6291456 | tf_op jit(solution)/shard_map/all_to_all | solution.py:158
  141.7 1.9 copy-done.5
  143.6 4.2 %attend.3 = bf16[8,2,256,128]{3,2,1,0:T(8,128)(2,1)S(1)} custom-call(s32[2]{0:T(128)S(1)} %pad_add_fusion.info, bf16[8,6,256,128]{3,2,1,0:T(8,128)(2,1)S(1)} %copy-done.5), custom_call_target="tpu_custom_call" | custom-call | flops 7000000000 | bytes 4194304 | tf_op jit(solution)/shard_map/attend/pallas_call | solution.py:104
  148.8 27.4 %all-to-all-done.4.x = bf16[8,6,256,128]{3,2,1,0:T(8,128)(2,1)S(1)} async-done(((bf16[8,6,256,128]{3,2,1,0:T(8,128)(2,1)}), bf16[8,6,256,128]{3,2,1,0:T(8,128)(2,1)S(1)}, u32[]{:S(2)}, u32[]{:S(2)}) %all-to-all-start.4) | async-done | bytes 3145760 | tf_op jit(solution)/shard_map/all_to_all | solution.py:158
  176.2 1.7 copy-done
  177.9 5.4 %all-to-all-start.1 = ((bf16[8,2,256,128]{3,2,1,0:T(8,128)(2,1)}), bf16[8,2,256,128]{3,2,1,0:T(8,128)(2,1)S(1)}, u32[]{:S(2)}, u32[]{:S(2)}) async-start(bf16[8,2,256,128]{3,2,1,0:T(8,128)(2,1)} %copy-done.6), calls=%async_computation.1 | async-start | bytes 2097152 | tf_op jit(solution)/shard_map/all_to_all | solution.py:158
  183.3 1.9 copy-done.3
  185.2 5.1 %attend.4 = bf16[8,2,256,128]{3,2,1,0:T(8,128)(2,1)} custom-call(s32[2]{0:T(128)S(1)} %pad_add_fusion.info, bf16[8,6,256,128]{3,2,1,0:T(8,128)(2,1)S(1)} %copy-done.3), custom_call_target="tpu_custom_call" | custom-call | flops 7000000000 | bytes 4194304 | tf_op jit(solution)/shard_map/attend/pallas_call | solution.py:104
  190.3 7.0 %all-to-all-done.1.refs_0_ = bf16[8,2,256,128]{3,2,1,0:T(8,128)(2,1)S(1)} async-done(((bf16[8,2,256,128]{3,2,1,0:T(8,128)(2,1)}), bf16[8,2,256,128]{3,2,1,0:T(8,128)(2,1)S(1)}, u32[]{:S(2)}, u32[]{:S(2)}) %all-to-all-start.1) | async-done | bytes 1048608 | tf_op jit(solution)/shard_map/all_to_all | solution.py:158
  197.3 5.4 %all-to-all-start.3 = ((bf16[8,2,256,128]{3,2,1,0:T(8,128)(2,1)}), bf16[8,2,256,128]{3,2,1,0:T(8,128)(2,1)S(1)}, u32[]{:S(2)}, u32[]{:S(2)}) async-start(bf16[8,2,256,128]{3,2,1,0:T(8,128)(2,1)} %attend.4), calls=%async_computation.3 | async-start | bytes 2097152 | tf_op jit(solution)/shard_map/all_to_all | solution.py:158
  202.8 1.9 copy-done.1
  204.7 4.2 %attend.5 = bf16[8,2,256,128]{3,2,1,0:T(8,128)(2,1)S(1)} custom-call(s32[2]{0:T(128)S(1)} %pad_add_fusion.info, bf16[8,6,256,128]{3,2,1,0:T(8,128)(2,1)S(1)} %copy-done.1), custom_call_target="tpu_custom_call" | custom-call | flops 7000000000 | bytes 4194304 | tf_op jit(solution)/shard_map/attend/pallas_call | solution.py:104
  209.8 7.0 %all-to-all-done.3.refs_1_ = bf16[8,2,256,128]{3,2,1,0:T(8,128)(2,1)S(1)} async-done(((bf16[8,2,256,128]{3,2,1,0:T(8,128)(2,1)}), bf16[8,2,256,128]{3,2,1,0:T(8,128)(2,1)S(1)}, u32[]{:S(2)}, u32[]{:S(2)}) %all-to-all-start.3) | async-done | bytes 1048608 | tf_op jit(solution)/shard_map/all_to_all | solution.py:158
  216.8 19.4 %all_to_all.30.refs_2_ = bf16[8,2,256,128]{3,2,1,0:T(8,128)(2,1)S(1)} all-to-all(bf16[8,2,256,128]{3,2,1,0:T(8,128)(2,1)} %copy-done.7), channel_id=1, replica_groups=mesh['dp'=16,'ulysses'=8] {'ulysses'}, dimensions={0} | all-to-all | bytes 2097152 | tf_op jit(solution)/shard_map/all_to_all | solution.py:158
  236.2 14.8 %project.1 = (bf16[256,3072]{1,0:T(8,128)(2,1)}, bf16[256,3072]{1,0:T(8,128)(2,1)}) custom-call(bf16[8,2,256,128]{3,2,1,0:T(8,128)(2,1)S(1)} %all-to-all-done.1.refs_0_, bf16[8,2,256,128]{3,2,1,0:T(8,128)(2,1)S(1)} %all-to-all-done.3.refs_1_, bf16[8,2,256,128]{3,2,1,0:T(8,128)(2,1)S(1)} %all_to_all.30.refs_2_, ...), custom_call_target="tpu_custom_call" | custom-call | tf_op jit(solution)/shard_map/project/pallas_call | solution.py:144
  (21 shorter events, 4.7 us)
Async XLA Ops:
  7.2 229.0 %all-gather.2.cloned.1.call-start = ((), (), s32[]{:S(2)}) async-start(), calls=%async_computation.6 | async-start | bytes 19021824 | tf_op jit(solution)/shard_map/all_gather | solution.py:171
  14.0 49.5 %all-to-all-start = ((bf16[8,6,256,128]{3,2,1,0:T(8,128)(2,1)}), bf16[8,6,256,128]{3,2,1,0:T(8,128)(2,1)S(1)}, u32[]{:S(2)}, u32[]{:S(2)}) async-start(bf16[8,6,256,128]{3,2,1,0:T(8,128)(2,1)} %pack.3), calls=%async_computation | async-start | bytes 6291456 | tf_op jit(solution)/shard_map/all_to_all | solution.py:158
  63.5 1.7 copy-start.4
  65.2 67.3 %all-to-all-start.2 = ((bf16[8,6,256,128]{3,2,1,0:T(8,128)(2,1)}), bf16[8,6,256,128]{3,2,1,0:T(8,128)(2,1)S(1)}, u32[]{:S(2)}, u32[]{:S(2)}) async-start(bf16[8,6,256,128]{3,2,1,0:T(8,128)(2,1)} %pack.4), calls=%async_computation.2 | async-start | bytes 6291456 | tf_op jit(solution)/shard_map/all_to_all | solution.py:158
  77.1 62.6 %copy-start.8 = (s32[32]{0:T(128)S(1)}, s32[32]{0:T(128)}, u32[]{:S(2)}) copy-start(s32[32]{0:T(128)} %param.17) | copy-start | bytes 388
  77.1 62.6 %copy-start.9 = (s32[32]{0:T(128)S(1)}, s32[32]{0:T(128)}, u32[]{:S(2)}) copy-start(s32[32]{0:T(128)} %param.18) | copy-start | bytes 388
  77.1 62.6 %copy-start.10 = (s32[32]{0:T(128)S(1)}, s32[32]{0:T(128)}, u32[]{:S(2)}) copy-start(s32[32]{0:T(128)} %param.19) | copy-start | bytes 388
  132.5 1.7 copy-start.2
  134.2 42.0 %all-to-all-start.4 = ((bf16[8,6,256,128]{3,2,1,0:T(8,128)(2,1)}), bf16[8,6,256,128]{3,2,1,0:T(8,128)(2,1)S(1)}, u32[]{:S(2)}, u32[]{:S(2)}) async-start(bf16[8,6,256,128]{3,2,1,0:T(8,128)(2,1)} %pack.5), calls=%async_computation.4 | async-start | bytes 6291456 | tf_op jit(solution)/shard_map/all_to_all | solution.py:158
  141.7 1.9 copy-start.5
  147.8 1.0 copy-start.6
  176.2 1.7 copy-start
  177.9 19.5 %all-to-all-start.1 = ((bf16[8,2,256,128]{3,2,1,0:T(8,128)(2,1)}), bf16[8,2,256,128]{3,2,1,0:T(8,128)(2,1)S(1)}, u32[]{:S(2)}, u32[]{:S(2)}) async-start(bf16[8,2,256,128]{3,2,1,0:T(8,128)(2,1)} %copy-done.6), calls=%async_computation.1 | async-start | bytes 2097152 | tf_op jit(solution)/shard_map/all_to_all | solution.py:158
  183.3 1.9 copy-start.3
  197.3 19.5 %all-to-all-start.3 = ((bf16[8,2,256,128]{3,2,1,0:T(8,128)(2,1)}), bf16[8,2,256,128]{3,2,1,0:T(8,128)(2,1)S(1)}, u32[]{:S(2)}, u32[]{:S(2)}) async-start(bf16[8,2,256,128]{3,2,1,0:T(8,128)(2,1)} %attend.4), calls=%async_computation.3 | async-start | bytes 2097152 | tf_op jit(solution)/shard_map/all_to_all | solution.py:158
  202.8 1.9 copy-start.1
  208.8 1.0 copy-start.7
Sparse Core Ops, SparseCore 0:
  11.0 116.9 all-gather.1

commit v2 on v1

v2 whole, which is shorter than its diff:
```python
import functools
import math

import jax
import jax.numpy as jnp
from jax import lax
from jax.experimental import pallas as pl
from jax.experimental.pallas import tpu as pltpu
from jax.sharding import PartitionSpec as P

HEAD_DIM = 128
FRAME = 128
FRAMES_MOST = 8
CORES = 2
LOG2E = 1.4426950408889634
BF16 = jnp.bfloat16
ANY = pl.BlockSpec(memory_space=pl.ANY)
SMEM = pl.BlockSpec(memory_space=pltpu.SMEM)


def run_copies(pairs, sems):
    copies = [pltpu.make_async_copy(a, b, sems.at[i]) for i, (a, b) in enumerate(pairs)]
    for copy in copies:
        copy.start()
    for copy in copies:
        copy.wait()


def head_columns(chip, heads, r, core):
    return pl.ds(pl.multiple_of((chip * heads + CORES * r + core) * HEAD_DIM, HEAD_DIM), HEAD_DIM)


def give_kernel(n, heads, rounds, place, *refs):
    tensors, out, sems = refs[:6], refs[6], refs[7]
    x, c = place[2], place[3]
    pairs = []
    for i, r in enumerate(rounds):
        for k in range(n):
            at = head_columns(lax.rem(x + k, n), heads, r, 1 - c)
            pairs += [(tensors[t].at[:, at], out.at[i, k, t]) for t in range(6)]
    run_copies(pairs, sems)


def give(place, tensors, n, heads, rounds):
    rows = tensors[0].shape[0]
    return pl.pallas_call(
        functools.partial(give_kernel, n, heads, rounds),
        in_specs=[SMEM] + [ANY] * 6,
        out_specs=ANY,
        out_shape=jax.ShapeDtypeStruct((len(rounds), n, 6, rows, HEAD_DIM), BF16),
        scratch_shapes=[pltpu.SemaphoreType.DMA((6 * n * len(rounds),))],
        name="give",
    )(place, *tensors)


def merge_kernel(n, heads, r, i, place, *refs):
    tensors, got, outs, sems = refs[:6], refs[6], refs[7 : 7 + n], refs[7 + n]
    x, c = place[2], place[3]
    rows = got.shape[-2]
    own = pl.ds(pl.multiple_of(c * rows, rows), rows)
    others = pl.ds(pl.multiple_of((1 - c) * rows, rows), rows)
    pairs = []
    for k in [*range(1, n), 0]:
        at = head_columns(lax.rem(x + k, n), heads, r, c)
        pairs += [(tensors[t].at[:, at], outs[k].at[t, own]) for t in range(6)]
        pairs += [(got.at[i, k], outs[k].at[:, others])]
    run_copies(pairs, sems)


def merge(place, tensors, got, n, heads, r, i):
    rows = tensors[0].shape[0]
    return pl.pallas_call(
        functools.partial(merge_kernel, n, heads, r, i),
        in_specs=[SMEM] + [ANY] * 7,
        out_specs=[ANY] * n,
        out_shape=[jax.ShapeDtypeStruct((6, CORES * rows, HEAD_DIM), BF16)] * n,
        scratch_shapes=[pltpu.SemaphoreType.DMA((7 * n,))],
        name="merge",
    )(place, *tensors, got)


def nt_dot(a, b):
    return lax.dot_general(a, b, (((1,), (1,)), ((), ())), preferred_element_type=jnp.float32)


def attend_kernel(n, info, *refs):
    moved, outs, (qq, kk, vv, held, sems) = refs[:n], refs[n : 2 * n], refs[2 * n :]
    rows = moved[0].shape[1]
    per = rows // FRAME
    x = info[2]
    idle = x >= n
    first_count = jnp.where(idle, 0, info[0])
    second_count = jnp.where(idle, 0, info[1])
    used = first_count + second_count
    factor = LOG2E / math.sqrt(HEAD_DIM)
    scale = 1.0 / math.sqrt(HEAD_DIM)

    pairs = []
    for k in range(n):
        at = pl.ds(pl.multiple_of(lax.rem(x + n - k, n) * rows, rows), rows)
        for t, (ref, half) in enumerate(((qq, 1), (kk, 0), (vv, 0), (qq, 0), (kk, 1), (vv, 1))):
            pairs.append((moved[k].at[t], ref.at[at, half * HEAD_DIM : (half + 1) * HEAD_DIM]))
    run_copies(pairs, sems)

    def store(frame, which, value):
        at = pl.multiple_of(lax.rem(frame, per) * FRAME, FRAME)
        held[lax.div(frame, per), which, pl.ds(at, FRAME), :] = value

    def one_video(start, count):
        keys = pl.ds(pl.multiple_of(start * FRAME, FRAME), count * FRAME)

        def one_frame(i, carry):
            frame = start + i
            at = pl.ds(pl.multiple_of(frame * FRAME, FRAME), FRAME)
            s = nt_dot(qq[at, HEAD_DIM:], kk[keys, :HEAD_DIM]) * factor
            t = nt_dot(qq[at, :], kk[keys, :]) * scale
            e = jnp.exp2(s - jnp.max(s, axis=1, keepdims=True))
            p = e * (1.0 / jnp.sum(e, axis=1, keepdims=True))
            mean = jnp.sum(p * t, axis=1, keepdims=True)
            low = p.astype(BF16)
            turned = (p * (t - mean)).astype(BF16)
            both = jnp.dot(low, vv[keys, :], preferred_element_type=jnp.float32)
            more = jnp.dot(turned, vv[keys, :HEAD_DIM], preferred_element_type=jnp.float32)
            store(frame, 0, both[:, :HEAD_DIM].astype(BF16))
            store(frame, 1, (both[:, HEAD_DIM:] + more).astype(BF16))
            return carry

        lax.fori_loop(0, count, one_frame, 0)

    def video(i, carry):
        start = jnp.where(i == 0, 0, first_count)
        count = jnp.where(i == 0, first_count, second_count)
        for frames in range(1, FRAMES_MOST + 1):
            pl.when(count == frames)(functools.partial(one_video, start, frames))
        return carry

    lax.fori_loop(0, 2, video, 0)

    def blank(frame, carry):
        nothing = jnp.zeros((FRAME, HEAD_DIM), BF16)
        store(frame, 0, nothing)
        store(frame, 1, nothing)
        return carry

    lax.fori_loop(used, n * per, blank, 0)
    for k in range(n):
        outs[k][...] = held[lax.rem(x + k, n)]


def attend(info, moved):
    n = len(moved)
    rows = moved[0].shape[1]
    return pl.pallas_call(
        functools.partial(attend_kernel, n),
        in_specs=[SMEM] + [ANY] * n,
        out_specs=[pl.BlockSpec(memory_space=pltpu.VMEM)] * n,
        out_shape=[jax.ShapeDtypeStruct((2, rows, HEAD_DIM), BF16)] * n,
        scratch_shapes=[pltpu.VMEM((n * rows, 2 * HEAD_DIM), BF16)] * 3
        + [pltpu.VMEM((n, 2, rows, HEAD_DIM), BF16), pltpu.SemaphoreType.DMA((6 * n,))],
        compiler_params=pltpu.CompilerParams(vmem_limit_bytes=40 * 2**20),
        cost_estimate=pl.CostEstimate(
            flops=5 * 10**9, bytes_accessed=4 * 2**20, transcendentals=2**21
        ),
        name="attend",
    )(info, *moved)


def project_kernel(n, heads, sizes, place, *refs):
    groups = len(sizes)
    mine, others = refs[: groups * n], refs[groups * n : groups * (n + 1)]
    w_own, w_other, out, tangent, held, sems = refs[groups * (n + 1) :]
    x, c = place[2], place[3]
    rows = out.shape[0]
    step = pl.program_id(0)
    half = pl.num_programs(0) // 2

    @pl.when(step == 0)
    def _():
        own = pl.ds(pl.multiple_of(c * rows, rows), rows)
        pairs, r = [], 0
        for g, size in enumerate(sizes):
            for i in range(size):
                for k in range(n):
                    chip = lax.rem(x + n - k, n)
                    for which in range(2):
                        down = slice(which * rows, (which + 1) * rows)
                        at = head_columns(chip, heads, r, c)
                        pairs.append((mine[g * n + k].at[i, which, own], held.at[down, at]))
                        at = head_columns(chip, heads, r, 1 - c)
                        pairs.append((others[g].at[i, k, which], held.at[down, at]))
                r += 1
        run_copies(pairs, sems)

    @pl.when(x >= n)
    def _():
        out[...] = jnp.zeros_like(out)
        tangent[...] = jnp.zeros_like(tangent)

    def finish(w):
        product = jnp.dot(held[...], w[...], preferred_element_type=jnp.float32)
        out[...] = product[:rows].astype(BF16)
        tangent[...] = product[rows:].astype(BF16)

    pl.when((x < n) & (step < half))(lambda: finish(w_own))
    pl.when((x < n) & (step >= half))(lambda: finish(w_other))


def project(place, mine, others, w_own, w_other, n, heads):
    sizes = tuple(o.shape[0] for o in others)
    rows = others[0].shape[3]
    depth, width = w_own.shape
    tile = 512
    half = width // tile

    def at(step, place):
        return (0, jnp.where(step < half, place[3] * half + step, (1 - place[3]) * half + step - half))

    given = pl.BlockSpec((rows, tile), at)
    return pl.pallas_call(
        functools.partial(project_kernel, n, heads, sizes),
        grid_spec=pltpu.PrefetchScalarGridSpec(
            num_scalar_prefetch=1,
            grid=(2 * half,),
            in_specs=[ANY] * (len(sizes) * (n + 1))
            + [
                pl.BlockSpec((depth, tile), lambda step, place: (0, jnp.minimum(step, half - 1))),
                pl.BlockSpec((depth, tile), lambda step, place: (0, jnp.maximum(step - half, 0))),
            ],
            out_specs=[given, given],
            scratch_shapes=[
                pltpu.VMEM((2 * rows, depth), BF16),
                pltpu.SemaphoreType.DMA((4 * n * sum(sizes),)),
            ],
        ),
        out_shape=[jax.ShapeDtypeStruct((rows, CORES * width), BF16)] * 2,
        compiler_params=pltpu.CompilerParams(vmem_limit_bytes=48 * 2**20),
        name="project",
    )(place, *[m for group in mine for m in group], *others, w_own, w_other)


def after(value, *done):
    return lax.optimization_barrier((value, done))[0]


def hop(value, chips):
    pairs = [(a * CORES + c, b * CORES + c) for a, b in chips for c in range(CORES)]
    return lax.ppermute(value, "ulysses", pairs)


def swap(value):
    members = lax.axis_size("ulysses")
    return lax.ppermute(value, "ulysses", [(u, u ^ 1) for u in range(members)])


def turn(blocks, line, x, parts=1):
    n = len(blocks) + 1
    if n == line:
        return [hop(b, [(i, (i + k) % n) for i in range(n)]) for k, b in enumerate(blocks, 1)]
    up, down = blocks
    came_up = hop(up, [(i, (i + 1) % n) for i in range(n)])
    pieces = []
    for piece in jnp.split(down, parts):
        first = hop(piece, [(1, 0), (2, 1), (0, 3)])
        second = hop(first, [(3, 2)])
        pieces.append(jnp.where(x == 2, second, first))
    return [came_up, jnp.concatenate(pieces) if parts > 1 else pieces[0]]


def gather_weight(out_weight, core):
    members = lax.axis_size("ulysses")
    left, right = jnp.split(out_weight, 2, axis=1)
    got = swap(jnp.where(core == 0, right, left))
    kept = jnp.where(core == 0, left, right)
    rows = jnp.concatenate([jnp.where(core == 0, kept, got), jnp.where(core == 0, got, kept)])
    same_core = [[u for u in range(members) if u % CORES == c] for c in range(CORES)]
    rows = lax.all_gather(rows, "ulysses", axis_index_groups=same_core, axis=0, tiled=True)
    own = lax.all_gather(rows, "dp", axis=0, tiled=True)
    return own, swap(own)


def run(n, line, place, out_weight, *tensors):
    heads = tensors[0].shape[1] // HEAD_DIM // n
    rounds = heads // CORES
    x, c = place[2], place[3]
    w_own, w_other = gather_weight(out_weight, c)
    got_first = swap(give(place, tensors, n, heads, (0,)))
    got_rest = swap(give(place, tensors, n, heads, tuple(range(1, rounds))))
    arrived, results = [], []
    for r in range(rounds):
        got, i = (got_first, 0) if r == 0 else (got_rest, r - 1)
        kept, *sent = merge(place, tensors, got, n, heads, r, i)
        if r >= 2:
            sent = list(after(tuple(sent), arrived[r - 2]))
        came = turn(sent, line, x, parts=2 if r == rounds - 1 else 1)
        arrived.append(tuple(came))
        results.append(attend(place, [kept, *came]))
    mine, others = [], []
    for group in (results[:-1], results[-1:]):
        kept, *sent = [jnp.stack([r[k] for r in group]) for k in range(n)]
        whole = [kept, *turn(sent, line, x)]
        rows = tensors[0].shape[0]
        theirs = [lax.dynamic_slice_in_dim(t, (1 - c) * rows, rows, 2) for t in whole]
        mine.append(whole)
        others.append(swap(jnp.stack(theirs, axis=1)))
    return tuple(project(place, mine, others, w_own, w_other, n, heads))


def shards(q, k, v, dq, dk, dv, out_weight, frame_counts, token_offsets, video_group):
    members, groups = lax.axis_size("ulysses"), lax.axis_size("dp")
    line = members // CORES
    per_chip = CORES * q.shape[0] // FRAME
    u = lax.axis_index("ulysses")
    mine = video_group == lax.axis_index("dp")
    place = jnp.stack(
        [
            jnp.sum(jnp.where(mine & (token_offsets == 0), frame_counts, 0)),
            jnp.sum(jnp.where(mine & (token_offsets > 0), frame_counts, 0)),
            u // CORES,
            u % CORES,
        ]
    ).astype(jnp.int32)
    in_group = video_group[None, :] == jnp.arange(groups, dtype=video_group.dtype)[:, None]
    most = jnp.max(jnp.sum(jnp.where(in_group, frame_counts[None, :], 0), axis=1))
    return lax.cond(
        most <= (line - 1) * per_chip,
        functools.partial(run, line - 1, line),
        functools.partial(run, line, line),
        place,
        out_weight,
        q,
        k,
        v,
        dq,
        dk,
        dv,
    )


def solution(mesh):
    split = P(("dp", "ulysses"), None)
    return jax.shard_map(
        shards,
        mesh=mesh,
        in_specs=(split,) * 7 + (P(),) * 3,
        out_specs=(split, split),
        check_vma=False,
    )
```

time: 261 us -> 632 us (2.42)
  Pallas kernels: 46.9 us -> 436 us
  waiting for transfers between devices: 136 us -> 104 us
  starting transfers between devices: 27.1 us -> 40.8 us
  local copies, waits for them, and re-layouts: 12.6 us -> 2.21 us
  loops' own time: 0 us -> 9.25 us
  blocking collectives: 19.4 us -> 10.8 us
    pallas_call x7 -> x9, Pallas kernels: 46.9 us -> 436 us  [the longest x3 268 us: merge(): pl.pallas_call(functools.partial(merge_kernel, n, heads, r, i), in_specs=...]
    all_to_all x5 -> x0, waiting for transfers between devices: 135 us -> none  [exchange(): return lax.all_to_all(x, 'ulysses', split_axis=0, concat_axis=0, tiled=True)]
    all_gather x1, waiting for transfers between devices: 0.01 us -> 80.7 us  [gather_weight(): own = lax.all_gather(rows, 'dp', axis=0, tiled=True)]
    ppermute x0 -> x21, starting transfers between devices: none -> 40.8 us  [the longest x15 30.1 us: hop(): return lax.ppermute(value, 'ulysses', pairs)]
    all_to_all x5 -> x0, starting transfers between devices: 27 us -> none  [exchange(): return lax.all_to_all(x, 'ulysses', split_axis=0, concat_axis=0, tiled=True)]
    ppermute x0 -> x21, waiting for transfers between devices: none -> 23.6 us  [the longest x15 17.8 us: hop(): return lax.ppermute(value, 'ulysses', pairs)]
    all_to_all x1 -> x0, blocking collectives: 19.4 us -> none  [exchange(): return lax.all_to_all(x, 'ulysses', split_axis=0, concat_axis=0, tiled=True)]
    unnamed x22 -> x0, local copies, waits for them, and re-layouts: 12.6 us -> none
  transfers between devices with their start and end apart: 6 -> 22, of which waited for: 5 -> 9; matrix products, arithmetic and copies ran while one was open for 1% -> 0% of each run, Pallas kernels for 12% -> 67%
where the time goes in v2:
time: 632 us; the launch traced here: 625 us
  Pallas kernels  436 us (69%)
  waiting for transfers between devices  104 us (16%)
  starting transfers between devices  40.8 us (6%)
  between operations  14.9 us (2%)
  blocking collectives  10.8 us (2%)
  loops' own time  9.25 us (1%)
  other arithmetic  6.55 us (1%)
    pallas_call x3, Pallas kernels, merge(): pl.pallas_call(functools.partial(merge_kernel, n, heads, r, i), in_specs=...  268 us
    pallas_call x2, Pallas kernels, give(): pl.pallas_call(functools.partial(give_kernel, n, heads, rounds), in_specs...  115 us
    all_gather x1, waiting for transfers between devices, gather_weight(): own = lax.all_gather(rows, 'dp', axis=0, tiled=True)  80.7 us
    pallas_call x3, Pallas kernels, attend(): pl.pallas_call(functools.partial(attend_kernel, n), in_specs=[SMEM] + [AN...  36.3 us
    ppermute x15, starting transfers between devices, hop(): return lax.ppermute(value, 'ulysses', pairs)  30.1 us
    ppermute x15, waiting for transfers between devices, hop(): return lax.ppermute(value, 'ulysses', pairs)  17.8 us
    pallas_call x1, Pallas kernels, project(): pl.pallas_call(functools.partial(project_kernel, n, heads, sizes), grid_s...  17.1 us
  transfers between devices with their start and end apart: 22, of which 9 were waited for; matrix products, arithmetic and copies ran while one was open for 0% of the time, Pallas kernels for 67%

profile of v2, /device:TPU:19, one launch (start us, length us, event | category | flops | bytes accessed | tf_op | source)
XLA Modules:
  0.0 625.2 jit_solution(3332497776688209491)
XLA Ops:
  12.0 606.2 %conditional.1 = ((bf16[256,3072]{1,0:T(8,128)(2,1)}, bf16[256,3072]{1,0:T(8,128)(2,1)})) conditional(s32[]{:T(128)} %convert_element_type.3, (s32[4]{0:T(128)S(1)}, bf16[256,3072]{1,0:T(8,128)(2,1)}, bf16[256,3072]{1,0:T(8,128)(2,1)}, bf16[256,3072]{1,0:T(8,128)(2,1)}, bf16[256,3072]{1,0:T(8,128)(2,1)}, /*index=5*/bf16[256,3072]{1,0:T(8,128)(2,1)}, ...), branch_computations={%region_4.5_spmd, %region_5.6_spmd} | conditional | flops 20006864896 | bytes 229656032 | solution.py:324
  15.7 10.8 %all_gather.8 = bf16[192,1536]{1,0:T(8,128)(2,1)} all-gather(bf16[48,1536]{1,0:T(8,128)(2,1)S(1)} %pad_maximum_fusion.6), channel_id=1, replica_groups={{0,2,4,6},{1,3,5,7},{8,10,12,14},{9,11,13,15},{16,18,20,22},{17,19,21,2..., dimensions={0}, use_global_device_ids=true | all-gather | bytes 737280 | tf_op jit(solution)/shard_map/cond/branch_0_fun/all_gather | solution.py:276
  26.5 80.7 %all-gather.3.cloned.1.call-done.refs_10_ = bf16[3072,1536]{1,0:T(8,128)(2,1)} async-done(((bf16[192,1536]{1,0:T(8,128)(2,1)}), bf16[3072,1536]{1,0:T(8,128)(2,1)}) %all-gather.3.cloned.1.call-update) | async-done | bytes 9437200 | tf_op jit(solution)/shard_map/cond/branch_0_fun/all_gather | solution.py:277
  107.9 81.5 %give.5 = bf16[2,4,6,256,128]{4,3,2,1,0:T(8,128)(2,1)} custom-call(s32[4]{0:T(128)S(1)} %get-tuple-element.38.place.info, bf16[256,3072]{1,0:T(8,128)(2,1)S(1)} %copy-done.11, bf16[256,3072]{1,0:T(8,128)(2,1)} %get-tuple-element.40.refs_1_, bf16[256,3072]{1,0:T(8,128)(2,1)} %get-tuple-element.41.refs_2_, bf16[256,3072]{1,0:T(8,128)(2,1)} %get-tuple-element.42.refs_3_, ...), custom_call_target="tpu_custom_call" | custom-call | tf_op jit(solution)/shard_map/cond/branch_0_fun/give/pallas_call | solution.py:46
  189.5 33.6 %give.4 = bf16[1,4,6,256,128]{4,3,2,1,0:T(8,128)(2,1)} custom-call(s32[4]{0:T(128)S(1)} %get-tuple-element.38.place.info, bf16[256,3072]{1,0:T(8,128)(2,1)S(1)} %copy-done.11, bf16[256,3072]{1,0:T(8,128)(2,1)S(1)} %copy-done.13, bf16[256,3072]{1,0:T(8,128)(2,1)} %get-tuple-element.41.refs_2_, bf16[256,3072]{1,0:T(8,128)(2,1)} %get-tuple-element.42.refs_3_, ...), custom_call_target="tpu_custom_call" | custom-call | tf_op jit(solution)/shard_map/cond/branch_0_fun/give/pallas_call | solution.py:46
  223.7 3.4 collective-permute-done.refs_6_
  227.1 81.3 %merge.7 = (bf16[6,512,128]{2,1,0:T(8,128)(2,1)}, bf16[6,512,128]{2,1,0:T(8,128)(2,1)}, bf16[6,512,128]{2,1,0:T(8,128)(2,1)}, bf16[6,512,128]{2,1,0:T(8,128)(2,1)}) custom-call(s32[4]{0:T(128)S(1)} %get-tuple-element.38.place.info, bf16[256,3072]{1,0:T(8,128)(2,1)S(1)} %copy-done.11, bf16[256,3072]{1,0:T(8,128)(2,1)S(1)} %copy-done.13, ...), custom_call_target="tpu_custom_call" | custom-call | tf_op jit(solution)/shard_map/cond/branch_0_fun/merge/pallas_call | solution.py:72
  310.6 1.8 collective-permute-start.3
  312.4 89.3 %merge.8 = (bf16[6,512,128]{2,1,0:T(8,128)(2,1)}, bf16[6,512,128]{2,1,0:T(8,128)(2,1)}, bf16[6,512,128]{2,1,0:T(8,128)(2,1)}, bf16[6,512,128]{2,1,0:T(8,128)(2,1)}) custom-call(s32[4]{0:T(128)S(1)} %get-tuple-element.38.place.info, bf16[256,3072]{1,0:T(8,128)(2,1)S(1)} %copy-done.11, bf16[256,3072]{1,0:T(8,128)(2,1)} %get-tuple-element.40.refs_1_, ...), custom_call_target="tpu_custom_call" | custom-call | tf_op jit(solution)/shard_map/cond/branch_0_fun/merge/pallas_call | solution.py:72
  402.7 2.9 collective-permute-start.6
  406.8 12.5 %attend.7 = (bf16[2,512,128]{2,1,0:T(8,128)(2,1)S(1)}, bf16[2,512,128]{2,1,0:T(8,128)(2,1)S(1)}, bf16[2,512,128]{2,1,0:T(8,128)(2,1)S(1)}, bf16[2,512,128]{2,1,0:T(8,128)(2,1)S(1)}) custom-call(s32[4]{0:T(128)S(1)} %get-tuple-element.38.place.info, bf16[6,512,128]{2,1,0:T(8,128)(2,1)S(1)} %copy-done.6, bf16[6,512,128]{2,1,0:T(8,128)(2,1)S(1)} %copy-done.8, ...), custom_call_target="tpu_custom_call" | custom-call | flops 5000000000 | bytes 4194304 | tf_op jit(solution)/shard_map/cond/branch_0_fun/attend/pallas_call | solution.py:153
  419.3 97.2 %merge.9 = (bf16[6,512,128]{2,1,0:T(8,128)(2,1)}, bf16[6,512,128]{2,1,0:T(8,128)(2,1)}, bf16[6,512,128]{2,1,0:T(8,128)(2,1)}, bf16[6,512,128]{2,1,0:T(8,128)(2,1)}) custom-call(s32[4]{0:T(128)S(1)} %get-tuple-element.38.place.info, bf16[256,3072]{1,0:T(8,128)(2,1)} %get-tuple-element.39.refs_0_, bf16[256,3072]{1,0:T(8,128)(2,1)} %get-tuple-element.40.refs_1_, ...), custom_call_target="tpu_custom_call" | custom-call | tf_op jit(solution)/shard_map/cond/branch_0_fun/merge/pallas_call | solution.py:72
  516.5 1.5 collective-permute-start.11
  520.1 12.4 %attend.8 = (bf16[2,512,128]{2,1,0:T(8,128)(2,1)S(1)}, bf16[2,512,128]{2,1,0:T(8,128)(2,1)S(1)}, bf16[2,512,128]{2,1,0:T(8,128)(2,1)S(1)}, bf16[2,512,128]{2,1,0:T(8,128)(2,1)S(1)}) custom-call(s32[4]{0:T(128)S(1)} %get-tuple-element.38.place.info, bf16[6,512,128]{2,1,0:T(8,128)(2,1)S(1)} %copy-done.1, ...), custom_call_target="tpu_custom_call" | custom-call | flops 5000000000 | bytes 4194304 | tf_op jit(solution)/shard_map/cond/branch_0_fun/attend/pallas_call | solution.py:153
  532.6 2.0 collective-permute-start.10
  536.6 15.6 %collective-permute-start.8 = (bf16[2,2,512,128]{3,2,1,0:T(8,128)(2,1)S(1)}, bf16[2,2,512,128]{3,2,1,0:T(8,128)(2,1)S(1)}, u32[]{:S(2)}, u32[]{:S(2)}) collective-permute-start(bf16[2,2,512,128]{3,2,1,0:T(8,128)(2,1)S(1)} %pad_maximum_fusion.2), channel_id=1, source_target_pairs={{0,2},{1,3},{2,4},{3,5},{4,6},{5,7},{6,0},{7,1},{8,10},{9,11},{10,... | collective-permute-start | bytes 1572872 | tf_op jit(solution)/shard_map/cond/branch_0_fun/ppermute | solution.py:247
  552.1 3.8 collective-permute-done.13.refs_3_
  555.9 11.4 %attend.9 = (bf16[2,512,128]{2,1,0:T(8,128)(2,1)S(1)}, bf16[2,512,128]{2,1,0:T(8,128)(2,1)S(1)}, bf16[2,512,128]{2,1,0:T(8,128)(2,1)S(1)}, bf16[2,512,128]{2,1,0:T(8,128)(2,1)S(1)}) custom-call(s32[4]{0:T(128)S(1)} %get-tuple-element.38.place.info, bf16[6,512,128]{2,1,0:T(8,128)(2,1)S(1)} %copy-done.4, ...), custom_call_target="tpu_custom_call" | custom-call | flops 5000000000 | bytes 4194304 | tf_op jit(solution)/shard_map/cond/branch_0_fun/attend/pallas_call | solution.py:153
  569.7 6.1 collective-permute-done.9.refs_2_
  576.1 6.2 collective-permute-start.17
  582.4 5.6 collective-permute-done.16.refs_7_
  588.1 2.4 collective-permute-start.18
  590.6 1.5 collective-permute-done.18.refs_9_
  592.0 17.1 %project.2 = (bf16[256,3072]{1,0:T(8,128)(2,1)}, bf16[256,3072]{1,0:T(8,128)(2,1)}) custom-call(s32[4]{0:T(128)S(1)} %get-tuple-element.38.place.info, bf16[2,2,512,128]{3,2,1,0:T(8,128)(2,1)S(1)} %pad_maximum_fusion.1.refs_0_, bf16[2,2,512,128]{3,2,1,0:T(8,128)(2,1)S(1)} %collective-permute-done.8.refs_1_, ...), custom_call_target="tpu_custom_call" | custom-call | tf_op jit(solution)/shard_map/cond/branch_0_fun/project/pallas_call | solution.py:219
  (67 shorter events, 20.2 us)
Async XLA Ops:
  12.0 96.0 %copy-start.11 = (bf16[256,3072]{1,0:T(8,128)(2,1)S(1)}, bf16[256,3072]{1,0:T(8,128)(2,1)}, u32[]{:S(2)}) copy-start(bf16[256,3072]{1,0:T(8,128)(2,1)} %get-tuple-element.39.refs_0_) | copy-start | bytes 4718596 | tf_op jit(solution)/shard_map/cond
  12.0 95.2 %all-gather.3.cloned.1.call-start = ((), (), s32[]{:S(2)}) async-start(), calls=%async_computation | async-start | bytes 10027008 | tf_op jit(solution)/shard_map/cond/branch_0_fun/all_gather | solution.py:277
  13.0 1.7 collective-permute-start.19
  107.2 484.8 %collective-permute-start.20 = (bf16[3072,1536]{1,0:T(8,128)(2,1)}, bf16[3072,1536]{1,0:T(8,128)(2,1)}, u32[]{:S(2)}, u32[]{:S(2)}) collective-permute-start(bf16[3072,1536]{1,0:T(8,128)(2,1)} %all-gather.3.cloned.1.call-done.refs_10_), channel_id=1, source_target_pairs={{0,1},{1,0},{2,3},{3,2},{4,5},{5,4},{6,7},{7,6},{8,9},{9,8},{10,11... | collective-permute-start | bytes 28311560 | tf_op jit(solution)/shard_map/cond/branch_0_fun/ppermute | solution.py:252
  189.4 123.0 %collective-permute-start.4 = (bf16[2,4,6,256,128]{4,3,2,1,0:T(8,128)(2,1)}, bf16[2,4,6,256,128]{4,3,2,1,0:T(8,128)(2,1)}, u32[]{:S(2)}, u32[]{:S(2)}) collective-permute-start(bf16[2,4,6,256,128]{4,3,2,1,0:T(8,128)(2,1)} %give.5), channel_id=1, source_target_pairs={{0,1},{1,0},{2,3},{3,2},{4,5},{5,4},{6,7},{7,6},{8,9},{9,8},{10,11... | collective-permute-start | bytes 9437192 | tf_op jit(solution)/shard_map/cond/branch_0_fun/ppermute | solution.py:252
  223.2 3.9 collective-permute-start
  308.4 93.3 %collective-permute-start.1 = (bf16[6,512,128]{2,1,0:T(8,128)(2,1)}, bf16[6,512,128]{2,1,0:T(8,128)(2,1)S(1)}, u32[]{:S(2)}, u32[]{:S(2)}) collective-permute-start(bf16[6,512,128]{2,1,0:T(8,128)(2,1)} %get-tuple-element.46), channel_id=1, source_target_pairs={{0,2},{1,3},{2,4},{3,5},{4,6},{5,7},{6,0},{7,1},{8,10},{9,11},{10,... | collective-permute-start | bytes 2359304 | tf_op jit(solution)/shard_map/cond/branch_0_fun/ppermute | solution.py:247
  309.7 95.9 %collective-permute-start.2 = (bf16[6,512,128]{2,1,0:T(8,128)(2,1)}, bf16[6,512,128]{2,1,0:T(8,128)(2,1)}, u32[]{:S(2)}, u32[]{:S(2)}) collective-permute-start(bf16[6,512,128]{2,1,0:T(8,128)(2,1)} %get-tuple-element.47), channel_id=1, source_target_pairs={{0,4},{1,5},{2,6},{3,7},{4,0},{5,1},{6,2},{7,3},{8,12},{9,13},{10,... | collective-permute-start | bytes 2359304 | tf_op jit(solution)/shard_map/cond/branch_0_fun/ppermute | solution.py:247
  310.6 95.1 %collective-permute-start.3 = (bf16[6,512,128]{2,1,0:T(8,128)(2,1)}, bf16[6,512,128]{2,1,0:T(8,128)(2,1)}, u32[]{:S(2)}, u32[]{:S(2)}) collective-permute-start(bf16[6,512,128]{2,1,0:T(8,128)(2,1)} %get-tuple-element.48), channel_id=1, source_target_pairs={{0,6},{1,7},{2,0},{3,1},{4,2},{5,3},{6,4},{7,5},{8,14},{9,15},{10,... | collective-permute-start | bytes 2359304 | tf_op jit(solution)/shard_map/cond/branch_0_fun/ppermute | solution.py:247
  401.6 116.4 %collective-permute-start.5 = (bf16[6,512,128]{2,1,0:T(8,128)(2,1)}, bf16[6,512,128]{2,1,0:T(8,128)(2,1)S(1)}, u32[]{:S(2)}, u32[]{:S(2)}) collective-permute-start(bf16[6,512,128]{2,1,0:T(8,128)(2,1)} %get-tuple-element.51), channel_id=1, source_target_pairs={{0,2},{1,3},{2,4},{3,5},{4,6},{5,7},{6,0},{7,1},{8,10},{9,11},{10,... | collective-permute-start | bytes 2359304 | tf_op jit(solution)/shard_map/cond/branch_0_fun/ppermute | solution.py:247
  402.7 116.6 %collective-permute-start.6 = (bf16[6,512,128]{2,1,0:T(8,128)(2,1)}, bf16[6,512,128]{2,1,0:T(8,128)(2,1)S(1)}, u32[]{:S(2)}, u32[]{:S(2)}) collective-permute-start(bf16[6,512,128]{2,1,0:T(8,128)(2,1)} %get-tuple-element.52), channel_id=1, source_target_pairs={{0,4},{1,5},{2,6},{3,7},{4,0},{5,1},{6,2},{7,3},{8,12},{9,13},{10,... | collective-permute-start | bytes 2359304 | tf_op jit(solution)/shard_map/cond/branch_0_fun/ppermute | solution.py:247
  405.6 114.5 %collective-permute-start.7 = (bf16[6,512,128]{2,1,0:T(8,128)(2,1)}, bf16[6,512,128]{2,1,0:T(8,128)(2,1)}, u32[]{:S(2)}, u32[]{:S(2)}) collective-permute-start(bf16[6,512,128]{2,1,0:T(8,128)(2,1)} %get-tuple-element.53), channel_id=1, source_target_pairs={{0,6},{1,7},{2,0},{3,1},{4,2},{5,3},{6,4},{7,5},{8,14},{9,15},{10,... | collective-permute-start | bytes 2359304 | tf_op jit(solution)/shard_map/cond/branch_0_fun/ppermute | solution.py:247
  419.3 100.8 %copy-start.1 = (bf16[6,512,128]{2,1,0:T(8,128)(2,1)S(1)}, bf16[6,512,128]{2,1,0:T(8,128)(2,1)}, u32[]{:S(2)}) copy-start(bf16[6,512,128]{2,1,0:T(8,128)(2,1)} %get-tuple-element.50.refs_0_) | copy-start | bytes 2359300 | tf_op jit(solution)/shard_map/cond
  516.5 18.3 %collective-permute-start.11 = (bf16[6,512,128]{2,1,0:T(8,128)(2,1)}, bf16[6,512,128]{2,1,0:T(8,128)(2,1)S(1)}, u32[]{:S(2)}, u32[]{:S(2)}) collective-permute-start(bf16[6,512,128]{2,1,0:T(8,128)(2,1)} %get-tuple-element.65), channel_id=1, source_target_pairs={{0,2},{1,3},{2,4},{3,5},{4,6},{5,7},{6,0},{7,1},{8,10},{9,11},{10,... | collective-permute-start | bytes 2359304 | tf_op jit(solution)/shard_map/cond/branch_0_fun/ppermute | solution.py:247
  518.1 18.5 %collective-permute-start.12 = (bf16[6,512,128]{2,1,0:T(8,128)(2,1)}, bf16[6,512,128]{2,1,0:T(8,128)(2,1)S(1)}, u32[]{:S(2)}, u32[]{:S(2)}) collective-permute-start(bf16[6,512,128]{2,1,0:T(8,128)(2,1)} %get-tuple-element.66), channel_id=1, source_target_pairs={{0,4},{1,5},{2,6},{3,7},{4,0},{5,1},{6,2},{7,3},{8,12},{9,13},{10,... | collective-permute-start | bytes 2359304 | tf_op jit(solution)/shard_map/cond/branch_0_fun/ppermute | solution.py:247
  519.3 36.6 %collective-permute-start.13 = (bf16[6,512,128]{2,1,0:T(8,128)(2,1)}, bf16[6,512,128]{2,1,0:T(8,128)(2,1)S(1)}, u32[]{:S(2)}, u32[]{:S(2)}) collective-permute-start(bf16[6,512,128]{2,1,0:T(8,128)(2,1)} %get-tuple-element.67), channel_id=1, source_target_pairs={{0,6},{1,7},{2,0},{3,1},{4,2},{5,3},{6,4},{7,5},{8,14},{9,15},{10,... | collective-permute-start | bytes 2359304 | tf_op jit(solution)/shard_map/cond/branch_0_fun/ppermute | solution.py:247
  532.6 37.1 %collective-permute-start.10 = (bf16[2,2,512,128]{3,2,1,0:T(8,128)(2,1)S(1)}, bf16[2,2,512,128]{3,2,1,0:T(8,128)(2,1)S(1)}, u32[]{:S(2)}, u32[]{:S(2)}) collective-permute-start(bf16[2,2,512,128]{3,2,1,0:T(8,128)(2,1)S(1)} %pad_maximum_fusion.4), channel_id=1, source_target_pairs={{0,6},{1,7},{2,0},{3,1},{4,2},{5,3},{6,4},{7,5},{8,14},{9,15},{10,... | collective-permute-start | bytes 1572872 | tf_op jit(solution)/shard_map/cond/branch_0_fun/ppermute | solution.py:247
  534.8 41.1 %collective-permute-start.9 = (bf16[2,2,512,128]{3,2,1,0:T(8,128)(2,1)S(1)}, bf16[2,2,512,128]{3,2,1,0:T(8,128)(2,1)S(1)}, u32[]{:S(2)}, u32[]{:S(2)}) collective-permute-start(bf16[2,2,512,128]{3,2,1,0:T(8,128)(2,1)S(1)} %pad_maximum_fusion.3), channel_id=1, source_target_pairs={{0,4},{1,5},{2,6},{3,7},{4,0},{5,1},{6,2},{7,3},{8,12},{9,13},{10,... | collective-permute-start | bytes 1572872 | tf_op jit(solution)/shard_map/cond/branch_0_fun/ppermute | solution.py:247
  536.6 39.4 %collective-permute-start.8 = (bf16[2,2,512,128]{3,2,1,0:T(8,128)(2,1)S(1)}, bf16[2,2,512,128]{3,2,1,0:T(8,128)(2,1)S(1)}, u32[]{:S(2)}, u32[]{:S(2)}) collective-permute-start(bf16[2,2,512,128]{3,2,1,0:T(8,128)(2,1)S(1)} %pad_maximum_fusion.2), channel_id=1, source_target_pairs={{0,2},{1,3},{2,4},{3,5},{4,6},{5,7},{6,0},{7,1},{8,10},{9,11},{10,... | collective-permute-start | bytes 1572872 | tf_op jit(solution)/shard_map/cond/branch_0_fun/ppermute | solution.py:247
  567.4 14.9 %collective-permute-start.15 = (bf16[1,2,512,128]{3,2,1,0:T(8,128)(2,1)S(1)}, bf16[1,2,512,128]{3,2,1,0:T(8,128)(2,1)S(1)}, u32[]{:S(2)}, u32[]{:S(2)}) collective-permute-start(bf16[1,2,512,128]{3,2,1,0:T(8,128)(2,1)S(1)} %bitcast.79), channel_id=1, source_target_pairs={{0,4},{1,5},{2,6},{3,7},{4,0},{5,1},{6,2},{7,3},{8,12},{9,13},{10,... | collective-permute-start | bytes 786440 | tf_op jit(solution)/shard_map/cond/branch_0_fun/ppermute | solution.py:247
  569.7 12.6 %collective-permute-start.14 = (bf16[1,2,512,128]{3,2,1,0:T(8,128)(2,1)S(1)}, bf16[1,2,512,128]{3,2,1,0:T(8,128)(2,1)S(1)}, u32[]{:S(2)}, u32[]{:S(2)}) collective-permute-start(bf16[1,2,512,128]{3,2,1,0:T(8,128)(2,1)S(1)} %bitcast.78), channel_id=1, source_target_pairs={{0,2},{1,3},{2,4},{3,5},{4,6},{5,7},{6,0},{7,1},{8,10},{9,11},{10,... | collective-permute-start | bytes 786440 | tf_op jit(solution)/shard_map/cond/branch_0_fun/ppermute | solution.py:247
  575.9 12.1 %collective-permute-start.16 = (bf16[1,2,512,128]{3,2,1,0:T(8,128)(2,1)S(1)}, bf16[1,2,512,128]{3,2,1,0:T(8,128)(2,1)S(1)}, u32[]{:S(2)}, u32[]{:S(2)}) collective-permute-start(bf16[1,2,512,128]{3,2,1,0:T(8,128)(2,1)S(1)} %bitcast.77), channel_id=1, source_target_pairs={{0,6},{1,7},{2,0},{3,1},{4,2},{5,3},{6,4},{7,5},{8,14},{9,15},{10,... | collective-permute-start | bytes 786440 | tf_op jit(solution)/shard_map/cond/branch_0_fun/ppermute | solution.py:247
  576.1 15.9 %collective-permute-start.17 = (bf16[2,4,2,256,128]{4,3,2,1,0:T(8,128)(2,1)S(1)}, bf16[2,4,2,256,128]{4,3,2,1,0:T(8,128)(2,1)S(1)}, u32[]{:S(2)}, u32[]{:S(2)}) collective-permute-start(bf16[2,4,2,256,128]{4,3,2,1,0:T(8,128)(2,1)S(1)} %pad_maximum_fusion), channel_id=1, source_target_pairs={{0,1},{1,0},{2,3},{3,2},{4,5},{5,4},{6,7},{7,6},{8,9},{9,8},{10,11... | collective-permute-start | bytes 3145736 | tf_op jit(solution)/shard_map/cond/branch_0_fun/ppermute | solution.py:252
  588.1 3.9 collective-permute-start.18
  (5 other events, 202.2 us)
Sparse Core Ops, SparseCore 0:
  26.6 80.5 all-gather.2

commit v3 on v1

v3 whole, which is shorter than its diff:
```python
import functools
import math

import jax
import jax.numpy as jnp
from jax import lax
from jax.experimental import pallas as pl
from jax.experimental.pallas import tpu as pltpu
from jax.sharding import PartitionSpec as P

HEAD_DIM = 128
FRAME = 128
FRAMES_MOST = 8
CORES = 2
LOG2E = 1.4426950408889634
BF16 = jnp.bfloat16
ANY = pl.BlockSpec(memory_space=pl.ANY)
SMEM = pl.BlockSpec(memory_space=pltpu.SMEM)
VMEM = pl.BlockSpec(memory_space=pltpu.VMEM)


def run_copies(pairs, sems):
    copies = [pltpu.make_async_copy(a, b, sems.at[i]) for i, (a, b) in enumerate(pairs)]
    for copy in copies:
        copy.start()
    for copy in copies:
        copy.wait()


def pack_kernel(r, rounds, *refs):
    tensors, out, sems = refs[:6], refs[6], refs[7]
    pairs = []
    for u in range(out.shape[0]):
        at = slice((u * rounds + r) * HEAD_DIM, (u * rounds + r + 1) * HEAD_DIM)
        pairs += [(tensors[t].at[:, at], out.at[u, t]) for t in range(6)]
    run_copies(pairs, sems)


def pack(tensors, r, rounds, members):
    rows = tensors[0].shape[0]
    return pl.pallas_call(
        functools.partial(pack_kernel, r, rounds),
        in_specs=[ANY] * 6,
        out_specs=VMEM,
        out_shape=jax.ShapeDtypeStruct((members, 6, rows, HEAD_DIM), BF16),
        scratch_shapes=[pltpu.SemaphoreType.DMA((6 * members,))],
        name="pack",
    )(*tensors)


def nt_dot(a, b):
    return lax.dot_general(a, b, (((1,), (1,)), ((), ())), preferred_element_type=jnp.float32)


def attend_kernel(info, x, out, qq, kk, vv, sems):
    members, _, rows, _ = x.shape
    per = rows // FRAME
    first_count, second_count = info[0], info[1]
    used = first_count + second_count
    factor = LOG2E / math.sqrt(HEAD_DIM)
    scale = 1.0 / math.sqrt(HEAD_DIM)

    pairs = []
    for u in range(members):
        at = slice(u * rows, (u + 1) * rows)
        for t, (to, half) in enumerate(((qq, 1), (kk, 0), (vv, 0), (qq, 0), (kk, 1), (vv, 1))):
            pairs.append((x.at[u, t], to.at[at, half * HEAD_DIM : (half + 1) * HEAD_DIM]))
    run_copies(pairs, sems)

    def store(frame, which, value):
        at = pl.multiple_of(lax.rem(frame, per) * FRAME, FRAME)
        out[lax.div(frame, per), which, pl.ds(at, FRAME), :] = value

    def one_video(start, count):
        keys = pl.ds(pl.multiple_of(start * FRAME, FRAME), count * FRAME)

        def block(frame, frames):
            at = pl.ds(pl.multiple_of(frame * FRAME, FRAME), frames * FRAME)
            s = nt_dot(qq[at, HEAD_DIM:], kk[keys, :HEAD_DIM]) * factor
            t = nt_dot(qq[at, :], kk[keys, :]) * scale
            e = jnp.exp2(s - jnp.max(s, axis=1, keepdims=True))
            p = e * (1.0 / jnp.sum(e, axis=1, keepdims=True))
            mean = jnp.sum(p * t, axis=1, keepdims=True)
            low = p.astype(BF16)
            turned = (p * (t - mean)).astype(BF16)
            both = jnp.dot(low, vv[keys, :], preferred_element_type=jnp.float32)
            more = jnp.dot(turned, vv[keys, :HEAD_DIM], preferred_element_type=jnp.float32)
            primal = both[:, :HEAD_DIM].astype(BF16)
            tangent = (both[:, HEAD_DIM:] + more).astype(BF16)
            for i in range(frames):
                part = slice(i * FRAME, (i + 1) * FRAME)
                store(frame + i, 0, primal[part])
                store(frame + i, 1, tangent[part])

        def two_frames(i, carry):
            block(start + 2 * i, 2)
            return carry

        lax.fori_loop(0, count // 2, two_frames, 0)
        if count % 2:
            block(start + count - 1, 1)

    def video(i, carry):
        start = jnp.where(i == 0, 0, first_count)
        count = jnp.where(i == 0, first_count, second_count)
        for frames in range(1, FRAMES_MOST + 1):
            pl.when(count == frames)(functools.partial(one_video, start, frames))
        return carry

    lax.fori_loop(0, 2, video, 0)

    def blank(frame, carry):
        nothing = jnp.zeros((FRAME, HEAD_DIM), BF16)
        store(frame, 0, nothing)
        store(frame, 1, nothing)
        return carry

    lax.fori_loop(used, members * per, blank, 0)


def attend(info, x):
    members, _, rows, _ = x.shape
    return pl.pallas_call(
        attend_kernel,
        in_specs=[SMEM, ANY],
        out_specs=VMEM,
        out_shape=jax.ShapeDtypeStruct((members, 2, rows, HEAD_DIM), BF16),
        scratch_shapes=[pltpu.VMEM((members * rows, 2 * HEAD_DIM), BF16)] * 3
        + [pltpu.SemaphoreType.DMA((6 * members,))],
        compiler_params=pltpu.CompilerParams(vmem_limit_bytes=40 * 2**20),
        name="attend",
    )(info, x)


def project_kernel(moved, w, *refs):
    if len(refs) == 5:
        total, out, tangent, held, sems = refs
    else:
        out, held, sems = refs
        total = None
    members, size, _, rows, _ = moved.shape

    @pl.when(pl.program_id(0) == 0)
    def _():
        pairs = []
        for u in range(members):
            for i in range(size):
                at = slice((u * size + i) * HEAD_DIM, (u * size + i + 1) * HEAD_DIM)
                for which in range(2):
                    down = slice(which * rows, (which + 1) * rows)
                    pairs.append((moved.at[u, i, which], held.at[down, at]))
        run_copies(pairs, sems)

    depth = held.shape[1]
    product = jnp.dot(held[...], w[...].reshape(depth, -1), preferred_element_type=jnp.float32)
    if total is None:
        out[...] = product
    else:
        out[...] = (total[:rows] + product[:rows]).astype(BF16)
        tangent[...] = (total[rows:] + product[rows:]).astype(BF16)


def project(moved, weight, rounds, first, total=None):
    members, size, _, rows, _ = moved.shape
    width = weight.shape[1]
    tile = 512
    by_round = weight.reshape(members, rounds, HEAD_DIM, width)
    sum_spec = pl.BlockSpec((2 * rows, tile), lambda step: (0, step))
    half_spec = pl.BlockSpec((rows, tile), lambda step: (0, step))
    last = total is not None
    return pl.pallas_call(
        project_kernel,
        grid=(width // tile,),
        in_specs=[ANY]
        + [pl.BlockSpec((members, size, HEAD_DIM, tile), lambda step: (0, first // size, 0, step))]
        + [sum_spec] * last,
        out_specs=[half_spec, half_spec] if last else sum_spec,
        scratch_shapes=[
            pltpu.VMEM((2 * rows, members * size * HEAD_DIM), BF16),
            pltpu.SemaphoreType.DMA((2 * members * size,)),
        ],
        out_shape=[jax.ShapeDtypeStruct((rows, width), BF16)] * 2
        if last
        else jax.ShapeDtypeStruct((2 * rows, width), jnp.float32),
        compiler_params=pltpu.CompilerParams(vmem_limit_bytes=40 * 2**20),
        name="project",
    )(moved, by_round, *([total] if last else []))


def after(value, *done):
    return lax.optimization_barrier((value, done))[0]


def exchange(x):
    return lax.all_to_all(x, "ulysses", split_axis=0, concat_axis=0, tiled=True)


def hop(value, chips):
    pairs = [(a * CORES + c, b * CORES + c) for a, b in chips for c in range(CORES)]
    return lax.ppermute(value, "ulysses", pairs)


def swap(value):
    members = lax.axis_size("ulysses")
    return lax.ppermute(value, "ulysses", [(u, u ^ 1) for u in range(members)])


def gather_line(shard, ready):
    u = lax.axis_index("ulysses")
    x, core = u // CORES, u % CORES
    line = lax.axis_size("ulysses") // CORES
    back = [hop(shard, [(i, (i + k) % line) for i in range(line)]) for k in range(line - 1, 0, -1)]
    back = after(tuple(back), ready)
    ring = jnp.stack([*back, shard] * 2)
    mine = lax.dynamic_slice_in_dim(ring, line - 1 - x, line, 0)
    theirs = swap(mine)
    pair = [jnp.where(core == 0, mine, theirs), jnp.where(core == 0, theirs, mine)]
    return jnp.stack(pair, axis=1).reshape(-1, shard.shape[1])


def shards(q, k, v, dq, dk, dv, out_weight, frame_counts, token_offsets, video_group):
    members = lax.axis_size("ulysses")
    rounds = q.shape[1] // HEAD_DIM // members
    tensors = (q, k, v, dq, dk, dv)
    packed = [pack(tensors, 0, rounds, members)]
    near = gather_line(out_weight, packed[0])
    weight = lax.all_gather(near, "dp", axis=0, tiled=True)
    arrived = exchange(packed[0])
    mine = video_group == lax.axis_index("dp")
    info = jnp.stack(
        [
            jnp.sum(jnp.where(mine & (token_offsets == 0), frame_counts, 0)),
            jnp.sum(jnp.where(mine & (token_offsets > 0), frame_counts, 0)),
        ]
    ).astype(jnp.int32)
    results = []
    for r in range(1, rounds):
        sent = pack(tensors, r, rounds, members)
        sent, arrived = lax.optimization_barrier((sent, arrived))
        came = exchange(sent)
        results.append(attend(info, arrived))
        arrived = came
    sent = jnp.stack(results, axis=1)
    sent, arrived = lax.optimization_barrier((sent, arrived))
    came = exchange(sent)
    sent = attend(info, arrived)[:, None]
    sent, came, weight = lax.optimization_barrier((sent, came, weight))
    last = exchange(sent)
    total = project(came, weight, rounds, 0)
    return tuple(project(last, weight, rounds, rounds - 1, total))


def solution(mesh):
    split = P(("dp", "ulysses"), None)
    return jax.shard_map(
        shards,
        mesh=mesh,
        in_specs=(split,) * 7 + (P(),) * 3,
        out_specs=(split, split),
        check_vma=False,
    )
```

time: 261 us -> 220 us (0.84)
  waiting for transfers between devices: 136 us -> 116 us
  blocking collectives: 19.4 us -> 0 us
  local copies, waits for them, and re-layouts: 12.6 us -> 5.55 us
  starting transfers between devices: 27.1 us -> 32.5 us
  Pallas kernels: 46.9 us -> 44.1 us
  other arithmetic: 2 us -> 4.66 us
    all_to_all x5, waiting for transfers between devices: 135 us -> 111 us  [exchange(): return lax.all_to_all(x, 'ulysses', split_axis=0, concat_axis=0, tiled=True)]
    all_to_all x1 -> x0, blocking collectives: 19.4 us -> none  [exchange(): return lax.all_to_all(x, 'ulysses', split_axis=0, concat_axis=0, tiled=True)]
    unnamed x22 -> x19, local copies, waits for them, and re-layouts: 12.6 us -> 5.49 us
    ppermute x0 -> x4, waiting for transfers between devices: none -> 4.85 us  [the longest x3 3.22 us: hop(): return lax.ppermute(value, 'ulysses', pairs)]
    ppermute x0 -> x4, starting transfers between devices: none -> 3.99 us  [the longest x3 3.39 us: hop(): return lax.ppermute(value, 'ulysses', pairs)]
    pallas_call x7 -> x8, Pallas kernels: 46.9 us -> 44.1 us  [the longest x2 19.5 us: project(): pl.pallas_call(project_kernel, grid=(width // tile,), in_specs=[ANY] + [p...]
    another operation x0 -> x3, other arithmetic: none -> 2.74 us  [the longest x1 1.53 us: shards(): sent = jnp.stack(results, axis=1)]
  transfers between devices with their start and end apart: 6 -> 10, of which waited for: 5 -> 7; matrix products, arithmetic and copies ran while one was open for 1% -> 2% of each run, Pallas kernels for 12% -> 17%
where the time goes in v3:
time: 220 us; the launch traced here: 217 us
  waiting for transfers between devices  116 us (53%)
  Pallas kernels  44.1 us (20%)
  starting transfers between devices  32.5 us (15%)
  between operations  14.2 us (6%)
  local copies, waits for them, and re-layouts  5.55 us (3%)
  other arithmetic  4.66 us (2%)
    all_to_all x5, waiting for transfers between devices, exchange(): return lax.all_to_all(x, 'ulysses', split_axis=0, concat_axis=0, tiled=True)  111 us
    all_to_all x5, starting transfers between devices, exchange(): return lax.all_to_all(x, 'ulysses', split_axis=0, concat_axis=0, tiled=True)  28.5 us
    pallas_call x2, Pallas kernels, project(): pl.pallas_call(project_kernel, grid=(width // tile,), in_specs=[ANY] + [p...  19.5 us
    pallas_call x3, Pallas kernels, attend(): pl.pallas_call(attend_kernel, in_specs=[SMEM, ANY], out_specs=VMEM, out_s...  12.4 us
    pallas_call x3, Pallas kernels, pack(): pl.pallas_call(functools.partial(pack_kernel, r, rounds), in_specs=[ANY]...  12.3 us
    unnamed x19, local copies, waits for them, and re-layouts  5.49 us
  transfers between devices with their start and end apart: 10, of which 7 were waited for; matrix products, arithmetic and copies ran while one was open for 2% of the time, Pallas kernels for 17%

profile of v3, /device:TPU:19, one launch (start us, length us, event | category | flops | bytes accessed | tf_op | source)
XLA Modules:
  0.0 217.0 jit_solution(114799643961097798)
XLA Ops:
  7.2 1.9 collective-permute-start.1
  10.6 4.1 %pack.4 = bf16[8,6,256,128]{3,2,1,0:T(8,128)(2,1)} custom-call(bf16[256,3072]{1,0:T(8,128)(2,1)} %refs_0_.5, bf16[256,3072]{1,0:T(8,128)(2,1)} %refs_1_.5, bf16[256,3072]{1,0:T(8,128)(2,1)} %refs_2_.5, bf16[256,3072]{1,0:T(8,128)(2,1)} %refs_3_.5, bf16[256,3072]{1,0:T(8,128)(2,1)} %refs_4_.5, bf16[256,3072]{1,0:T(8,128)(2,1)} %refs_5_.5), custom_call_target="tpu_custom_call" | custom-call | tf_op jit(solution)/shard_map/pack/pallas_call | solution.py:41
  14.7 3.2 %collective-permute-done = bf16[24,3072]{1,0:T(8,128)(2,1)S(1)} collective-permute-done((bf16[24,3072]{1,0:T(8,128)(2,1)}, bf16[24,3072]{1,0:T(8,128)(2,1)S(1)}, u32[]{:S(2)}, u32[]{:S(2)}) %collective-permute-start) | collective-permute-done | bytes 147488 | tf_op jit(solution)/shard_map/ppermute | solution.py:200
  18.8 1.6 collective-permute-done.3
  21.6 4.8 %all-to-all-start = ((bf16[8,6,256,128]{3,2,1,0:T(8,128)(2,1)}), bf16[8,6,256,128]{3,2,1,0:T(8,128)(2,1)S(1)}, u32[]{:S(2)}, u32[]{:S(2)}) async-start(bf16[8,6,256,128]{3,2,1,0:T(8,128)(2,1)} %pack.4), calls=%async_computation | async-start | bytes 6291456 | tf_op jit(solution)/shard_map/all_to_all | solution.py:195
  26.4 4.1 %pack.3 = bf16[8,6,256,128]{3,2,1,0:T(8,128)(2,1)} custom-call(bf16[256,3072]{1,0:T(8,128)(2,1)} %refs_0_.5, bf16[256,3072]{1,0:T(8,128)(2,1)} %refs_1_.5, bf16[256,3072]{1,0:T(8,128)(2,1)} %refs_2_.5, bf16[256,3072]{1,0:T(8,128)(2,1)} %refs_3_.5, bf16[256,3072]{1,0:T(8,128)(2,1)} %refs_4_.5, bf16[256,3072]{1,0:T(8,128)(2,1)} %refs_5_.5), custom_call_target="tpu_custom_call" | custom-call | tf_op jit(solution)/shard_map/pack/pallas_call | solution.py:41
  30.6 32.4 %all-to-all-done.x = bf16[8,6,256,128]{3,2,1,0:T(8,128)(2,1)S(1)} async-done(((bf16[8,6,256,128]{3,2,1,0:T(8,128)(2,1)}), bf16[8,6,256,128]{3,2,1,0:T(8,128)(2,1)S(1)}, u32[]{:S(2)}, u32[]{:S(2)}) %all-to-all-start) | async-done | bytes 3145760 | tf_op jit(solution)/shard_map/all_to_all | solution.py:195
  62.9 6.4 %all-to-all-start.1 = ((bf16[8,6,256,128]{3,2,1,0:T(8,128)(2,1)}), bf16[8,6,256,128]{3,2,1,0:T(8,128)(2,1)}, u32[]{:S(2)}, u32[]{:S(2)}) async-start(bf16[8,6,256,128]{3,2,1,0:T(8,128)(2,1)} %pack.3), calls=%async_computation.1 | async-start | bytes 6291456 | tf_op jit(solution)/shard_map/all_to_all | solution.py:195
  69.3 4.1 %pack.5 = bf16[8,6,256,128]{3,2,1,0:T(8,128)(2,1)} custom-call(bf16[256,3072]{1,0:T(8,128)(2,1)} %refs_0_.5, bf16[256,3072]{1,0:T(8,128)(2,1)} %refs_1_.5, bf16[256,3072]{1,0:T(8,128)(2,1)} %refs_2_.5, bf16[256,3072]{1,0:T(8,128)(2,1)} %refs_3_.5, bf16[256,3072]{1,0:T(8,128)(2,1)} %refs_4_.5, bf16[256,3072]{1,0:T(8,128)(2,1)} %refs_5_.5), custom_call_target="tpu_custom_call" | custom-call | tf_op jit(solution)/shard_map/pack/pallas_call | solution.py:41
  73.5 32.5 %all-to-all-done.1.x = bf16[8,6,256,128]{3,2,1,0:T(8,128)(2,1)} async-done(((bf16[8,6,256,128]{3,2,1,0:T(8,128)(2,1)}), bf16[8,6,256,128]{3,2,1,0:T(8,128)(2,1)}, u32[]{:S(2)}, u32[]{:S(2)}) %all-to-all-start.1) | async-done | bytes 3145760 | tf_op jit(solution)/shard_map/all_to_all | solution.py:195
  105.9 6.3 %all-to-all-start.2 = ((bf16[8,6,256,128]{3,2,1,0:T(8,128)(2,1)}), bf16[8,6,256,128]{3,2,1,0:T(8,128)(2,1)}, u32[]{:S(2)}, u32[]{:S(2)}) async-start(bf16[8,6,256,128]{3,2,1,0:T(8,128)(2,1)} %pack.5), calls=%async_computation.2 | async-start | bytes 6291456 | tf_op jit(solution)/shard_map/all_to_all | solution.py:195
  112.9 1.3 pad_add_fusion.info
  114.2 3.1 %attend.3 = bf16[8,2,256,128]{3,2,1,0:T(8,128)(2,1)S(1)} custom-call(s32[2]{0:T(128)S(1)} %pad_add_fusion.info, bf16[8,6,256,128]{3,2,1,0:T(8,128)(2,1)S(1)} %all-to-all-done.x), custom_call_target="tpu_custom_call" | custom-call | tf_op jit(solution)/shard_map/attend/pallas_call | solution.py:123
  117.3 4.2 %attend.4 = bf16[8,2,256,128]{3,2,1,0:T(8,128)(2,1)S(1)} custom-call(s32[2]{0:T(128)S(1)} %pad_add_fusion.info, bf16[8,6,256,128]{3,2,1,0:T(8,128)(2,1)} %all-to-all-done.1.x), custom_call_target="tpu_custom_call" | custom-call | tf_op jit(solution)/shard_map/attend/pallas_call | solution.py:123
  121.5 1.5 pad_maximum_fusion
  123.0 25.9 %all-to-all-done.2.x = bf16[8,6,256,128]{3,2,1,0:T(8,128)(2,1)} async-done(((bf16[8,6,256,128]{3,2,1,0:T(8,128)(2,1)}), bf16[8,6,256,128]{3,2,1,0:T(8,128)(2,1)}, u32[]{:S(2)}, u32[]{:S(2)}) %all-to-all-start.2) | async-done | bytes 3145760 | tf_op jit(solution)/shard_map/all_to_all | solution.py:195
  148.9 5.5 %all-to-all-start.3 = ((bf16[8,2,2,256,128]{4,3,2,1,0:T(8,128)(2,1)}), bf16[8,2,2,256,128]{4,3,2,1,0:T(8,128)(2,1)S(1)}, u32[]{:S(2)}, u32[]{:S(2)}) async-start(bf16[8,2,2,256,128]{4,3,2,1,0:T(8,128)(2,1)} %pad_maximum_fusion), calls=%async_computation.3 | async-start | bytes 4194304 | tf_op jit(solution)/shard_map/all_to_all | solution.py:195
  154.4 5.1 %attend.5 = bf16[8,2,256,128]{3,2,1,0:T(8,128)(2,1)} custom-call(s32[2]{0:T(128)S(1)} %pad_add_fusion.info, bf16[8,6,256,128]{3,2,1,0:T(8,128)(2,1)} %all-to-all-done.2.x), custom_call_target="tpu_custom_call" | custom-call | tf_op jit(solution)/shard_map/attend/pallas_call | solution.py:123
  159.5 20.1 %all-to-all-done.3.moved = bf16[8,2,2,256,128]{4,3,2,1,0:T(8,128)(2,1)S(1)} async-done(((bf16[8,2,2,256,128]{4,3,2,1,0:T(8,128)(2,1)}), bf16[8,2,2,256,128]{4,3,2,1,0:T(8,128)(2,1)S(1)}, u32[]{:S(2)}, u32[]{:S(2)}) %all-to-all-start.3) | async-done | bytes 2097184 | tf_op jit(solution)/shard_map/all_to_all | solution.py:195
  179.6 5.4 %all-to-all-start.4 = ((bf16[8,1,2,256,128]{4,3,2,1,0:T(8,128)(2,1)}), bf16[8,1,2,256,128]{4,3,2,1,0:T(8,128)(2,1)S(1)}, u32[]{:S(2)}, u32[]{:S(2)}) async-start(bf16[8,1,2,256,128]{4,3,2,1,0:T(8,128)(2,1)} %bitcast.4), calls=%async_computation.4 | async-start | bytes 2097152 | tf_op jit(solution)/shard_map/all_to_all | solution.py:195
  185.0 11.2 %project.2.refs_0_ = f32[512,3072]{1,0:T(8,128)S(1)} custom-call(bf16[8,2,2,256,128]{4,3,2,1,0:T(8,128)(2,1)S(1)} %all-to-all-done.3.moved, bf16[8,3,128,3072]{3,2,1,0:T(8,128)(2,1)} %bitcast.27), custom_call_target="tpu_custom_call" | custom-call | tf_op jit(solution)/shard_map/project/pallas_call | solution.py:171
  196.3 2.6 %copy-done = f32[512,3072]{1,0:T(8,128)} copy-done((f32[512,3072]{1,0:T(8,128)}, f32[512,3072]{1,0:T(8,128)S(1)}, u32[]{:S(2)}) %copy-start) | copy-done | bytes 6291480
  199.1 2.8 %copy-done.1 = f32[512,3072]{1,0:T(8,128)S(1)} copy-done((f32[512,3072]{1,0:T(8,128)S(1)}, f32[512,3072]{1,0:T(8,128)}, u32[]{:S(2)}) %copy-start.1) | copy-done | bytes 6291480
  201.9 8.3 %project.3 = (bf16[256,3072]{1,0:T(8,128)(2,1)}, bf16[256,3072]{1,0:T(8,128)(2,1)}) custom-call(bf16[8,1,2,256,128]{4,3,2,1,0:T(8,128)(2,1)S(1)} %all-to-all-done.4.moved, bf16[8,3,128,3072]{3,2,1,0:T(8,128)(2,1)} %bitcast.28, f32[512,3072]{1,0:T(8,128)S(1)} %copy-done.1), custom_call_target="tpu_custom_call" | custom-call | tf_op jit(solution)/shard_map/project/pallas_call | solution.py:171
  (31 shorter events, 4.3 us)
Async XLA Ops:
  7.2 172.5 %all-gather.2.cloned.1.call-start = ((), (), s32[]{:S(2)}) async-start(), calls=%async_computation.5 | async-start | bytes 20054016 | tf_op jit(solution)/shard_map/all_gather | solution.py:227
  7.2 7.5 %collective-permute-start.1 = (bf16[24,3072]{1,0:T(8,128)(2,1)}, bf16[24,3072]{1,0:T(8,128)(2,1)S(1)}, u32[]{:S(2)}, u32[]{:S(2)}) collective-permute-start(bf16[24,3072]{1,0:T(8,128)(2,1)} %param.16), channel_id=1, source_target_pairs={{0,4},{1,5},{2,6},{3,7},{4,0},{5,1},{6,2},{7,3},{8,12},{9,13},{10,... | collective-permute-start | bytes 442376 | tf_op jit(solution)/shard_map/ppermute | solution.py:200
  9.1 8.8 %collective-permute-start = (bf16[24,3072]{1,0:T(8,128)(2,1)}, bf16[24,3072]{1,0:T(8,128)(2,1)S(1)}, u32[]{:S(2)}, u32[]{:S(2)}) collective-permute-start(bf16[24,3072]{1,0:T(8,128)(2,1)} %param.16), channel_id=1, source_target_pairs={{0,6},{1,7},{2,0},{3,1},{4,2},{5,3},{6,4},{7,5},{8,14},{9,15},{10,... | collective-permute-start | bytes 442376 | tf_op jit(solution)/shard_map/ppermute | solution.py:200
  10.3 7.6 %collective-permute-start.2 = (bf16[24,3072]{1,0:T(8,128)(2,1)}, bf16[24,3072]{1,0:T(8,128)(2,1)S(1)}, u32[]{:S(2)}, u32[]{:S(2)}) collective-permute-start(bf16[24,3072]{1,0:T(8,128)(2,1)} %param.16), channel_id=1, source_target_pairs={{0,2},{1,3},{2,4},{3,5},{4,6},{5,7},{6,0},{7,1},{8,10},{9,11},{10,... | collective-permute-start | bytes 442376 | tf_op jit(solution)/shard_map/ppermute | solution.py:200
  10.6 7.4 %copy-start.2 = (bf16[24,3072]{1,0:T(8,128)(2,1)S(1)}, bf16[24,3072]{1,0:T(8,128)(2,1)}, u32[]{:S(2)}) copy-start(bf16[24,3072]{1,0:T(8,128)(2,1)} %param.16) | copy-start | bytes 442372
  18.2 2.2 %collective-permute-start.3 = (bf16[4,24,3072]{2,1,0:T(8,128)(2,1)S(1)}, bf16[4,24,3072]{2,1,0:T(8,128)(2,1)S(1)}, u32[]{:S(2)}, u32[]{:S(2)}) collective-permute-start(bf16[4,24,3072]{2,1,0:T(8,128)(2,1)S(1)} %constant_dynamic-slice_fusion), channel_id=1, source_target_pairs={{0,1},{1,0},{2,3},{3,2},{4,5},{5,4},{6,7},{7,6},{8,9},{9,8},{10,11... | collective-permute-start | bytes 1769480 | tf_op jit(solution)/shard_map/ppermute | solution.py:205
  21.6 41.3 %all-to-all-start = ((bf16[8,6,256,128]{3,2,1,0:T(8,128)(2,1)}), bf16[8,6,256,128]{3,2,1,0:T(8,128)(2,1)S(1)}, u32[]{:S(2)}, u32[]{:S(2)}) async-start(bf16[8,6,256,128]{3,2,1,0:T(8,128)(2,1)} %pack.4), calls=%async_computation | async-start | bytes 6291456 | tf_op jit(solution)/shard_map/all_to_all | solution.py:195
  62.9 43.0 %all-to-all-start.1 = ((bf16[8,6,256,128]{3,2,1,0:T(8,128)(2,1)}), bf16[8,6,256,128]{3,2,1,0:T(8,128)(2,1)}, u32[]{:S(2)}, u32[]{:S(2)}) async-start(bf16[8,6,256,128]{3,2,1,0:T(8,128)(2,1)} %pack.3), calls=%async_computation.1 | async-start | bytes 6291456 | tf_op jit(solution)/shard_map/all_to_all | solution.py:195
  73.4 38.9 %copy-start.3 = (s32[32]{0:T(128)S(1)}, s32[32]{0:T(128)}, u32[]{:S(2)}) copy-start(s32[32]{0:T(128)} %param.17) | copy-start | bytes 388
  73.4 38.9 %copy-start.4 = (s32[32]{0:T(128)S(1)}, s32[32]{0:T(128)}, u32[]{:S(2)}) copy-start(s32[32]{0:T(128)} %param.18) | copy-start | bytes 388
  73.5 38.8 %copy-start.5 = (s32[32]{0:T(128)S(1)}, s32[32]{0:T(128)}, u32[]{:S(2)}) copy-start(s32[32]{0:T(128)} %param.19) | copy-start | bytes 388
  105.9 42.9 %all-to-all-start.2 = ((bf16[8,6,256,128]{3,2,1,0:T(8,128)(2,1)}), bf16[8,6,256,128]{3,2,1,0:T(8,128)(2,1)}, u32[]{:S(2)}, u32[]{:S(2)}) async-start(bf16[8,6,256,128]{3,2,1,0:T(8,128)(2,1)} %pack.5), calls=%async_computation.2 | async-start | bytes 6291456 | tf_op jit(solution)/shard_map/all_to_all | solution.py:195
  148.9 30.7 %all-to-all-start.3 = ((bf16[8,2,2,256,128]{4,3,2,1,0:T(8,128)(2,1)}), bf16[8,2,2,256,128]{4,3,2,1,0:T(8,128)(2,1)S(1)}, u32[]{:S(2)}, u32[]{:S(2)}) async-start(bf16[8,2,2,256,128]{4,3,2,1,0:T(8,128)(2,1)} %pad_maximum_fusion), calls=%async_computation.3 | async-start | bytes 4194304 | tf_op jit(solution)/shard_map/all_to_all | solution.py:195
  179.6 19.5 %all-to-all-start.4 = ((bf16[8,1,2,256,128]{4,3,2,1,0:T(8,128)(2,1)}), bf16[8,1,2,256,128]{4,3,2,1,0:T(8,128)(2,1)S(1)}, u32[]{:S(2)}, u32[]{:S(2)}) async-start(bf16[8,1,2,256,128]{4,3,2,1,0:T(8,128)(2,1)} %bitcast.4), calls=%async_computation.4 | async-start | bytes 2097152 | tf_op jit(solution)/shard_map/all_to_all | solution.py:195
  196.3 2.6 %copy-start = (f32[512,3072]{1,0:T(8,128)}, f32[512,3072]{1,0:T(8,128)S(1)}, u32[]{:S(2)}) copy-start(f32[512,3072]{1,0:T(8,128)S(1)} %project.2.refs_0_) | copy-start | bytes 18874372
  199.1 2.8 %copy-start.1 = (f32[512,3072]{1,0:T(8,128)S(1)}, f32[512,3072]{1,0:T(8,128)}, u32[]{:S(2)}) copy-start(f32[512,3072]{1,0:T(8,128)} %copy-done) | copy-start | bytes 18874372
Sparse Core Ops, SparseCore 0:
  21.7 123.9 all-gather.1

commit v4 on v3

v4 whole, which is shorter than its diff:
```python
import functools
import math

import jax
import jax.numpy as jnp
from jax import lax
from jax.experimental import pallas as pl
from jax.experimental.pallas import tpu as pltpu
from jax.sharding import PartitionSpec as P

HEAD_DIM = 128
FRAME = 128
FRAMES_MOST = 8
CORES = 2
LOG2E = 1.4426950408889634
BF16 = jnp.bfloat16
ANY = pl.BlockSpec(memory_space=pl.ANY)
SMEM = pl.BlockSpec(memory_space=pltpu.SMEM)
VMEM = pl.BlockSpec(memory_space=pltpu.VMEM)


def run_copies(pairs, sems):
    copies = [pltpu.make_async_copy(a, b, sems.at[i]) for i, (a, b) in enumerate(pairs)]
    for copy in copies:
        copy.start()
    for copy in copies:
        copy.wait()


def member(block, members, back=False):
    u = lax.axis_index("ulysses")
    x, c = lax.div(u, CORES), lax.rem(u, CORES)
    line = members // CORES
    k, f = block // CORES, block % CORES
    return lax.rem(x + (line - k if back else k), line) * CORES + (1 - c if f else c)


def pack_kernel(first, rounds, members, blocks, *refs):
    tensors, outs, (held, sems, out_sems) = refs[:6], refs[6:-3], refs[-3:]
    size = outs[0].shape[0]
    loads, stores = [], []
    for j, b in enumerate(blocks):
        for i in range(size):
            head = member(b, members) * rounds + first + i
            at = pl.ds(pl.multiple_of(head * HEAD_DIM, HEAD_DIM), HEAD_DIM)
            for t in range(6):
                source, to = tensors[t].at[:, at], held.at[j, i, t]
                loads.append(pltpu.make_async_copy(source, to, sems.at[j, i, t]))
        stores.append(pltpu.make_async_copy(held.at[j], outs[j], out_sems.at[j]))
    for load in loads:
        load.start()
    for j, store in enumerate(stores):
        for load in loads[j * size * 6 : (j + 1) * size * 6]:
            load.wait()
        store.start()
    for store in stores:
        store.wait()


def pack(tensors, first, size, rounds, members, blocks):
    rows = tensors[0].shape[0]
    count = len(blocks)
    return pl.pallas_call(
        functools.partial(pack_kernel, first, rounds, members, blocks),
        in_specs=[ANY] * 6,
        out_specs=[ANY] * count,
        out_shape=[jax.ShapeDtypeStruct((size, 6, rows, HEAD_DIM), BF16)] * count,
        scratch_shapes=[
            pltpu.VMEM((count, size, 6, rows, HEAD_DIM), BF16),
            pltpu.SemaphoreType.DMA((count, size, 6)),
            pltpu.SemaphoreType.DMA((count,)),
        ],
        name="pack",
    )(*tensors)


def nt_dot(a, b):
    return lax.dot_general(a, b, (((1,), (1,)), ((), ())), preferred_element_type=jnp.float32)


def attend_kernel(members, info, *refs):
    moved, (out, qq, kk, vv, sems) = refs[:members], refs[members:]
    size, _, rows, _ = moved[0].shape
    per = rows // FRAME
    first_count, second_count = info[0], info[1]
    used = first_count + second_count
    factor = LOG2E / math.sqrt(HEAD_DIM)
    scale = 1.0 / math.sqrt(HEAD_DIM)

    def store(head, frame, which, value):
        at = pl.multiple_of(lax.rem(frame, per) * FRAME, FRAME)
        out[lax.div(frame, per), head, which, pl.ds(at, FRAME), :] = value

    def one_video(head, start, count):
        keys = pl.ds(pl.multiple_of(start * FRAME, FRAME), count * FRAME)

        def block(frame, frames):
            at = pl.ds(pl.multiple_of(frame * FRAME, FRAME), frames * FRAME)
            s = nt_dot(qq[at, HEAD_DIM:], kk[keys, :HEAD_DIM]) * factor
            t = nt_dot(qq[at, :], kk[keys, :]) * scale
            e = jnp.exp2(s - jnp.max(s, axis=1, keepdims=True))
            p = e * (1.0 / jnp.sum(e, axis=1, keepdims=True))
            mean = jnp.sum(p * t, axis=1, keepdims=True)
            low = p.astype(BF16)
            turned = (p * (t - mean)).astype(BF16)
            both = jnp.dot(low, vv[keys, :], preferred_element_type=jnp.float32)
            more = jnp.dot(turned, vv[keys, :HEAD_DIM], preferred_element_type=jnp.float32)
            primal = both[:, :HEAD_DIM].astype(BF16)
            tangent = (both[:, HEAD_DIM:] + more).astype(BF16)
            for i in range(frames):
                part = slice(i * FRAME, (i + 1) * FRAME)
                store(head, frame + i, 0, primal[part])
                store(head, frame + i, 1, tangent[part])

        def two_frames(i, carry):
            block(start + 2 * i, 2)
            return carry

        lax.fori_loop(0, count // 2, two_frames, 0)
        if count % 2:
            block(start + count - 1, 1)

    def one_head(head, carry):
        pairs = []
        for b in range(members):
            at = pl.ds(pl.multiple_of(member(b, members, True) * rows, rows), rows)
            for t, (to, half) in enumerate(((qq, 1), (kk, 0), (vv, 0), (qq, 0), (kk, 1), (vv, 1))):
                part = slice(half * HEAD_DIM, (half + 1) * HEAD_DIM)
                pairs.append((moved[b].at[head, t], to.at[at, part]))
        run_copies(pairs, sems)

        def video(i, carry):
            start = jnp.where(i == 0, 0, first_count)
            count = jnp.where(i == 0, first_count, second_count)
            for frames in range(1, FRAMES_MOST + 1):
                pl.when(count == frames)(functools.partial(one_video, head, start, frames))
            return carry

        def blank(frame, carry):
            nothing = jnp.zeros((FRAME, HEAD_DIM), BF16)
            store(head, frame, 0, nothing)
            store(head, frame, 1, nothing)
            return carry

        lax.fori_loop(0, 2, video, 0)
        lax.fori_loop(used, members * per, blank, 0)
        return carry

    lax.fori_loop(0, size, one_head, 0)


def attend(info, moved):
    members = len(moved)
    size, _, rows, _ = moved[0].shape
    return pl.pallas_call(
        functools.partial(attend_kernel, members),
        in_specs=[SMEM] + [ANY] * members,
        out_specs=VMEM,
        out_shape=jax.ShapeDtypeStruct((members, size, 2, rows, HEAD_DIM), BF16),
        scratch_shapes=[pltpu.VMEM((members * rows, 2 * HEAD_DIM), BF16)] * 3
        + [pltpu.SemaphoreType.DMA((6 * members,))],
        compiler_params=pltpu.CompilerParams(vmem_limit_bytes=40 * 2**20),
        name="attend",
    )(info, *moved)


def project_kernel(moved, w, *refs):
    if len(refs) == 5:
        total, out, tangent, held, sems = refs
    else:
        out, held, sems = refs
        total = None
    members, size, _, rows, _ = moved.shape

    @pl.when(pl.program_id(0) == 0)
    def _():
        pairs = []
        for u in range(members):
            for i in range(size):
                at = slice((u * size + i) * HEAD_DIM, (u * size + i + 1) * HEAD_DIM)
                for which in range(2):
                    down = slice(which * rows, (which + 1) * rows)
                    pairs.append((moved.at[u, i, which], held.at[down, at]))
        run_copies(pairs, sems)

    depth = held.shape[1]
    product = jnp.dot(held[...], w[...].reshape(depth, -1), preferred_element_type=jnp.float32)
    if total is None:
        out[...] = product
    else:
        out[...] = (total[:rows] + product[:rows]).astype(BF16)
        tangent[...] = (total[rows:] + product[rows:]).astype(BF16)


def project(moved, weight, rounds, first, total=None):
    members, size, _, rows, _ = moved.shape
    width = weight.shape[1]
    tile = 512
    by_round = weight.reshape(members, rounds, HEAD_DIM, width)
    sum_spec = pl.BlockSpec((2 * rows, tile), lambda step: (0, step))
    half_spec = pl.BlockSpec((rows, tile), lambda step: (0, step))
    last = total is not None
    return pl.pallas_call(
        project_kernel,
        grid=(width // tile,),
        in_specs=[ANY]
        + [pl.BlockSpec((members, size, HEAD_DIM, tile), lambda step: (0, first // size, 0, step))]
        + [sum_spec] * last,
        out_specs=[half_spec, half_spec] if last else sum_spec,
        scratch_shapes=[
            pltpu.VMEM((2 * rows, members * size * HEAD_DIM), BF16),
            pltpu.SemaphoreType.DMA((2 * members * size,)),
        ],
        out_shape=[jax.ShapeDtypeStruct((rows, width), BF16)] * 2
        if last
        else jax.ShapeDtypeStruct((2 * rows, width), jnp.float32),
        compiler_params=pltpu.CompilerParams(vmem_limit_bytes=56 * 2**20),
        name="project",
    )(moved, by_round, *([total] if last else []))


def after(value, *done):
    return lax.optimization_barrier((value, done))[0]


def hop(value, k, f=0):
    members = lax.axis_size("ulysses")
    pairs = [(u, (u + k * CORES) % members ^ f) for u in range(members)]
    return lax.ppermute(value, "ulysses", pairs)


def gather_line(shard, ready):
    u = lax.axis_index("ulysses")
    x, core = u // CORES, u % CORES
    line = lax.axis_size("ulysses") // CORES
    back = [hop(shard, k) for k in range(line - 1, 0, -1)]
    back = after(tuple(back), ready)
    ring = jnp.stack([*back, shard] * 2)
    mine = lax.dynamic_slice_in_dim(ring, line - 1 - x, line, 0)
    theirs = hop(mine, 0, 1)
    pair = [jnp.where(core == 0, mine, theirs), jnp.where(core == 0, theirs, mine)]
    return jnp.stack(pair, axis=1).reshape(-1, shard.shape[1])


def exchange(x):
    return lax.all_to_all(x, "ulysses", split_axis=0, concat_axis=0, tiled=True)


def send(blocks):
    return {b: hop(block, b // CORES, b % CORES) if b else block for b, block in blocks.items()}


def shards(q, k, v, dq, dk, dv, out_weight, frame_counts, token_offsets, video_group):
    members = lax.axis_size("ulysses")
    rounds = q.shape[1] // HEAD_DIM // members
    tensors = (q, k, v, dq, dk, dv)
    same = tuple(range(CORES, members, CORES))
    other = tuple(range(CORES + 1, members, CORES)) + (1, 0)

    def packed(first, size, blocks):
        return dict(zip(blocks, pack(tensors, first, size, rounds, members, blocks)))

    def in_order(arrived):
        return [arrived[b] for b in range(members)]

    early = packed(0, rounds - 1, same) | packed(0, rounds - 1, other)
    near = gather_line(out_weight, early)
    weight = lax.all_gather(near, "dp", axis=0, tiled=True)
    arrived = in_order(send(early))
    mine = video_group == lax.axis_index("dp")
    info = jnp.stack(
        [
            jnp.sum(jnp.where(mine & (token_offsets == 0), frame_counts, 0)),
            jnp.sum(jnp.where(mine & (token_offsets > 0), frame_counts, 0)),
        ]
    ).astype(jnp.int32)
    late = packed(rounds - 1, 1, same + other)
    late, arrived = lax.optimization_barrier((late, arrived))
    late, result = in_order(send(late)), attend(info, arrived)
    result, late = lax.optimization_barrier((result, late))
    moved, result = exchange(result), attend(info, late)
    result, moved, weight = lax.optimization_barrier((result, moved, weight))
    last, total = exchange(result), project(moved, weight, rounds, 0)
    return tuple(project(last, weight, rounds, rounds - 1, total))


def solution(mesh):
    split = P(("dp", "ulysses"), None)
    return jax.shard_map(
        shards,
        mesh=mesh,
        in_specs=(split,) * 7 + (P(),) * 3,
        out_specs=(split, split),
        check_vma=False,
    )
```

time: 220 us -> 206 us (0.936)
  waiting for transfers between devices: 116 us -> 73.1 us
  starting transfers between devices: 32.5 us -> 52.6 us
  Pallas kernels: 44.1 us -> 58.9 us
  local copies, waits for them, and re-layouts: 5.55 us -> 0.93 us
    all_to_all x5 -> x2, waiting for transfers between devices: 111 us -> 16.7 us  [exchange(): return lax.all_to_all(x, 'ulysses', split_axis=0, concat_axis=0, tiled=True)]
    ppermute x3 -> x18, waiting for transfers between devices: 3.22 us -> 56.4 us  [hop(): return lax.ppermute(value, 'ulysses', pairs)]
    ppermute x3 -> x18, starting transfers between devices: 3.39 us -> 42.6 us  [hop(): return lax.ppermute(value, 'ulysses', pairs)]
    all_to_all x5 -> x2, starting transfers between devices: 28.5 us -> 9.89 us  [exchange(): return lax.all_to_all(x, 'ulysses', split_axis=0, concat_axis=0, tiled=True)]
    pallas_call x6 -> x5, Pallas kernels: 24.6 us -> 34.7 us  [the longest x2 24.1 us: attend(): pl.pallas_call(functools.partial(attend_kernel, members), in_specs=[SMEM]...]
    pallas_call x2, Pallas kernels: 19.5 us -> 24.2 us  [project(): pl.pallas_call(project_kernel, grid=(width // tile,), in_specs=[ANY] + [p...]
    unnamed x19 -> x25, local copies, waits for them, and re-layouts: 5.49 us -> 0.87 us
  transfers between devices with their start and end apart: 10 -> 21, of which waited for: 7 -> 10; matrix products, arithmetic and copies ran while one was open for 2% -> 1% of each run, Pallas kernels for 17% -> 24%
where the time goes in v4:
time: 206 us; the launch traced here: 203 us
  waiting for transfers between devices  73.1 us (35%)
  Pallas kernels  58.9 us (29%)
  starting transfers between devices  52.6 us (26%)
  between operations  14.3 us (7%)
  other arithmetic  3.3 us (2%)
    ppermute x18, waiting for transfers between devices, hop(): return lax.ppermute(value, 'ulysses', pairs)  56.4 us
    ppermute x18, starting transfers between devices, hop(): return lax.ppermute(value, 'ulysses', pairs)  42.6 us
    pallas_call x2, Pallas kernels, project(): pl.pallas_call(project_kernel, grid=(width // tile,), in_specs=[ANY] + [p...  24.2 us
    pallas_call x2, Pallas kernels, attend(): pl.pallas_call(functools.partial(attend_kernel, members), in_specs=[SMEM]...  24.1 us
    all_to_all x2, waiting for transfers between devices, exchange(): return lax.all_to_all(x, 'ulysses', split_axis=0, concat_axis=0, tiled=True)  16.7 us
    pallas_call x3, Pallas kernels, pack(): pl.pallas_call(functools.partial(pack_kernel, first, rounds, members, blo...  10.7 us
    all_to_all x2, starting transfers between devices, exchange(): return lax.all_to_all(x, 'ulysses', split_axis=0, concat_axis=0, tiled=True)  9.89 us
  transfers between devices with their start and end apart: 21, of which 10 were waited for; matrix products, arithmetic and copies ran while one was open for 1% of the time, Pallas kernels for 24%

profile of v4, /device:TPU:19, one launch (start us, length us, event | category | flops | bytes accessed | tf_op | source)
XLA Modules:
  0.0 203.1 jit_solution(7787627958038571862)
XLA Ops:
  7.2 1.9 collective-permute-start.15
  10.6 2.9 %pack.5 = (bf16[2,6,256,128]{3,2,1,0:T(8,128)(2,1)}, bf16[2,6,256,128]{3,2,1,0:T(8,128)(2,1)}, bf16[2,6,256,128]{3,2,1,0:T(8,128)(2,1)}) custom-call(bf16[256,3072]{1,0:T(8,128)(2,1)} %refs_0_.5, bf16[256,3072]{1,0:T(8,128)(2,1)} %refs_1_.5, bf16[256,3072]{1,0:T(8,128)(2,1)} %refs_2_.5, bf16[256,3072]{1,0:T(8,128)(2,1)} %refs_3_.5, ...), custom_call_target="tpu_custom_call" | custom-call | tf_op jit(solution)/shard_map/pack/pallas_call | solution.py:63
  13.6 4.2 %pack.4 = (bf16[2,6,256,128]{3,2,1,0:T(8,128)(2,1)}, bf16[2,6,256,128]{3,2,1,0:T(8,128)(2,1)}, bf16[2,6,256,128]{3,2,1,0:T(8,128)(2,1)}, bf16[2,6,256,128]{3,2,1,0:T(8,128)(2,1)}, bf16[2,6,256,128]{3,2,1,0:T(8,128)(2,1)}) custom-call(bf16[256,3072]{1,0:T(8,128)(2,1)} %refs_0_.5, bf16[256,3072]{1,0:T(8,128)(2,1)} %refs_1_.5, bf16[256,3072]{1,0:T(8,128)(2,1)} %refs_2_.5, ...), custom_call_target="tpu_custom_call" | custom-call | tf_op jit(solution)/shard_map/pack/pallas_call | solution.py:63
  19.7 1.6 collective-permute-done.17
  22.9 2.7 %collective-permute-start.3 = (bf16[2,6,256,128]{3,2,1,0:T(8,128)(2,1)}, bf16[2,6,256,128]{3,2,1,0:T(8,128)(2,1)S(1)}, u32[]{:S(2)}, u32[]{:S(2)}) collective-permute-start(bf16[2,6,256,128]{3,2,1,0:T(8,128)(2,1)} %get-tuple-element.61), channel_id=1, source_target_pairs={{0,4},{1,5},{2,6},{3,7},{4,0},{5,1},{6,2},{7,3},{8,12},{9,13},{10,... | collective-permute-start | bytes 2359304 | tf_op jit(solution)/shard_map/ppermute | solution.py:229
  28.3 13.4 %collective-permute-done.1.refs_2_ = bf16[2,6,256,128]{3,2,1,0:T(8,128)(2,1)S(1)} collective-permute-done((bf16[2,6,256,128]{3,2,1,0:T(8,128)(2,1)}, bf16[2,6,256,128]{3,2,1,0:T(8,128)(2,1)S(1)}, u32[]{:S(2)}, u32[]{:S(2)}) %collective-permute-start.1) | collective-permute-done | bytes 786464 | tf_op jit(solution)/shard_map/ppermute | solution.py:229
  41.7 4.1 %collective-permute-start.4 = (bf16[2,6,256,128]{3,2,1,0:T(8,128)(2,1)}, bf16[2,6,256,128]{3,2,1,0:T(8,128)(2,1)}, u32[]{:S(2)}, u32[]{:S(2)}) collective-permute-start(bf16[2,6,256,128]{3,2,1,0:T(8,128)(2,1)} %get-tuple-element.62), channel_id=1, source_target_pairs={{0,5},{1,4},{2,7},{3,6},{4,1},{5,0},{6,3},{7,2},{8,13},{9,12},{10,... | collective-permute-start | bytes 2359304 | tf_op jit(solution)/shard_map/ppermute | solution.py:229
  45.9 17.5 %collective-permute-start.6 = (bf16[2,6,256,128]{3,2,1,0:T(8,128)(2,1)}, bf16[2,6,256,128]{3,2,1,0:T(8,128)(2,1)}, u32[]{:S(2)}, u32[]{:S(2)}) collective-permute-start(bf16[2,6,256,128]{3,2,1,0:T(8,128)(2,1)} %get-tuple-element.64), channel_id=1, source_target_pairs={{0,7},{1,6},{2,1},{3,0},{4,3},{5,2},{6,5},{7,4},{8,15},{9,14},{10,... | collective-permute-start | bytes 2359304 | tf_op jit(solution)/shard_map/ppermute | solution.py:229
  63.4 3.5 %pack.3 = (bf16[1,6,256,128]{3,2,1,0:T(8,128)(2,1)}, bf16[1,6,256,128]{3,2,1,0:T(8,128)(2,1)}, bf16[1,6,256,128]{3,2,1,0:T(8,128)(2,1)}, bf16[1,6,256,128]{3,2,1...) custom-call(bf16[256,3072]{1,0:T(8,128)(2,1)} %refs_0_.5, ...), custom_call_target="tpu_custom_call" | custom-call | tf_op jit(solution)/shard_map/pack/pallas_call | solution.py:63
  66.9 10.2 %collective-permute-done.2.refs_3_ = bf16[2,6,256,128]{3,2,1,0:T(8,128)(2,1)} collective-permute-done((bf16[2,6,256,128]{3,2,1,0:T(8,128)(2,1)}, bf16[2,6,256,128]{3,2,1,0:T(8,128)(2,1)}, u32[]{:S(2)}, u32[]{:S(2)}) %collective-permute-start.2) | collective-permute-done | bytes 786464 | tf_op jit(solution)/shard_map/ppermute | solution.py:229
  77.1 2.1 %collective-permute-done.4.refs_5_ = bf16[2,6,256,128]{3,2,1,0:T(8,128)(2,1)} collective-permute-done((bf16[2,6,256,128]{3,2,1,0:T(8,128)(2,1)}, bf16[2,6,256,128]{3,2,1,0:T(8,128)(2,1)}, u32[]{:S(2)}, u32[]{:S(2)}) %collective-permute-start.4) | collective-permute-done | bytes 786464 | tf_op jit(solution)/shard_map/ppermute | solution.py:229
  79.2 15.6 %collective-permute-done.6.refs_7_ = bf16[2,6,256,128]{3,2,1,0:T(8,128)(2,1)} collective-permute-done((bf16[2,6,256,128]{3,2,1,0:T(8,128)(2,1)}, bf16[2,6,256,128]{3,2,1,0:T(8,128)(2,1)}, u32[]{:S(2)}, u32[]{:S(2)}) %collective-permute-start.6) | collective-permute-done | bytes 786464 | tf_op jit(solution)/shard_map/ppermute | solution.py:229
  95.3 3.2 %collective-permute-start.9 = (bf16[1,6,256,128]{3,2,1,0:T(8,128)(2,1)}, bf16[1,6,256,128]{3,2,1,0:T(8,128)(2,1)}, u32[]{:S(2)}, u32[]{:S(2)}) collective-permute-start(bf16[1,6,256,128]{3,2,1,0:T(8,128)(2,1)} %get-tuple-element.76), channel_id=1, source_target_pairs={{0,3},{1,2},{2,5},{3,4},{4,7},{5,6},{6,1},{7,0},{8,11},{9,10},{10,... | collective-permute-start | bytes 1179656 | tf_op jit(solution)/shard_map/ppermute | solution.py:229
  98.7 2.9 %collective-permute-start.11 = (bf16[1,6,256,128]{3,2,1,0:T(8,128)(2,1)}, bf16[1,6,256,128]{3,2,1,0:T(8,128)(2,1)}, u32[]{:S(2)}, u32[]{:S(2)}) collective-permute-start(bf16[1,6,256,128]{3,2,1,0:T(8,128)(2,1)} %get-tuple-element.78), channel_id=1, source_target_pairs={{0,5},{1,4},{2,7},{3,6},{4,1},{5,0},{6,3},{7,2},{8,13},{9,12},{10,... | collective-permute-start | bytes 1179656 | tf_op jit(solution)/shard_map/ppermute | solution.py:229
  101.6 4.7 %collective-permute-done.8.refs_2_ = bf16[1,6,256,128]{3,2,1,0:T(8,128)(2,1)S(1)} collective-permute-done((bf16[1,6,256,128]{3,2,1,0:T(8,128)(2,1)}, bf16[1,6,256,128]{3,2,1,0:T(8,128)(2,1)S(1)}, u32[]{:S(2)}, u32[]{:S(2)}) %collective-permute-start.8) | collective-permute-done | bytes 393248 | tf_op jit(solution)/shard_map/ppermute | solution.py:229
  107.1 3.6 %collective-permute-start.13 = (bf16[1,6,256,128]{3,2,1,0:T(8,128)(2,1)}, bf16[1,6,256,128]{3,2,1,0:T(8,128)(2,1)}, u32[]{:S(2)}, u32[]{:S(2)}) collective-permute-start(bf16[1,6,256,128]{3,2,1,0:T(8,128)(2,1)} %get-tuple-element.80), channel_id=1, source_target_pairs={{0,7},{1,6},{2,1},{3,0},{4,3},{5,2},{6,5},{7,4},{8,15},{9,14},{10,... | collective-permute-start | bytes 1179656 | tf_op jit(solution)/shard_map/ppermute | solution.py:229
  112.8 15.4 %attend.2 = bf16[8,2,2,256,128]{4,3,2,1,0:T(8,128)(2,1)} custom-call(s32[2]{0:T(128)S(1)} %pad_add_fusion.info, bf16[2,6,256,128]{3,2,1,0:T(8,128)(2,1)S(1)} %copy-done, bf16[2,6,256,128]{3,2,1,0:T(8,128)(2,1)} %collective-permute-done.refs_1_, bf16[2,6,256,128]{3,2,1,0:T(8,128)(2,1)S(1)} %collective-permute-done.1.refs_2_, ...), custom_call_target="tpu_custom_call" | custom-call | tf_op jit(solution)/shard_map/attend/pallas_call | solution.py:155
  128.3 8.5 %collective-permute-done.13.refs_7_ = bf16[1,6,256,128]{3,2,1,0:T(8,128)(2,1)} collective-permute-done((bf16[1,6,256,128]{3,2,1,0:T(8,128)(2,1)}, bf16[1,6,256,128]{3,2,1,0:T(8,128)(2,1)}, u32[]{:S(2)}, u32[]{:S(2)}) %collective-permute-start.13) | collective-permute-done | bytes 393248 | tf_op jit(solution)/shard_map/ppermute | solution.py:229
  136.8 3.8 %all-to-all-start = ((bf16[8,2,2,256,128]{4,3,2,1,0:T(8,128)(2,1)}), bf16[8,2,2,256,128]{4,3,2,1,0:T(8,128)(2,1)S(1)}, u32[]{:S(2)}, u32[]{:S(2)}) async-start(bf16[8,2,2,256,128]{4,3,2,1,0:T(8,128)(2,1)} %attend.2), calls=%async_computation | async-start | bytes 4194304 | tf_op jit(solution)/shard_map/all_to_all | solution.py:246
  140.6 8.7 %attend.3 = bf16[8,1,2,256,128]{4,3,2,1,0:T(8,128)(2,1)} custom-call(s32[2]{0:T(128)S(1)} %pad_add_fusion.info, bf16[1,6,256,128]{3,2,1,0:T(8,128)(2,1)S(1)} %copy-done.1, bf16[1,6,256,128]{3,2,1,0:T(8,128)(2,1)S(1)} %collective-permute-done.7.refs_1_, bf16[1,6,256,128]{3,2,1,0:T(8,128)(2,1)S(1)} %copy-done.3, ...), custom_call_target="tpu_custom_call" | custom-call | tf_op jit(solution)/shard_map/attend/pallas_call | solution.py:155
  149.3 16.4 %all-to-all-done.moved = bf16[8,2,2,256,128]{4,3,2,1,0:T(8,128)(2,1)S(1)} async-done(((bf16[8,2,2,256,128]{4,3,2,1,0:T(8,128)(2,1)}), bf16[8,2,2,256,128]{4,3,2,1,0:T(8,128)(2,1)S(1)}, u32[]{:S(2)}, u32[]{:S(2)}) %all-to-all-start) | async-done | bytes 2097184 | tf_op jit(solution)/shard_map/all_to_all | solution.py:246
  165.7 6.1 %all-to-all-start.1 = ((bf16[8,1,2,256,128]{4,3,2,1,0:T(8,128)(2,1)}), bf16[8,1,2,256,128]{4,3,2,1,0:T(8,128)(2,1)}, u32[]{:S(2)}, u32[]{:S(2)}) async-start(bf16[8,1,2,256,128]{4,3,2,1,0:T(8,128)(2,1)} %attend.3), calls=%async_computation.1 | async-start | bytes 2097152 | tf_op jit(solution)/shard_map/all_to_all | solution.py:246
  171.8 13.9 %project.2.refs_0_ = f32[512,3072]{1,0:T(8,128)} custom-call(bf16[8,2,2,256,128]{4,3,2,1,0:T(8,128)(2,1)} %copy-done.4, bf16[8,3,128,3072]{3,2,1,0:T(8,128)(2,1)} %bitcast.22), custom_call_target="tpu_custom_call" | custom-call | tf_op jit(solution)/shard_map/project/pallas_call | solution.py:203
  185.9 10.3 %project.3 = (bf16[256,3072]{1,0:T(8,128)(2,1)}, bf16[256,3072]{1,0:T(8,128)(2,1)}) custom-call(bf16[8,1,2,256,128]{4,3,2,1,0:T(8,128)(2,1)} %all-to-all-done.1.moved, bf16[8,3,128,3072]{3,2,1,0:T(8,128)(2,1)} %bitcast.23, f32[512,3072]{1,0:T(8,128)} %project.2.refs_0_), custom_call_target="tpu_custom_call" | custom-call | tf_op jit(solution)/shard_map/project/pallas_call | solution.py:203
  (57 shorter events, 11.4 us)
Async XLA Ops:
  7.2 158.5 %all-gather.2.cloned.1.call-start = ((), (), s32[]{:S(2)}) async-start(), calls=%async_computation.2 | async-start | bytes 20054016 | tf_op jit(solution)/shard_map/all_gather | solution.py:268
  7.2 10.6 %collective-permute-start.15 = (bf16[24,3072]{1,0:T(8,128)(2,1)}, bf16[24,3072]{1,0:T(8,128)(2,1)S(1)}, u32[]{:S(2)}, u32[]{:S(2)}) collective-permute-start(bf16[24,3072]{1,0:T(8,128)(2,1)} %param.16), channel_id=1, source_target_pairs={{0,4},{1,5},{2,6},{3,7},{4,0},{5,1},{6,2},{7,3},{8,12},{9,13},{10,... | collective-permute-start | bytes 442376 | tf_op jit(solution)/shard_map/ppermute | solution.py:229
  9.1 8.8 %collective-permute-start.14 = (bf16[24,3072]{1,0:T(8,128)(2,1)}, bf16[24,3072]{1,0:T(8,128)(2,1)S(1)}, u32[]{:S(2)}, u32[]{:S(2)}) collective-permute-start(bf16[24,3072]{1,0:T(8,128)(2,1)} %param.16), channel_id=1, source_target_pairs={{0,6},{1,7},{2,0},{3,1},{4,2},{5,3},{6,4},{7,5},{8,14},{9,15},{10,... | collective-permute-start | bytes 442376 | tf_op jit(solution)/shard_map/ppermute | solution.py:229
  10.3 7.6 %collective-permute-start.16 = (bf16[24,3072]{1,0:T(8,128)(2,1)}, bf16[24,3072]{1,0:T(8,128)(2,1)S(1)}, u32[]{:S(2)}, u32[]{:S(2)}) collective-permute-start(bf16[24,3072]{1,0:T(8,128)(2,1)} %param.16), channel_id=1, source_target_pairs={{0,2},{1,3},{2,4},{3,5},{4,6},{5,7},{6,0},{7,1},{8,10},{9,11},{10,... | collective-permute-start | bytes 442376 | tf_op jit(solution)/shard_map/ppermute | solution.py:229
  18.2 3.2 %collective-permute-start.17 = (bf16[4,24,3072]{2,1,0:T(8,128)(2,1)S(1)}, bf16[4,24,3072]{2,1,0:T(8,128)(2,1)S(1)}, u32[]{:S(2)}, u32[]{:S(2)}) collective-permute-start(bf16[4,24,3072]{2,1,0:T(8,128)(2,1)S(1)} %constant_dynamic-slice_fusion), channel_id=1, source_target_pairs={{0,1},{1,0},{2,3},{3,2},{4,5},{5,4},{6,7},{7,6},{8,9},{9,8},{10,11... | collective-permute-start | bytes 1769480 | tf_op jit(solution)/shard_map/ppermute | solution.py:229
  22.5 88.1 %copy-start.6 = (s32[32]{0:T(128)S(1)}, s32[32]{0:T(128)}, u32[]{:S(2)}) copy-start(s32[32]{0:T(128)} %param.17) | copy-start | bytes 388
  22.6 88.1 %copy-start.7 = (s32[32]{0:T(128)S(1)}, s32[32]{0:T(128)}, u32[]{:S(2)}) copy-start(s32[32]{0:T(128)} %param.18) | copy-start | bytes 388
  22.6 90.2 %copy-start = (bf16[2,6,256,128]{3,2,1,0:T(8,128)(2,1)S(1)}, bf16[2,6,256,128]{3,2,1,0:T(8,128)(2,1)}, u32[]{:S(2)}) copy-start(bf16[2,6,256,128]{3,2,1,0:T(8,128)(2,1)} %get-tuple-element.65.refs_0_) | copy-start | bytes 2359300
  22.6 19.1 %collective-permute-start.1 = (bf16[2,6,256,128]{3,2,1,0:T(8,128)(2,1)}, bf16[2,6,256,128]{3,2,1,0:T(8,128)(2,1)S(1)}, u32[]{:S(2)}, u32[]{:S(2)}) collective-permute-start(bf16[2,6,256,128]{3,2,1,0:T(8,128)(2,1)} %get-tuple-element.59), channel_id=1, source_target_pairs={{0,2},{1,3},{2,4},{3,5},{4,6},{5,7},{6,0},{7,1},{8,10},{9,11},{10,... | collective-permute-start | bytes 2359304 | tf_op jit(solution)/shard_map/ppermute | solution.py:229
  22.9 22.9 %collective-permute-start.3 = (bf16[2,6,256,128]{3,2,1,0:T(8,128)(2,1)}, bf16[2,6,256,128]{3,2,1,0:T(8,128)(2,1)S(1)}, u32[]{:S(2)}, u32[]{:S(2)}) collective-permute-start(bf16[2,6,256,128]{3,2,1,0:T(8,128)(2,1)} %get-tuple-element.61), channel_id=1, source_target_pairs={{0,4},{1,5},{2,6},{3,7},{4,0},{5,1},{6,2},{7,3},{8,12},{9,13},{10,... | collective-permute-start | bytes 2359304 | tf_op jit(solution)/shard_map/ppermute | solution.py:229
  25.6 41.2 %collective-permute-start.5 = (bf16[2,6,256,128]{3,2,1,0:T(8,128)(2,1)}, bf16[2,6,256,128]{3,2,1,0:T(8,128)(2,1)S(1)}, u32[]{:S(2)}, u32[]{:S(2)}) collective-permute-start(bf16[2,6,256,128]{3,2,1,0:T(8,128)(2,1)} %get-tuple-element.63), channel_id=1, source_target_pairs={{0,6},{1,7},{2,0},{3,1},{4,2},{5,3},{6,4},{7,5},{8,14},{9,15},{10,... | collective-permute-start | bytes 2359304 | tf_op jit(solution)/shard_map/ppermute | solution.py:229
  27.1 39.8 %collective-permute-start = (bf16[2,6,256,128]{3,2,1,0:T(8,128)(2,1)}, bf16[2,6,256,128]{3,2,1,0:T(8,128)(2,1)}, u32[]{:S(2)}, u32[]{:S(2)}) collective-permute-start(bf16[2,6,256,128]{3,2,1,0:T(8,128)(2,1)} %get-tuple-element.58), channel_id=1, source_target_pairs={{0,1},{1,0},{2,3},{3,2},{4,5},{5,4},{6,7},{7,6},{8,9},{9,8},{10,11... | collective-permute-start | bytes 2359304 | tf_op jit(solution)/shard_map/ppermute | solution.py:229
  28.3 48.8 %collective-permute-start.2 = (bf16[2,6,256,128]{3,2,1,0:T(8,128)(2,1)}, bf16[2,6,256,128]{3,2,1,0:T(8,128)(2,1)}, u32[]{:S(2)}, u32[]{:S(2)}) collective-permute-start(bf16[2,6,256,128]{3,2,1,0:T(8,128)(2,1)} %get-tuple-element.60), channel_id=1, source_target_pairs={{0,3},{1,2},{2,5},{3,4},{4,7},{5,6},{6,1},{7,0},{8,11},{9,10},{10,... | collective-permute-start | bytes 2359304 | tf_op jit(solution)/shard_map/ppermute | solution.py:229
  41.7 37.5 %collective-permute-start.4 = (bf16[2,6,256,128]{3,2,1,0:T(8,128)(2,1)}, bf16[2,6,256,128]{3,2,1,0:T(8,128)(2,1)}, u32[]{:S(2)}, u32[]{:S(2)}) collective-permute-start(bf16[2,6,256,128]{3,2,1,0:T(8,128)(2,1)} %get-tuple-element.62), channel_id=1, source_target_pairs={{0,5},{1,4},{2,7},{3,6},{4,1},{5,0},{6,3},{7,2},{8,13},{9,12},{10,... | collective-permute-start | bytes 2359304 | tf_op jit(solution)/shard_map/ppermute | solution.py:229
  45.9 48.9 %collective-permute-start.6 = (bf16[2,6,256,128]{3,2,1,0:T(8,128)(2,1)}, bf16[2,6,256,128]{3,2,1,0:T(8,128)(2,1)}, u32[]{:S(2)}, u32[]{:S(2)}) collective-permute-start(bf16[2,6,256,128]{3,2,1,0:T(8,128)(2,1)} %get-tuple-element.64), channel_id=1, source_target_pairs={{0,7},{1,6},{2,1},{3,0},{4,3},{5,2},{6,5},{7,4},{8,15},{9,14},{10,... | collective-permute-start | bytes 2359304 | tf_op jit(solution)/shard_map/ppermute | solution.py:229
  94.8 6.8 %collective-permute-start.7 = (bf16[1,6,256,128]{3,2,1,0:T(8,128)(2,1)}, bf16[1,6,256,128]{3,2,1,0:T(8,128)(2,1)S(1)}, u32[]{:S(2)}, u32[]{:S(2)}) collective-permute-start(bf16[1,6,256,128]{3,2,1,0:T(8,128)(2,1)} %get-tuple-element.74), channel_id=1, source_target_pairs={{0,1},{1,0},{2,3},{3,2},{4,5},{5,4},{6,7},{7,6},{8,9},{9,8},{10,11... | collective-permute-start | bytes 1179656 | tf_op jit(solution)/shard_map/ppermute | solution.py:229
  95.3 11.1 %collective-permute-start.8 = (bf16[1,6,256,128]{3,2,1,0:T(8,128)(2,1)}, bf16[1,6,256,128]{3,2,1,0:T(8,128)(2,1)S(1)}, u32[]{:S(2)}, u32[]{:S(2)}) collective-permute-start(bf16[1,6,256,128]{3,2,1,0:T(8,128)(2,1)} %get-tuple-element.75), channel_id=1, source_target_pairs={{0,2},{1,3},{2,4},{3,5},{4,6},{5,7},{6,0},{7,1},{8,10},{9,11},{10,... | collective-permute-start | bytes 1179656 | tf_op jit(solution)/shard_map/ppermute | solution.py:229
  95.3 32.9 %collective-permute-start.9 = (bf16[1,6,256,128]{3,2,1,0:T(8,128)(2,1)}, bf16[1,6,256,128]{3,2,1,0:T(8,128)(2,1)}, u32[]{:S(2)}, u32[]{:S(2)}) collective-permute-start(bf16[1,6,256,128]{3,2,1,0:T(8,128)(2,1)} %get-tuple-element.76), channel_id=1, source_target_pairs={{0,3},{1,2},{2,5},{3,4},{4,7},{5,6},{6,1},{7,0},{8,11},{9,10},{10,... | collective-permute-start | bytes 1179656 | tf_op jit(solution)/shard_map/ppermute | solution.py:229
  98.5 29.7 %collective-permute-start.10 = (bf16[1,6,256,128]{3,2,1,0:T(8,128)(2,1)}, bf16[1,6,256,128]{3,2,1,0:T(8,128)(2,1)}, u32[]{:S(2)}, u32[]{:S(2)}) collective-permute-start(bf16[1,6,256,128]{3,2,1,0:T(8,128)(2,1)} %get-tuple-element.77), channel_id=1, source_target_pairs={{0,4},{1,5},{2,6},{3,7},{4,0},{5,1},{6,2},{7,3},{8,12},{9,13},{10,... | collective-permute-start | bytes 1179656 | tf_op jit(solution)/shard_map/ppermute | solution.py:229
  98.7 29.5 %collective-permute-start.11 = (bf16[1,6,256,128]{3,2,1,0:T(8,128)(2,1)}, bf16[1,6,256,128]{3,2,1,0:T(8,128)(2,1)}, u32[]{:S(2)}, u32[]{:S(2)}) collective-permute-start(bf16[1,6,256,128]{3,2,1,0:T(8,128)(2,1)} %get-tuple-element.78), channel_id=1, source_target_pairs={{0,5},{1,4},{2,7},{3,6},{4,1},{5,0},{6,3},{7,2},{8,13},{9,12},{10,... | collective-permute-start | bytes 1179656 | tf_op jit(solution)/shard_map/ppermute | solution.py:229
  101.6 26.6 %collective-permute-start.12 = (bf16[1,6,256,128]{3,2,1,0:T(8,128)(2,1)}, bf16[1,6,256,128]{3,2,1,0:T(8,128)(2,1)}, u32[]{:S(2)}, u32[]{:S(2)}) collective-permute-start(bf16[1,6,256,128]{3,2,1,0:T(8,128)(2,1)} %get-tuple-element.79), channel_id=1, source_target_pairs={{0,6},{1,7},{2,0},{3,1},{4,2},{5,3},{6,4},{7,5},{8,14},{9,15},{10,... | collective-permute-start | bytes 1179656 | tf_op jit(solution)/shard_map/ppermute | solution.py:229
  107.1 29.7 %collective-permute-start.13 = (bf16[1,6,256,128]{3,2,1,0:T(8,128)(2,1)}, bf16[1,6,256,128]{3,2,1,0:T(8,128)(2,1)}, u32[]{:S(2)}, u32[]{:S(2)}) collective-permute-start(bf16[1,6,256,128]{3,2,1,0:T(8,128)(2,1)} %get-tuple-element.80), channel_id=1, source_target_pairs={{0,7},{1,6},{2,1},{3,0},{4,3},{5,2},{6,5},{7,4},{8,15},{9,14},{10,... | collective-permute-start | bytes 1179656 | tf_op jit(solution)/shard_map/ppermute | solution.py:229
  136.8 28.9 %all-to-all-start = ((bf16[8,2,2,256,128]{4,3,2,1,0:T(8,128)(2,1)}), bf16[8,2,2,256,128]{4,3,2,1,0:T(8,128)(2,1)S(1)}, u32[]{:S(2)}, u32[]{:S(2)}) async-start(bf16[8,2,2,256,128]{4,3,2,1,0:T(8,128)(2,1)} %attend.2), calls=%async_computation | async-start | bytes 4194304 | tf_op jit(solution)/shard_map/all_to_all | solution.py:246
  165.7 20.2 %all-to-all-start.1 = ((bf16[8,1,2,256,128]{4,3,2,1,0:T(8,128)(2,1)}), bf16[8,1,2,256,128]{4,3,2,1,0:T(8,128)(2,1)}, u32[]{:S(2)}, u32[]{:S(2)}) async-start(bf16[8,1,2,256,128]{4,3,2,1,0:T(8,128)(2,1)} %attend.3), calls=%async_computation.1 | async-start | bytes 2097152 | tf_op jit(solution)/shard_map/all_to_all | solution.py:246
  (6 other events, 124.2 us)
Sparse Core Ops, SparseCore 0:
  22.7 124.2 all-gather.1

commit v5 on v4

--- a/solution.py
+++ b/solution.py
@@ -78,8 +78,12 @@
     return lax.dot_general(a, b, (((1,), (1,)), ((), ())), preferred_element_type=jnp.float32)
 
 
-def attend_kernel(members, info, *refs):
-    moved, (out, qq, kk, vv, sems) = refs[:members], refs[members:]
+def attend_kernel(members, apart, info, *refs):
+    moved, outs, (qq, kk, vv, sems) = refs[:members], refs[members:-4], refs[-4:]
+    if apart:
+        *outs, out = outs
+    else:
+        (out,) = outs
     size, _, rows, _ = moved[0].shape
     per = rows // FRAME
     first_count, second_count = info[0], info[1]
@@ -147,76 +151,70 @@
         return carry
 
     lax.fori_loop(0, size, one_head, 0)
-
-
-def attend(info, moved):
+    if apart:
+        for b in range(members):
+            outs[b][...] = out[member(b, members)]
+
+
+def attend(info, moved, apart=False):
     members = len(moved)
     size, _, rows, _ = moved[0].shape
+    whole = (members, size, 2, rows, HEAD_DIM)
+    block = jax.ShapeDtypeStruct(whole[1:], BF16)
     return pl.pallas_call(
-        functools.partial(attend_kernel, members),
+        functools.partial(attend_kernel, members, apart),
         in_specs=[SMEM] + [ANY] * members,
-        out_specs=VMEM,
-        out_shape=jax.ShapeDtypeStruct((members, size, 2, rows, HEAD_DIM), BF16),
-        scratch_shapes=[pltpu.VMEM((members * rows, 2 * HEAD_DIM), BF16)] * 3
+        out_specs=[VMEM] * members if apart else VMEM,
+        out_shape=[block] * members if apart else jax.ShapeDtypeStruct(whole, BF16),
+        scratch_shapes=[pltpu.VMEM(whole, BF16)] * apart
+        + [pltpu.VMEM((members * rows, 2 * HEAD_DIM), BF16)] * 3
         + [pltpu.SemaphoreType.DMA((6 * members,))],
         compiler_params=pltpu.CompilerParams(vmem_limit_bytes=40 * 2**20),
         name="attend",
     )(info, *moved)
 
 
-def project_kernel(moved, w, *refs):
-    if len(refs) == 5:
-        total, out, tangent, held, sems = refs
-    else:
-        out, held, sems = refs
-        total = None
-    members, size, _, rows, _ = moved.shape
+def project_kernel(members, moved, *refs):
+    last, (w, out, tangent, held, sems) = refs[:members], refs[members:]
+    _, size, _, rows, _ = moved.shape
+    rounds = size + last[0].shape[0]
 
     @pl.when(pl.program_id(0) == 0)
     def _():
         pairs = []
-        for u in range(members):
-            for i in range(size):
-                at = slice((u * size + i) * HEAD_DIM, (u * size + i + 1) * HEAD_DIM)
+        for b in range(members):
+            u = member(b, members, True)
+            for r in range(rounds):
                 for which in range(2):
-                    down = slice(which * rows, (which + 1) * rows)
-                    pairs.append((moved.at[u, i, which], held.at[down, at]))
+                    source = moved.at[b, r, which] if r < size else last[b].at[r - size, which]
+                    head = (b if r < size else u) * rounds + r
+                    at = pl.ds(pl.multiple_of(head * HEAD_DIM, HEAD_DIM), HEAD_DIM)
+                    pairs.append((source, held.at[which * rows : (which + 1) * rows, at]))
         run_copies(pairs, sems)
 
-    depth = held.shape[1]
-    product = jnp.dot(held[...], w[...].reshape(depth, -1), preferred_element_type=jnp.float32)
-    if total is None:
-        out[...] = product
-    else:
-        out[...] = (total[:rows] + product[:rows]).astype(BF16)
-        tangent[...] = (total[rows:] + product[rows:]).astype(BF16)
-
-
-def project(moved, weight, rounds, first, total=None):
+    product = jnp.dot(held[...], w[...], preferred_element_type=jnp.float32)
+    out[...] = product[:rows].astype(BF16)
+    tangent[...] = product[rows:].astype(BF16)
+
+
+def project(moved, last, weight):
     members, size, _, rows, _ = moved.shape
-    width = weight.shape[1]
-    tile = 512
-    by_round = weight.reshape(members, rounds, HEAD_DIM, width)
-    sum_spec = pl.BlockSpec((2 * rows, tile), lambda step: (0, step))
-    half_spec = pl.BlockSpec((rows, tile), lambda step: (0, step))
-    last = total is not None
+    depth, width = weight.shape
+    tile = 768
+    given = pl.BlockSpec((rows, tile), lambda step: (0, step))
     return pl.pallas_call(
-        project_kernel,
+        functools.partial(project_kernel, members),
         grid=(width // tile,),
-        in_specs=[ANY]
-        + [pl.BlockSpec((members, size, HEAD_DIM, tile), lambda step: (0, first // size, 0, step))]
-        + [sum_spec] * last,
-        out_specs=[half_spec, half_spec] if last else sum_spec,
+        in_specs=[ANY] * (1 + members) + [pl.BlockSpec((depth, tile), lambda step: (0, step))],
+        out_specs=[given, given],
+        out_shape=[jax.ShapeDtypeStruct((rows, width), BF16)] * 2,
         scratch_shapes=[
-            pltpu.VMEM((2 * rows, members * size * HEAD_DIM), BF16),
-            pltpu.SemaphoreType.DMA((2 * members * size,)),
+            pltpu.VMEM((2 * rows, depth), BF16),
+            pltpu.SemaphoreType.DMA((2 * depth // HEAD_DIM,)),
         ],
-        out_shape=[jax.ShapeDtypeStruct((rows, width), BF16)] * 2
-        if last
-        else jax.ShapeDtypeStruct((2 * rows, width), jnp.float32),
-        compiler_params=pltpu.CompilerParams(vmem_limit_bytes=56 * 2**20),
+        compiler_params=pltpu.CompilerParams(vmem_limit_bytes=40 * 2**20),
         name="project",
-    )(moved, by_round, *([total] if last else []))
+    )(moved, *last, weight)
 
 
 def after(value, *done):
@@ -275,13 +273,14 @@
         ]
     ).astype(jnp.int32)
     late = packed(rounds - 1, 1, same + other)
-    late, arrived = lax.optimization_barrier((late, arrived))
+    ready = [arrived[b] for b in same]
+    late, ready = lax.optimization_barrier((late, ready))
+    arrived = [ready[same.index(b)] if b in same else arrived[b] for b in range(members)]
     late, result = in_order(send(late)), attend(info, arrived)
     result, late = lax.optimization_barrier((result, late))
-    moved, result = exchange(result), attend(info, late)
-    result, moved, weight = lax.optimization_barrier((result, moved, weight))
-    last, total = exchange(result), project(moved, weight, rounds, 0)
-    return tuple(project(last, weight, rounds, rounds - 1, total))
+    moved = exchange(result)
+    last = send(dict(enumerate(attend(info, late, True))))
+    return tuple(project(moved, in_order(last), weight))
 
 
 def solution(mesh):

time: 206 us -> 196 us (0.951)
  Pallas kernels: 58.9 us -> 39.7 us
  starting transfers between devices: 52.6 us -> 58.6 us
  waiting for transfers between devices: 73.1 us -> 76.3 us
    ppermute x18 -> x25, waiting for transfers between devices: 56.4 us -> 76.2 us  [hop(): return lax.ppermute(value, 'ulysses', pairs)]
    pallas_call x4 -> x3, Pallas kernels: 48.3 us -> 29 us  [the longest x1 15.1 us: project(): pl.pallas_call(functools.partial(project_kernel, members), grid=(width //...]
    all_to_all x2 -> x1, waiting for transfers between devices: 16.7 us -> 0.01 us  [exchange(): return lax.all_to_all(x, 'ulysses', split_axis=0, concat_axis=0, tiled=True)]
    ppermute x18 -> x25, starting transfers between devices: 42.6 us -> 52.6 us  [hop(): return lax.ppermute(value, 'ulysses', pairs)]
    all_to_all x2 -> x1, starting transfers between devices: 9.89 us -> 6 us  [exchange(): return lax.all_to_all(x, 'ulysses', split_axis=0, concat_axis=0, tiled=True)]
  transfers between devices with their start and end apart: 21 -> 27, of which waited for: 10 -> 13; matrix products, arithmetic and copies ran while one was open for 1% -> 1% of each run, Pallas kernels for 24% -> 13%
where the time goes in v5:
time: 196 us; the launch traced here: 193 us
  waiting for transfers between devices  76.3 us (39%)
  starting transfers between devices  58.6 us (30%)
  Pallas kernels  39.7 us (20%)
  between operations  14.3 us (7%)
  other arithmetic  2.16 us (1%)
  local copies, waits for them, and re-layouts  2.03 us (1%)
    ppermute x25, waiting for transfers between devices, hop(): return lax.ppermute(value, 'ulysses', pairs)  76.2 us
    ppermute x25, starting transfers between devices, hop(): return lax.ppermute(value, 'ulysses', pairs)  52.6 us
    pallas_call x1, Pallas kernels, project(): pl.pallas_call(functools.partial(project_kernel, members), grid=(width //...  15.1 us
    pallas_call x2, Pallas kernels, attend(): pl.pallas_call(functools.partial(attend_kernel, members, apart), in_specs...  13.9 us
    pallas_call x3, Pallas kernels, pack(): pl.pallas_call(functools.partial(pack_kernel, first, rounds, members, blo...  10.7 us
    all_to_all x1, starting transfers between devices, exchange(): return lax.all_to_all(x, 'ulysses', split_axis=0, concat_axis=0, tiled=True)  6 us
  transfers between devices with their start and end apart: 27, of which 13 were waited for; matrix products, arithmetic and copies ran while one was open for 1% of the time, Pallas kernels for 13%

profile of v5, /device:TPU:19, one launch (start us, length us, event | category | flops | bytes accessed | tf_op | source)
XLA Modules:
  0.0 193.1 jit_solution(15513582496540368206)
XLA Ops:
  7.2 1.9 collective-permute-start.22
  10.6 2.9 %pack.5 = (bf16[2,6,256,128]{3,2,1,0:T(8,128)(2,1)}, bf16[2,6,256,128]{3,2,1,0:T(8,128)(2,1)}, bf16[2,6,256,128]{3,2,1,0:T(8,128)(2,1)}) custom-call(bf16[256,3072]{1,0:T(8,128)(2,1)} %refs_0_.5, bf16[256,3072]{1,0:T(8,128)(2,1)} %refs_1_.5, bf16[256,3072]{1,0:T(8,128)(2,1)} %refs_2_.5, bf16[256,3072]{1,0:T(8,128)(2,1)} %refs_3_.5, ...), custom_call_target="tpu_custom_call" | custom-call | tf_op jit(solution)/shard_map/pack/pallas_call | solution.py:63
  13.5 4.2 %pack.3 = (bf16[2,6,256,128]{3,2,1,0:T(8,128)(2,1)}, bf16[2,6,256,128]{3,2,1,0:T(8,128)(2,1)}, bf16[2,6,256,128]{3,2,1,0:T(8,128)(2,1)}, bf16[2,6,256,128]{3,2,1,0:T(8,128)(2,1)}, bf16[2,6,256,128]{3,2,1,0:T(8,128)(2,1)}) custom-call(bf16[256,3072]{1,0:T(8,128)(2,1)} %refs_0_.5, bf16[256,3072]{1,0:T(8,128)(2,1)} %refs_1_.5, bf16[256,3072]{1,0:T(8,128)(2,1)} %refs_2_.5, ...), custom_call_target="tpu_custom_call" | custom-call | tf_op jit(solution)/shard_map/pack/pallas_call | solution.py:63
  23.0 2.7 %collective-permute-start.2 = (bf16[2,6,256,128]{3,2,1,0:T(8,128)(2,1)}, bf16[2,6,256,128]{3,2,1,0:T(8,128)(2,1)S(1)}, u32[]{:S(2)}, u32[]{:S(2)}) collective-permute-start(bf16[2,6,256,128]{3,2,1,0:T(8,128)(2,1)} %get-tuple-element.60), channel_id=1, source_target_pairs={{0,4},{1,5},{2,6},{3,7},{4,0},{5,1},{6,2},{7,3},{8,12},{9,13},{10,... | collective-permute-start | bytes 2359304 | tf_op jit(solution)/shard_map/ppermute | solution.py:227
  28.4 13.4 %collective-permute-done.1.refs_2_ = bf16[2,6,256,128]{3,2,1,0:T(8,128)(2,1)S(1)} collective-permute-done((bf16[2,6,256,128]{3,2,1,0:T(8,128)(2,1)}, bf16[2,6,256,128]{3,2,1,0:T(8,128)(2,1)S(1)}, u32[]{:S(2)}, u32[]{:S(2)}) %collective-permute-start.1) | collective-permute-done | bytes 786464 | tf_op jit(solution)/shard_map/ppermute | solution.py:227
  41.8 4.1 %collective-permute-start.5 = (bf16[2,6,256,128]{3,2,1,0:T(8,128)(2,1)}, bf16[2,6,256,128]{3,2,1,0:T(8,128)(2,1)}, u32[]{:S(2)}, u32[]{:S(2)}) collective-permute-start(bf16[2,6,256,128]{3,2,1,0:T(8,128)(2,1)} %get-tuple-element.65), channel_id=1, source_target_pairs={{0,5},{1,4},{2,7},{3,6},{4,1},{5,0},{6,3},{7,2},{8,13},{9,12},{10,... | collective-permute-start | bytes 2359304 | tf_op jit(solution)/shard_map/ppermute | solution.py:227
  45.9 17.5 %collective-permute-start.6 = (bf16[2,6,256,128]{3,2,1,0:T(8,128)(2,1)}, bf16[2,6,256,128]{3,2,1,0:T(8,128)(2,1)}, u32[]{:S(2)}, u32[]{:S(2)}) collective-permute-start(bf16[2,6,256,128]{3,2,1,0:T(8,128)(2,1)} %get-tuple-element.67), channel_id=1, source_target_pairs={{0,7},{1,6},{2,1},{3,0},{4,3},{5,2},{6,5},{7,4},{8,15},{9,14},{10,... | collective-permute-start | bytes 2359304 | tf_op jit(solution)/shard_map/ppermute | solution.py:227
  63.4 3.5 %pack.4 = (bf16[1,6,256,128]{3,2,1,0:T(8,128)(2,1)}, bf16[1,6,256,128]{3,2,1,0:T(8,128)(2,1)}, bf16[1,6,256,128]{3,2,1,0:T(8,128)(2,1)}, bf16[1,6,256,128]{3,2,1...) custom-call(bf16[256,3072]{1,0:T(8,128)(2,1)} %refs_0_.5, ...), custom_call_target="tpu_custom_call" | custom-call | tf_op jit(solution)/shard_map/pack/pallas_call | solution.py:63
  67.1 10.0 %collective-permute-done.4.refs_3_ = bf16[2,6,256,128]{3,2,1,0:T(8,128)(2,1)} collective-permute-done((bf16[2,6,256,128]{3,2,1,0:T(8,128)(2,1)}, bf16[2,6,256,128]{3,2,1,0:T(8,128)(2,1)}, u32[]{:S(2)}, u32[]{:S(2)}) %collective-permute-start.4) | collective-permute-done | bytes 786464 | tf_op jit(solution)/shard_map/ppermute | solution.py:227
  79.3 2.4 %collective-permute-start.10 = (bf16[1,6,256,128]{3,2,1,0:T(8,128)(2,1)}, bf16[1,6,256,128]{3,2,1,0:T(8,128)(2,1)}, u32[]{:S(2)}, u32[]{:S(2)}) collective-permute-start(bf16[1,6,256,128]{3,2,1,0:T(8,128)(2,1)} %get-tuple-element.72), channel_id=1, source_target_pairs={{0,4},{1,5},{2,6},{3,7},{4,0},{5,1},{6,2},{7,3},{8,12},{9,13},{10,... | collective-permute-start | bytes 1179656 | tf_op jit(solution)/shard_map/ppermute | solution.py:227
  81.7 14.2 %collective-permute-done.6.refs_7_ = bf16[2,6,256,128]{3,2,1,0:T(8,128)(2,1)} collective-permute-done((bf16[2,6,256,128]{3,2,1,0:T(8,128)(2,1)}, bf16[2,6,256,128]{3,2,1,0:T(8,128)(2,1)}, u32[]{:S(2)}, u32[]{:S(2)}) %collective-permute-start.6) | collective-permute-done | bytes 786464 | tf_op jit(solution)/shard_map/ppermute | solution.py:227
  95.9 2.8 %collective-permute-start.11 = (bf16[1,6,256,128]{3,2,1,0:T(8,128)(2,1)}, bf16[1,6,256,128]{3,2,1,0:T(8,128)(2,1)}, u32[]{:S(2)}, u32[]{:S(2)}) collective-permute-start(bf16[1,6,256,128]{3,2,1,0:T(8,128)(2,1)} %get-tuple-element.73), channel_id=1, source_target_pairs={{0,5},{1,4},{2,7},{3,6},{4,1},{5,0},{6,3},{7,2},{8,13},{9,12},{10,... | collective-permute-start | bytes 1179656 | tf_op jit(solution)/shard_map/ppermute | solution.py:227
  99.0 1.9 collective-permute-done.8.refs_2_
  101.6 4.1 %collective-permute-start.13 = (bf16[1,6,256,128]{3,2,1,0:T(8,128)(2,1)}, bf16[1,6,256,128]{3,2,1,0:T(8,128)(2,1)}, u32[]{:S(2)}, u32[]{:S(2)}) collective-permute-start(bf16[1,6,256,128]{3,2,1,0:T(8,128)(2,1)} %get-tuple-element.75), channel_id=1, source_target_pairs={{0,7},{1,6},{2,1},{3,0},{4,3},{5,2},{6,5},{7,4},{8,15},{9,14},{10,... | collective-permute-start | bytes 1179656 | tf_op jit(solution)/shard_map/ppermute | solution.py:227
  107.7 9.2 %attend.2 = bf16[8,2,2,256,128]{4,3,2,1,0:T(8,128)(2,1)} custom-call(s32[2]{0:T(128)S(1)} %pad_add_fusion.info, bf16[2,6,256,128]{3,2,1,0:T(8,128)(2,1)S(1)} %copy-done, bf16[2,6,256,128]{3,2,1,0:T(8,128)(2,1)} %collective-permute-done.refs_1_, bf16[2,6,256,128]{3,2,1,0:T(8,128)(2,1)S(1)} %collective-permute-done.1.refs_2_, ...), custom_call_target="tpu_custom_call" | custom-call | tf_op jit(solution)/shard_map/attend/pallas_call | solution.py:164
  117.0 3.6 %collective-permute-done.12.refs_6_ = bf16[1,6,256,128]{3,2,1,0:T(8,128)(2,1)} collective-permute-done((bf16[1,6,256,128]{3,2,1,0:T(8,128)(2,1)}, bf16[1,6,256,128]{3,2,1,0:T(8,128)(2,1)}, u32[]{:S(2)}, u32[]{:S(2)}) %collective-permute-start.12) | collective-permute-done | bytes 393248 | tf_op jit(solution)/shard_map/ppermute | solution.py:227
  120.6 8.5 %collective-permute-done.13.refs_7_ = bf16[1,6,256,128]{3,2,1,0:T(8,128)(2,1)} collective-permute-done((bf16[1,6,256,128]{3,2,1,0:T(8,128)(2,1)}, bf16[1,6,256,128]{3,2,1,0:T(8,128)(2,1)}, u32[]{:S(2)}, u32[]{:S(2)}) %collective-permute-start.13) | collective-permute-done | bytes 393248 | tf_op jit(solution)/shard_map/ppermute | solution.py:227
  129.1 6.0 %all-to-all-start = ((bf16[8,2,2,256,128]{4,3,2,1,0:T(8,128)(2,1)}), bf16[8,2,2,256,128]{4,3,2,1,0:T(8,128)(2,1)S(1)}, u32[]{:S(2)}, u32[]{:S(2)}) async-start(bf16[8,2,2,256,128]{4,3,2,1,0:T(8,128)(2,1)} %attend.2), calls=%async_computation | async-start | bytes 4194304 | tf_op jit(solution)/shard_map/all_to_all | solution.py:244
  135.1 4.7 %attend.3 = (bf16[1,2,256,128]{3,2,1,0:T(8,128)(2,1)S(1)}, bf16[1,2,256,128]{3,2,1,0:T(8,128)(2,1)S(1)}, bf16[1,2,256,128]{3,2,1,0:T(8,128)(2,1)S(1)}, bf16[1,2,...) custom-call(s32[2]{0:T(128)S(1)} %pad_add_fusion.info, ...), custom_call_target="tpu_custom_call" | custom-call | tf_op jit(solution)/shard_map/attend/pallas_call | solution.py:164
  143.8 2.0 %collective-permute-start.18 = (bf16[1,2,256,128]{3,2,1,0:T(8,128)(2,1)S(1)}, bf16[1,2,256,128]{3,2,1,0:T(8,128)(2,1)S(1)}, u32[]{:S(2)}, u32[]{:S(2)}) collective-permute-start(bf16[1,2,256,128]{3,2,1,0:T(8,128)(2,1)S(1)} %get-tuple-element.90), channel_id=1, source_target_pairs={{0,5},{1,4},{2,7},{3,6},{4,1},{5,0},{6,3},{7,2},{8,13},{9,12},{10,... | collective-permute-start | bytes 393224 | tf_op jit(solution)/shard_map/ppermute | solution.py:227
  146.4 15.3 %collective-permute-done.15.refs_2_ = bf16[1,2,256,128]{3,2,1,0:T(8,128)(2,1)S(1)} collective-permute-done((bf16[1,2,256,128]{3,2,1,0:T(8,128)(2,1)S(1)}, bf16[1,2,256,128]{3,2,1,0:T(8,128)(2,1)S(1)}, u32[]{:S(2)}, u32[]{:S(2)}) %collective-permute-start.15) | collective-permute-done | bytes 131104 | tf_op jit(solution)/shard_map/ppermute | solution.py:227
  161.8 3.3 %collective-permute-start.20 = (bf16[1,2,256,128]{3,2,1,0:T(8,128)(2,1)S(1)}, bf16[1,2,256,128]{3,2,1,0:T(8,128)(2,1)S(1)}, u32[]{:S(2)}, u32[]{:S(2)}) collective-permute-start(bf16[1,2,256,128]{3,2,1,0:T(8,128)(2,1)S(1)} %get-tuple-element.92), channel_id=1, source_target_pairs={{0,7},{1,6},{2,1},{3,0},{4,3},{5,2},{6,5},{7,4},{8,15},{9,14},{10,... | collective-permute-start | bytes 393224 | tf_op jit(solution)/shard_map/ppermute | solution.py:227
  168.2 3.0 %collective-permute-done.20.refs_7_ = bf16[1,2,256,128]{3,2,1,0:T(8,128)(2,1)S(1)} collective-permute-done((bf16[1,2,256,128]{3,2,1,0:T(8,128)(2,1)S(1)}, bf16[1,2,256,128]{3,2,1,0:T(8,128)(2,1)S(1)}, u32[]{:S(2)}, u32[]{:S(2)}) %collective-permute-start.20) | collective-permute-done | bytes 131104 | tf_op jit(solution)/shard_map/ppermute | solution.py:227
  171.2 15.1 %project.1 = (bf16[256,3072]{1,0:T(8,128)(2,1)}, bf16[256,3072]{1,0:T(8,128)(2,1)}) custom-call(bf16[8,2,2,256,128]{4,3,2,1,0:T(8,128)(2,1)S(1)} %all-to-all-done.moved, bf16[1,2,256,128]{3,2,1,0:T(8,128)(2,1)S(1)} %get-tuple-element.85.refs_0_, bf16[1,2,256,128]{3,2,1,0:T(8,128)(2,1)S(1)} %collective-permute-done.14.refs_1_, ...), custom_call_target="tpu_custom_call" | custom-call | tf_op jit(solution)/shard_map/project/pallas_call | solution.py:205
  (67 shorter events, 22.2 us)
Async XLA Ops:
  7.2 164.0 %all-gather.2.cloned.1.call-start = ((), (), s32[]{:S(2)}) async-start(), calls=%async_computation.1 | async-start | bytes 20054016 | tf_op jit(solution)/shard_map/all_gather | solution.py:266
  7.2 10.6 %collective-permute-start.22 = (bf16[24,3072]{1,0:T(8,128)(2,1)}, bf16[24,3072]{1,0:T(8,128)(2,1)S(1)}, u32[]{:S(2)}, u32[]{:S(2)}) collective-permute-start(bf16[24,3072]{1,0:T(8,128)(2,1)} %param.16), channel_id=1, source_target_pairs={{0,4},{1,5},{2,6},{3,7},{4,0},{5,1},{6,2},{7,3},{8,12},{9,13},{10,... | collective-permute-start | bytes 442376 | tf_op jit(solution)/shard_map/ppermute | solution.py:227
  9.1 8.8 %collective-permute-start.21 = (bf16[24,3072]{1,0:T(8,128)(2,1)}, bf16[24,3072]{1,0:T(8,128)(2,1)S(1)}, u32[]{:S(2)}, u32[]{:S(2)}) collective-permute-start(bf16[24,3072]{1,0:T(8,128)(2,1)} %param.16), channel_id=1, source_target_pairs={{0,6},{1,7},{2,0},{3,1},{4,2},{5,3},{6,4},{7,5},{8,14},{9,15},{10,... | collective-permute-start | bytes 442376 | tf_op jit(solution)/shard_map/ppermute | solution.py:227
  22.7 19.1 %collective-permute-start.1 = (bf16[2,6,256,128]{3,2,1,0:T(8,128)(2,1)}, bf16[2,6,256,128]{3,2,1,0:T(8,128)(2,1)S(1)}, u32[]{:S(2)}, u32[]{:S(2)}) collective-permute-start(bf16[2,6,256,128]{3,2,1,0:T(8,128)(2,1)} %get-tuple-element.59), channel_id=1, source_target_pairs={{0,2},{1,3},{2,4},{3,5},{4,6},{5,7},{6,0},{7,1},{8,10},{9,11},{10,... | collective-permute-start | bytes 2359304 | tf_op jit(solution)/shard_map/ppermute | solution.py:227
  23.0 22.9 %collective-permute-start.2 = (bf16[2,6,256,128]{3,2,1,0:T(8,128)(2,1)}, bf16[2,6,256,128]{3,2,1,0:T(8,128)(2,1)S(1)}, u32[]{:S(2)}, u32[]{:S(2)}) collective-permute-start(bf16[2,6,256,128]{3,2,1,0:T(8,128)(2,1)} %get-tuple-element.60), channel_id=1, source_target_pairs={{0,4},{1,5},{2,6},{3,7},{4,0},{5,1},{6,2},{7,3},{8,12},{9,13},{10,... | collective-permute-start | bytes 2359304 | tf_op jit(solution)/shard_map/ppermute | solution.py:227
  25.7 41.3 %collective-permute-start.3 = (bf16[2,6,256,128]{3,2,1,0:T(8,128)(2,1)}, bf16[2,6,256,128]{3,2,1,0:T(8,128)(2,1)S(1)}, u32[]{:S(2)}, u32[]{:S(2)}) collective-permute-start(bf16[2,6,256,128]{3,2,1,0:T(8,128)(2,1)} %get-tuple-element.61), channel_id=1, source_target_pairs={{0,6},{1,7},{2,0},{3,1},{4,2},{5,3},{6,4},{7,5},{8,14},{9,15},{10,... | collective-permute-start | bytes 2359304 | tf_op jit(solution)/shard_map/ppermute | solution.py:227
  27.2 39.9 %collective-permute-start = (bf16[2,6,256,128]{3,2,1,0:T(8,128)(2,1)}, bf16[2,6,256,128]{3,2,1,0:T(8,128)(2,1)}, u32[]{:S(2)}, u32[]{:S(2)}) collective-permute-start(bf16[2,6,256,128]{3,2,1,0:T(8,128)(2,1)} %get-tuple-element.50), channel_id=1, source_target_pairs={{0,1},{1,0},{2,3},{3,2},{4,5},{5,4},{6,7},{7,6},{8,9},{9,8},{10,11... | collective-permute-start | bytes 2359304 | tf_op jit(solution)/shard_map/ppermute | solution.py:227
  28.4 48.8 %collective-permute-start.4 = (bf16[2,6,256,128]{3,2,1,0:T(8,128)(2,1)}, bf16[2,6,256,128]{3,2,1,0:T(8,128)(2,1)}, u32[]{:S(2)}, u32[]{:S(2)}) collective-permute-start(bf16[2,6,256,128]{3,2,1,0:T(8,128)(2,1)} %get-tuple-element.63), channel_id=1, source_target_pairs={{0,3},{1,2},{2,5},{3,4},{4,7},{5,6},{6,1},{7,0},{8,11},{9,10},{10,... | collective-permute-start | bytes 2359304 | tf_op jit(solution)/shard_map/ppermute | solution.py:227
  41.8 37.5 %collective-permute-start.5 = (bf16[2,6,256,128]{3,2,1,0:T(8,128)(2,1)}, bf16[2,6,256,128]{3,2,1,0:T(8,128)(2,1)}, u32[]{:S(2)}, u32[]{:S(2)}) collective-permute-start(bf16[2,6,256,128]{3,2,1,0:T(8,128)(2,1)} %get-tuple-element.65), channel_id=1, source_target_pairs={{0,5},{1,4},{2,7},{3,6},{4,1},{5,0},{6,3},{7,2},{8,13},{9,12},{10,... | collective-permute-start | bytes 2359304 | tf_op jit(solution)/shard_map/ppermute | solution.py:227
  45.9 49.9 %collective-permute-start.6 = (bf16[2,6,256,128]{3,2,1,0:T(8,128)(2,1)}, bf16[2,6,256,128]{3,2,1,0:T(8,128)(2,1)}, u32[]{:S(2)}, u32[]{:S(2)}) collective-permute-start(bf16[2,6,256,128]{3,2,1,0:T(8,128)(2,1)} %get-tuple-element.67), channel_id=1, source_target_pairs={{0,7},{1,6},{2,1},{3,0},{4,3},{5,2},{6,5},{7,4},{8,15},{9,14},{10,... | collective-permute-start | bytes 2359304 | tf_op jit(solution)/shard_map/ppermute | solution.py:227
  67.0 31.7 %collective-permute-start.7 = (bf16[1,6,256,128]{3,2,1,0:T(8,128)(2,1)}, bf16[1,6,256,128]{3,2,1,0:T(8,128)(2,1)S(1)}, u32[]{:S(2)}, u32[]{:S(2)}) collective-permute-start(bf16[1,6,256,128]{3,2,1,0:T(8,128)(2,1)} %get-tuple-element.69), channel_id=1, source_target_pairs={{0,1},{1,0},{2,3},{3,2},{4,5},{5,4},{6,7},{7,6},{8,9},{9,8},{10,11... | collective-permute-start | bytes 1179656 | tf_op jit(solution)/shard_map/ppermute | solution.py:227
  67.1 33.8 %collective-permute-start.8 = (bf16[1,6,256,128]{3,2,1,0:T(8,128)(2,1)}, bf16[1,6,256,128]{3,2,1,0:T(8,128)(2,1)S(1)}, u32[]{:S(2)}, u32[]{:S(2)}) collective-permute-start(bf16[1,6,256,128]{3,2,1,0:T(8,128)(2,1)} %get-tuple-element.70), channel_id=1, source_target_pairs={{0,2},{1,3},{2,4},{3,5},{4,6},{5,7},{6,0},{7,1},{8,10},{9,11},{10,... | collective-permute-start | bytes 1179656 | tf_op jit(solution)/shard_map/ppermute | solution.py:227
  77.2 39.8 %collective-permute-start.9 = (bf16[1,6,256,128]{3,2,1,0:T(8,128)(2,1)}, bf16[1,6,256,128]{3,2,1,0:T(8,128)(2,1)}, u32[]{:S(2)}, u32[]{:S(2)}) collective-permute-start(bf16[1,6,256,128]{3,2,1,0:T(8,128)(2,1)} %get-tuple-element.71), channel_id=1, source_target_pairs={{0,3},{1,2},{2,5},{3,4},{4,7},{5,6},{6,1},{7,0},{8,11},{9,10},{10,... | collective-permute-start | bytes 1179656 | tf_op jit(solution)/shard_map/ppermute | solution.py:227
  79.3 37.6 %collective-permute-start.10 = (bf16[1,6,256,128]{3,2,1,0:T(8,128)(2,1)}, bf16[1,6,256,128]{3,2,1,0:T(8,128)(2,1)}, u32[]{:S(2)}, u32[]{:S(2)}) collective-permute-start(bf16[1,6,256,128]{3,2,1,0:T(8,128)(2,1)} %get-tuple-element.72), channel_id=1, source_target_pairs={{0,4},{1,5},{2,6},{3,7},{4,0},{5,1},{6,2},{7,3},{8,12},{9,13},{10,... | collective-permute-start | bytes 1179656 | tf_op jit(solution)/shard_map/ppermute | solution.py:227
  95.9 21.1 %collective-permute-start.11 = (bf16[1,6,256,128]{3,2,1,0:T(8,128)(2,1)}, bf16[1,6,256,128]{3,2,1,0:T(8,128)(2,1)}, u32[]{:S(2)}, u32[]{:S(2)}) collective-permute-start(bf16[1,6,256,128]{3,2,1,0:T(8,128)(2,1)} %get-tuple-element.73), channel_id=1, source_target_pairs={{0,5},{1,4},{2,7},{3,6},{4,1},{5,0},{6,3},{7,2},{8,13},{9,12},{10,... | collective-permute-start | bytes 1179656 | tf_op jit(solution)/shard_map/ppermute | solution.py:227
  98.7 21.9 %collective-permute-start.12 = (bf16[1,6,256,128]{3,2,1,0:T(8,128)(2,1)}, bf16[1,6,256,128]{3,2,1,0:T(8,128)(2,1)}, u32[]{:S(2)}, u32[]{:S(2)}) collective-permute-start(bf16[1,6,256,128]{3,2,1,0:T(8,128)(2,1)} %get-tuple-element.74), channel_id=1, source_target_pairs={{0,6},{1,7},{2,0},{3,1},{4,2},{5,3},{6,4},{7,5},{8,14},{9,15},{10,... | collective-permute-start | bytes 1179656 | tf_op jit(solution)/shard_map/ppermute | solution.py:227
  101.6 27.5 %collective-permute-start.13 = (bf16[1,6,256,128]{3,2,1,0:T(8,128)(2,1)}, bf16[1,6,256,128]{3,2,1,0:T(8,128)(2,1)}, u32[]{:S(2)}, u32[]{:S(2)}) collective-permute-start(bf16[1,6,256,128]{3,2,1,0:T(8,128)(2,1)} %get-tuple-element.75), channel_id=1, source_target_pairs={{0,7},{1,6},{2,1},{3,0},{4,3},{5,2},{6,5},{7,4},{8,15},{9,14},{10,... | collective-permute-start | bytes 1179656 | tf_op jit(solution)/shard_map/ppermute | solution.py:227
  129.1 42.1 %all-to-all-start = ((bf16[8,2,2,256,128]{4,3,2,1,0:T(8,128)(2,1)}), bf16[8,2,2,256,128]{4,3,2,1,0:T(8,128)(2,1)S(1)}, u32[]{:S(2)}, u32[]{:S(2)}) async-start(bf16[8,2,2,256,128]{4,3,2,1,0:T(8,128)(2,1)} %attend.2), calls=%async_computation | async-start | bytes 4194304 | tf_op jit(solution)/shard_map/all_to_all | solution.py:244
  140.2 21.5 %collective-permute-start.15 = (bf16[1,2,256,128]{3,2,1,0:T(8,128)(2,1)S(1)}, bf16[1,2,256,128]{3,2,1,0:T(8,128)(2,1)S(1)}, u32[]{:S(2)}, u32[]{:S(2)}) collective-permute-start(bf16[1,2,256,128]{3,2,1,0:T(8,128)(2,1)S(1)} %get-tuple-element.87), channel_id=1, source_target_pairs={{0,2},{1,3},{2,4},{3,5},{4,6},{5,7},{6,0},{7,1},{8,10},{9,11},{10,... | collective-permute-start | bytes 393224 | tf_op jit(solution)/shard_map/ppermute | solution.py:227
  141.4 23.7 %collective-permute-start.16 = (bf16[1,2,256,128]{3,2,1,0:T(8,128)(2,1)S(1)}, bf16[1,2,256,128]{3,2,1,0:T(8,128)(2,1)S(1)}, u32[]{:S(2)}, u32[]{:S(2)}) collective-permute-start(bf16[1,2,256,128]{3,2,1,0:T(8,128)(2,1)S(1)} %get-tuple-element.88), channel_id=1, source_target_pairs={{0,3},{1,2},{2,5},{3,4},{4,7},{5,6},{6,1},{7,0},{8,11},{9,10},{10,... | collective-permute-start | bytes 393224 | tf_op jit(solution)/shard_map/ppermute | solution.py:227
  142.7 22.5 %collective-permute-start.17 = (bf16[1,2,256,128]{3,2,1,0:T(8,128)(2,1)S(1)}, bf16[1,2,256,128]{3,2,1,0:T(8,128)(2,1)S(1)}, u32[]{:S(2)}, u32[]{:S(2)}) collective-permute-start(bf16[1,2,256,128]{3,2,1,0:T(8,128)(2,1)S(1)} %get-tuple-element.89), channel_id=1, source_target_pairs={{0,4},{1,5},{2,6},{3,7},{4,0},{5,1},{6,2},{7,3},{8,12},{9,13},{10,... | collective-permute-start | bytes 393224 | tf_op jit(solution)/shard_map/ppermute | solution.py:227
  143.8 22.8 %collective-permute-start.18 = (bf16[1,2,256,128]{3,2,1,0:T(8,128)(2,1)S(1)}, bf16[1,2,256,128]{3,2,1,0:T(8,128)(2,1)S(1)}, u32[]{:S(2)}, u32[]{:S(2)}) collective-permute-start(bf16[1,2,256,128]{3,2,1,0:T(8,128)(2,1)S(1)} %get-tuple-element.90), channel_id=1, source_target_pairs={{0,5},{1,4},{2,7},{3,6},{4,1},{5,0},{6,3},{7,2},{8,13},{9,12},{10,... | collective-permute-start | bytes 393224 | tf_op jit(solution)/shard_map/ppermute | solution.py:227
  145.9 22.3 %collective-permute-start.19 = (bf16[1,2,256,128]{3,2,1,0:T(8,128)(2,1)S(1)}, bf16[1,2,256,128]{3,2,1,0:T(8,128)(2,1)S(1)}, u32[]{:S(2)}, u32[]{:S(2)}) collective-permute-start(bf16[1,2,256,128]{3,2,1,0:T(8,128)(2,1)S(1)} %get-tuple-element.91), channel_id=1, source_target_pairs={{0,6},{1,7},{2,0},{3,1},{4,2},{5,3},{6,4},{7,5},{8,14},{9,15},{10,... | collective-permute-start | bytes 393224 | tf_op jit(solution)/shard_map/ppermute | solution.py:227
  161.8 9.4 %collective-permute-start.20 = (bf16[1,2,256,128]{3,2,1,0:T(8,128)(2,1)S(1)}, bf16[1,2,256,128]{3,2,1,0:T(8,128)(2,1)S(1)}, u32[]{:S(2)}, u32[]{:S(2)}) collective-permute-start(bf16[1,2,256,128]{3,2,1,0:T(8,128)(2,1)S(1)} %get-tuple-element.92), channel_id=1, source_target_pairs={{0,7},{1,6},{2,1},{3,0},{4,3},{5,2},{6,5},{7,4},{8,15},{9,14},{10,... | collective-permute-start | bytes 393224 | tf_op jit(solution)/shard_map/ppermute | solution.py:227
  (11 other events, 392.6 us)
Sparse Core Ops, SparseCore 0:
  22.8 124.2 all-gather.1

commit v6 on v5

--- a/solution.py
+++ b/solution.py
@@ -116,11 +116,13 @@
                 store(head, frame + i, 0, primal[part])
                 store(head, frame + i, 1, tangent[part])
 
-        def two_frames(i, carry):
-            block(start + 2 * i, 2)
+        def four_frames(i, carry):
+            block(start + 4 * i, 4)
             return carry
 
-        lax.fori_loop(0, count // 2, two_frames, 0)
+        lax.fori_loop(0, count // 4, four_frames, 0)
+        if count % 4 >= 2:
+            block(start + count - count % 4, 2)
         if count % 2:
             block(start + count - 1, 1)
 
@@ -175,12 +177,20 @@
 
 
 def project_kernel(members, moved, *refs):
-    last, (w, out, tangent, held, sems) = refs[:members], refs[members:]
+    last, (w, out, tangent, held, tiles, sems, tile_sems) = refs[:members], refs[members:]
     _, size, _, rows, _ = moved.shape
     rounds = size + last[0].shape[0]
-
-    @pl.when(pl.program_id(0) == 0)
+    width = tiles.shape[2]
+    step, steps = pl.program_id(0), pl.num_programs(0)
+
+    def load(n):
+        at = pl.ds(pl.multiple_of(n * width, width), width)
+        slot = lax.rem(n, 2)
+        return pltpu.make_async_copy(w.at[:, at], tiles.at[slot], tile_sems.at[slot])
+
+    @pl.when(step == 0)
     def _():
+        load(step).start()
         pairs = []
         for b in range(members):
             u = member(b, members, True)
@@ -192,7 +202,12 @@
                     pairs.append((source, held.at[which * rows : (which + 1) * rows, at]))
         run_copies(pairs, sems)
 
-    product = jnp.dot(held[...], w[...], preferred_element_type=jnp.float32)
+    @pl.when(step + 1 < steps)
+    def _():
+        load(step + 1).start()
+
+    load(step).wait()
+    product = jnp.dot(held[...], tiles[lax.rem(step, 2)], preferred_element_type=jnp.float32)
     out[...] = product[:rows].astype(BF16)
     tangent[...] = product[rows:].astype(BF16)
 
@@ -200,17 +215,19 @@
 def project(moved, last, weight):
     members, size, _, rows, _ = moved.shape
     depth, width = weight.shape
-    tile = 768
+    tile = 512
     given = pl.BlockSpec((rows, tile), lambda step: (0, step))
     return pl.pallas_call(
         functools.partial(project_kernel, members),
         grid=(width // tile,),
-        in_specs=[ANY] * (1 + members) + [pl.BlockSpec((depth, tile), lambda step: (0, step))],
+        in_specs=[ANY] * (2 + members),
         out_specs=[given, given],
         out_shape=[jax.ShapeDtypeStruct((rows, width), BF16)] * 2,
         scratch_shapes=[
             pltpu.VMEM((2 * rows, depth), BF16),
+            pltpu.VMEM((2, depth, tile), BF16),
             pltpu.SemaphoreType.DMA((2 * depth // HEAD_DIM,)),
+            pltpu.SemaphoreType.DMA((2,)),
         ],
         compiler_params=pltpu.CompilerParams(vmem_limit_bytes=40 * 2**20),
         name="project",

time: 196 us -> 196 us (level)
  waiting for transfers between devices: 76.3 us -> 72.7 us
  Pallas kernels: 39.7 us -> 42.5 us
    ppermute x25, waiting for transfers between devices: 76.2 us -> 72.7 us  [hop(): return lax.ppermute(value, 'ulysses', pairs)]
    pallas_call x2, Pallas kernels: 13.9 us -> 17.4 us  [attend(): pl.pallas_call(functools.partial(attend_kernel, members, apart), in_specs...]
  transfers between devices with their start and end apart: 27 -> 27, of which waited for: 13 -> 13; matrix products, arithmetic and copies ran while one was open for 1% -> 1% of each run, Pallas kernels for 13% -> 15%
where the time goes in v6:
time: 196 us; the launch traced here: 192 us
  waiting for transfers between devices  72.7 us (37%)
  starting transfers between devices  58.6 us (30%)
  Pallas kernels  42.5 us (22%)
  between operations  14.3 us (7%)
  other arithmetic  2.16 us (1%)
  local copies, waits for them, and re-layouts  2.03 us (1%)
    ppermute x25, waiting for transfers between devices, hop(): return lax.ppermute(value, 'ulysses', pairs)  72.7 us
    ppermute x25, starting transfers between devices, hop(): return lax.ppermute(value, 'ulysses', pairs)  52.6 us
    pallas_call x2, Pallas kernels, attend(): pl.pallas_call(functools.partial(attend_kernel, members, apart), in_specs...  17.4 us
    pallas_call x1, Pallas kernels, project(): pl.pallas_call(functools.partial(project_kernel, members), grid=(width //...  14.4 us
    pallas_call x3, Pallas kernels, pack(): pl.pallas_call(functools.partial(pack_kernel, first, rounds, members, blo...  10.7 us
    all_to_all x1, starting transfers between devices, exchange(): return lax.all_to_all(x, 'ulysses', split_axis=0, concat_axis=0, tiled=True)  6 us
  transfers between devices with their start and end apart: 27, of which 13 were waited for; matrix products, arithmetic and copies ran while one was open for 1% of the time, Pallas kernels for 15%

profile of v6, /device:TPU:19, one launch (start us, length us, event | category | flops | bytes accessed | tf_op | source)
XLA Modules:
  0.0 192.4 jit_solution(18270508587869529910)
XLA Ops:
  7.2 1.9 %collective-permute-start.22 = (bf16[24,3072]{1,0:T(8,128)(2,1)}, bf16[24,3072]{1,0:T(8,128)(2,1)S(1)}, u32[]{:S(2)}, u32[]{:S(2)}) collective-permute-start(bf16[24,3072]{1,0:T(8,128)(2,1)} %param.16), channel_id=1, source_target_pairs={{0,4},{1,5},{2,6},{3,7},{4,0},{5,1},{6,2},{7,3},{8,12},{9,13},{10,... | collective-permute-start | bytes 442376 | tf_op jit(solution)/shard_map/ppermute | solution.py:244
  10.6 2.9 %pack.5 = (bf16[2,6,256,128]{3,2,1,0:T(8,128)(2,1)}, bf16[2,6,256,128]{3,2,1,0:T(8,128)(2,1)}, bf16[2,6,256,128]{3,2,1,0:T(8,128)(2,1)}) custom-call(bf16[256,3072]{1,0:T(8,128)(2,1)} %refs_0_.5, bf16[256,3072]{1,0:T(8,128)(2,1)} %refs_1_.5, bf16[256,3072]{1,0:T(8,128)(2,1)} %refs_2_.5, bf16[256,3072]{1,0:T(8,128)(2,1)} %refs_3_.5, ...), custom_call_target="tpu_custom_call" | custom-call | tf_op jit(solution)/shard_map/pack/pallas_call | solution.py:63
  13.5 4.2 %pack.3 = (bf16[2,6,256,128]{3,2,1,0:T(8,128)(2,1)}, bf16[2,6,256,128]{3,2,1,0:T(8,128)(2,1)}, bf16[2,6,256,128]{3,2,1,0:T(8,128)(2,1)}, bf16[2,6,256,128]{3,2,1,0:T(8,128)(2,1)}, bf16[2,6,256,128]{3,2,1,0:T(8,128)(2,1)}) custom-call(bf16[256,3072]{1,0:T(8,128)(2,1)} %refs_0_.5, bf16[256,3072]{1,0:T(8,128)(2,1)} %refs_1_.5, bf16[256,3072]{1,0:T(8,128)(2,1)} %refs_2_.5, ...), custom_call_target="tpu_custom_call" | custom-call | tf_op jit(solution)/shard_map/pack/pallas_call | solution.py:63
  19.7 1.6 collective-permute-done.24
  23.0 2.7 %collective-permute-start.2 = (bf16[2,6,256,128]{3,2,1,0:T(8,128)(2,1)}, bf16[2,6,256,128]{3,2,1,0:T(8,128)(2,1)S(1)}, u32[]{:S(2)}, u32[]{:S(2)}) collective-permute-start(bf16[2,6,256,128]{3,2,1,0:T(8,128)(2,1)} %get-tuple-element.60), channel_id=1, source_target_pairs={{0,4},{1,5},{2,6},{3,7},{4,0},{5,1},{6,2},{7,3},{8,12},{9,13},{10,... | collective-permute-start | bytes 2359304 | tf_op jit(solution)/shard_map/ppermute | solution.py:244
  28.4 13.4 %collective-permute-done.1.refs_2_ = bf16[2,6,256,128]{3,2,1,0:T(8,128)(2,1)S(1)} collective-permute-done((bf16[2,6,256,128]{3,2,1,0:T(8,128)(2,1)}, bf16[2,6,256,128]{3,2,1,0:T(8,128)(2,1)S(1)}, u32[]{:S(2)}, u32[]{:S(2)}) %collective-permute-start.1) | collective-permute-done | bytes 786464 | tf_op jit(solution)/shard_map/ppermute | solution.py:244
  41.8 4.1 %collective-permute-start.5 = (bf16[2,6,256,128]{3,2,1,0:T(8,128)(2,1)}, bf16[2,6,256,128]{3,2,1,0:T(8,128)(2,1)}, u32[]{:S(2)}, u32[]{:S(2)}) collective-permute-start(bf16[2,6,256,128]{3,2,1,0:T(8,128)(2,1)} %get-tuple-element.65), channel_id=1, source_target_pairs={{0,5},{1,4},{2,7},{3,6},{4,1},{5,0},{6,3},{7,2},{8,13},{9,12},{10,... | collective-permute-start | bytes 2359304 | tf_op jit(solution)/shard_map/ppermute | solution.py:244
  45.9 17.5 %collective-permute-start.6 = (bf16[2,6,256,128]{3,2,1,0:T(8,128)(2,1)}, bf16[2,6,256,128]{3,2,1,0:T(8,128)(2,1)}, u32[]{:S(2)}, u32[]{:S(2)}) collective-permute-start(bf16[2,6,256,128]{3,2,1,0:T(8,128)(2,1)} %get-tuple-element.67), channel_id=1, source_target_pairs={{0,7},{1,6},{2,1},{3,0},{4,3},{5,2},{6,5},{7,4},{8,15},{9,14},{10,... | collective-permute-start | bytes 2359304 | tf_op jit(solution)/shard_map/ppermute | solution.py:244
  63.4 3.5 %pack.4 = (bf16[1,6,256,128]{3,2,1,0:T(8,128)(2,1)}, bf16[1,6,256,128]{3,2,1,0:T(8,128)(2,1)}, bf16[1,6,256,128]{3,2,1,0:T(8,128)(2,1)}, bf16[1,6,256,128]{3,2,1...) custom-call(bf16[256,3072]{1,0:T(8,128)(2,1)} %refs_0_.5, ...), custom_call_target="tpu_custom_call" | custom-call | tf_op jit(solution)/shard_map/pack/pallas_call | solution.py:63
  67.1 10.0 %collective-permute-done.4.refs_3_ = bf16[2,6,256,128]{3,2,1,0:T(8,128)(2,1)} collective-permute-done((bf16[2,6,256,128]{3,2,1,0:T(8,128)(2,1)}, bf16[2,6,256,128]{3,2,1,0:T(8,128)(2,1)}, u32[]{:S(2)}, u32[]{:S(2)}) %collective-permute-start.4) | collective-permute-done | bytes 786464 | tf_op jit(solution)/shard_map/ppermute | solution.py:244
  79.3 2.4 %collective-permute-start.10 = (bf16[1,6,256,128]{3,2,1,0:T(8,128)(2,1)}, bf16[1,6,256,128]{3,2,1,0:T(8,128)(2,1)}, u32[]{:S(2)}, u32[]{:S(2)}) collective-permute-start(bf16[1,6,256,128]{3,2,1,0:T(8,128)(2,1)} %get-tuple-element.72), channel_id=1, source_target_pairs={{0,4},{1,5},{2,6},{3,7},{4,0},{5,1},{6,2},{7,3},{8,12},{9,13},{10,... | collective-permute-start | bytes 1179656 | tf_op jit(solution)/shard_map/ppermute | solution.py:244
  81.7 14.2 %collective-permute-done.6.refs_7_ = bf16[2,6,256,128]{3,2,1,0:T(8,128)(2,1)} collective-permute-done((bf16[2,6,256,128]{3,2,1,0:T(8,128)(2,1)}, bf16[2,6,256,128]{3,2,1,0:T(8,128)(2,1)}, u32[]{:S(2)}, u32[]{:S(2)}) %collective-permute-start.6) | collective-permute-done | bytes 786464 | tf_op jit(solution)/shard_map/ppermute | solution.py:244
  95.9 2.8 %collective-permute-start.11 = (bf16[1,6,256,128]{3,2,1,0:T(8,128)(2,1)}, bf16[1,6,256,128]{3,2,1,0:T(8,128)(2,1)}, u32[]{:S(2)}, u32[]{:S(2)}) collective-permute-start(bf16[1,6,256,128]{3,2,1,0:T(8,128)(2,1)} %get-tuple-element.73), channel_id=1, source_target_pairs={{0,5},{1,4},{2,7},{3,6},{4,1},{5,0},{6,3},{7,2},{8,13},{9,12},{10,... | collective-permute-start | bytes 1179656 | tf_op jit(solution)/shard_map/ppermute | solution.py:244
  99.0 1.9 collective-permute-done.8.refs_2_
  101.6 4.1 %collective-permute-start.13 = (bf16[1,6,256,128]{3,2,1,0:T(8,128)(2,1)}, bf16[1,6,256,128]{3,2,1,0:T(8,128)(2,1)}, u32[]{:S(2)}, u32[]{:S(2)}) collective-permute-start(bf16[1,6,256,128]{3,2,1,0:T(8,128)(2,1)} %get-tuple-element.75), channel_id=1, source_target_pairs={{0,7},{1,6},{2,1},{3,0},{4,3},{5,2},{6,5},{7,4},{8,15},{9,14},{10,... | collective-permute-start | bytes 1179656 | tf_op jit(solution)/shard_map/ppermute | solution.py:244
  107.7 11.6 %attend.2 = bf16[8,2,2,256,128]{4,3,2,1,0:T(8,128)(2,1)} custom-call(s32[2]{0:T(128)S(1)} %pad_add_fusion.info, bf16[2,6,256,128]{3,2,1,0:T(8,128)(2,1)S(1)} %copy-done, bf16[2,6,256,128]{3,2,1,0:T(8,128)(2,1)} %collective-permute-done.refs_1_, bf16[2,6,256,128]{3,2,1,0:T(8,128)(2,1)S(1)} %collective-permute-done.1.refs_2_, ...), custom_call_target="tpu_custom_call" | custom-call | tf_op jit(solution)/shard_map/attend/pallas_call | solution.py:166
  120.6 8.5 %collective-permute-done.13.refs_7_ = bf16[1,6,256,128]{3,2,1,0:T(8,128)(2,1)} collective-permute-done((bf16[1,6,256,128]{3,2,1,0:T(8,128)(2,1)}, bf16[1,6,256,128]{3,2,1,0:T(8,128)(2,1)}, u32[]{:S(2)}, u32[]{:S(2)}) %collective-permute-start.13) | collective-permute-done | bytes 393248 | tf_op jit(solution)/shard_map/ppermute | solution.py:244
  129.1 6.0 %all-to-all-start = ((bf16[8,2,2,256,128]{4,3,2,1,0:T(8,128)(2,1)}), bf16[8,2,2,256,128]{4,3,2,1,0:T(8,128)(2,1)S(1)}, u32[]{:S(2)}, u32[]{:S(2)}) async-start(bf16[8,2,2,256,128]{4,3,2,1,0:T(8,128)(2,1)} %attend.2), calls=%async_computation | async-start | bytes 4194304 | tf_op jit(solution)/shard_map/all_to_all | solution.py:261
  135.1 5.9 %attend.3 = (bf16[1,2,256,128]{3,2,1,0:T(8,128)(2,1)S(1)}, bf16[1,2,256,128]{3,2,1,0:T(8,128)(2,1)S(1)}, bf16[1,2,256,128]{3,2,1,0:T(8,128)(2,1)S(1)}, bf16[1,2,...) custom-call(s32[2]{0:T(128)S(1)} %pad_add_fusion.info, ...), custom_call_target="tpu_custom_call" | custom-call | tf_op jit(solution)/shard_map/attend/pallas_call | solution.py:166
  145.0 2.0 %collective-permute-start.18 = (bf16[1,2,256,128]{3,2,1,0:T(8,128)(2,1)S(1)}, bf16[1,2,256,128]{3,2,1,0:T(8,128)(2,1)S(1)}, u32[]{:S(2)}, u32[]{:S(2)}) collective-permute-start(bf16[1,2,256,128]{3,2,1,0:T(8,128)(2,1)S(1)} %get-tuple-element.90), channel_id=1, source_target_pairs={{0,5},{1,4},{2,7},{3,6},{4,1},{5,0},{6,3},{7,2},{8,13},{9,12},{10,... | collective-permute-start | bytes 393224 | tf_op jit(solution)/shard_map/ppermute | solution.py:244
  147.6 14.1 %collective-permute-done.15.refs_2_ = bf16[1,2,256,128]{3,2,1,0:T(8,128)(2,1)S(1)} collective-permute-done((bf16[1,2,256,128]{3,2,1,0:T(8,128)(2,1)S(1)}, bf16[1,2,256,128]{3,2,1,0:T(8,128)(2,1)S(1)}, u32[]{:S(2)}, u32[]{:S(2)}) %collective-permute-start.15) | collective-permute-done | bytes 131104 | tf_op jit(solution)/shard_map/ppermute | solution.py:244
  161.8 3.3 %collective-permute-start.20 = (bf16[1,2,256,128]{3,2,1,0:T(8,128)(2,1)S(1)}, bf16[1,2,256,128]{3,2,1,0:T(8,128)(2,1)S(1)}, u32[]{:S(2)}, u32[]{:S(2)}) collective-permute-start(bf16[1,2,256,128]{3,2,1,0:T(8,128)(2,1)S(1)} %get-tuple-element.92), channel_id=1, source_target_pairs={{0,7},{1,6},{2,1},{3,0},{4,3},{5,2},{6,5},{7,4},{8,15},{9,14},{10,... | collective-permute-start | bytes 393224 | tf_op jit(solution)/shard_map/ppermute | solution.py:244
  168.2 3.0 %collective-permute-done.20.refs_7_ = bf16[1,2,256,128]{3,2,1,0:T(8,128)(2,1)S(1)} collective-permute-done((bf16[1,2,256,128]{3,2,1,0:T(8,128)(2,1)S(1)}, bf16[1,2,256,128]{3,2,1,0:T(8,128)(2,1)S(1)}, u32[]{:S(2)}, u32[]{:S(2)}) %collective-permute-start.20) | collective-permute-done | bytes 131104 | tf_op jit(solution)/shard_map/ppermute | solution.py:244
  171.2 14.4 %project.1 = (bf16[256,3072]{1,0:T(8,128)(2,1)}, bf16[256,3072]{1,0:T(8,128)(2,1)}) custom-call(bf16[8,2,2,256,128]{4,3,2,1,0:T(8,128)(2,1)S(1)} %all-to-all-done.moved, bf16[1,2,256,128]{3,2,1,0:T(8,128)(2,1)S(1)} %get-tuple-element.85.refs_0_, bf16[1,2,256,128]{3,2,1,0:T(8,128)(2,1)S(1)} %collective-permute-done.14.refs_1_, ...), custom_call_target="tpu_custom_call" | custom-call | tf_op jit(solution)/shard_map/project/pallas_call | solution.py:220
  (67 shorter events, 21.9 us)
Async XLA Ops:
  7.2 164.0 %all-gather.2.cloned.1.call-start = ((), (), s32[]{:S(2)}) async-start(), calls=%async_computation.1 | async-start | bytes 20054016 | tf_op jit(solution)/shard_map/all_gather | solution.py:283
  7.2 10.6 %collective-permute-start.22 = (bf16[24,3072]{1,0:T(8,128)(2,1)}, bf16[24,3072]{1,0:T(8,128)(2,1)S(1)}, u32[]{:S(2)}, u32[]{:S(2)}) collective-permute-start(bf16[24,3072]{1,0:T(8,128)(2,1)} %param.16), channel_id=1, source_target_pairs={{0,4},{1,5},{2,6},{3,7},{4,0},{5,1},{6,2},{7,3},{8,12},{9,13},{10,... | collective-permute-start | bytes 442376 | tf_op jit(solution)/shard_map/ppermute | solution.py:244
  9.1 8.8 %collective-permute-start.21 = (bf16[24,3072]{1,0:T(8,128)(2,1)}, bf16[24,3072]{1,0:T(8,128)(2,1)S(1)}, u32[]{:S(2)}, u32[]{:S(2)}) collective-permute-start(bf16[24,3072]{1,0:T(8,128)(2,1)} %param.16), channel_id=1, source_target_pairs={{0,6},{1,7},{2,0},{3,1},{4,2},{5,3},{6,4},{7,5},{8,14},{9,15},{10,... | collective-permute-start | bytes 442376 | tf_op jit(solution)/shard_map/ppermute | solution.py:244
  22.7 19.1 %collective-permute-start.1 = (bf16[2,6,256,128]{3,2,1,0:T(8,128)(2,1)}, bf16[2,6,256,128]{3,2,1,0:T(8,128)(2,1)S(1)}, u32[]{:S(2)}, u32[]{:S(2)}) collective-permute-start(bf16[2,6,256,128]{3,2,1,0:T(8,128)(2,1)} %get-tuple-element.59), channel_id=1, source_target_pairs={{0,2},{1,3},{2,4},{3,5},{4,6},{5,7},{6,0},{7,1},{8,10},{9,11},{10,... | collective-permute-start | bytes 2359304 | tf_op jit(solution)/shard_map/ppermute | solution.py:244
  23.0 22.9 %collective-permute-start.2 = (bf16[2,6,256,128]{3,2,1,0:T(8,128)(2,1)}, bf16[2,6,256,128]{3,2,1,0:T(8,128)(2,1)S(1)}, u32[]{:S(2)}, u32[]{:S(2)}) collective-permute-start(bf16[2,6,256,128]{3,2,1,0:T(8,128)(2,1)} %get-tuple-element.60), channel_id=1, source_target_pairs={{0,4},{1,5},{2,6},{3,7},{4,0},{5,1},{6,2},{7,3},{8,12},{9,13},{10,... | collective-permute-start | bytes 2359304 | tf_op jit(solution)/shard_map/ppermute | solution.py:244
  25.7 41.3 %collective-permute-start.3 = (bf16[2,6,256,128]{3,2,1,0:T(8,128)(2,1)}, bf16[2,6,256,128]{3,2,1,0:T(8,128)(2,1)S(1)}, u32[]{:S(2)}, u32[]{:S(2)}) collective-permute-start(bf16[2,6,256,128]{3,2,1,0:T(8,128)(2,1)} %get-tuple-element.61), channel_id=1, source_target_pairs={{0,6},{1,7},{2,0},{3,1},{4,2},{5,3},{6,4},{7,5},{8,14},{9,15},{10,... | collective-permute-start | bytes 2359304 | tf_op jit(solution)/shard_map/ppermute | solution.py:244
  27.2 39.9 %collective-permute-start = (bf16[2,6,256,128]{3,2,1,0:T(8,128)(2,1)}, bf16[2,6,256,128]{3,2,1,0:T(8,128)(2,1)}, u32[]{:S(2)}, u32[]{:S(2)}) collective-permute-start(bf16[2,6,256,128]{3,2,1,0:T(8,128)(2,1)} %get-tuple-element.50), channel_id=1, source_target_pairs={{0,1},{1,0},{2,3},{3,2},{4,5},{5,4},{6,7},{7,6},{8,9},{9,8},{10,11... | collective-permute-start | bytes 2359304 | tf_op jit(solution)/shard_map/ppermute | solution.py:244
  28.4 48.8 %collective-permute-start.4 = (bf16[2,6,256,128]{3,2,1,0:T(8,128)(2,1)}, bf16[2,6,256,128]{3,2,1,0:T(8,128)(2,1)}, u32[]{:S(2)}, u32[]{:S(2)}) collective-permute-start(bf16[2,6,256,128]{3,2,1,0:T(8,128)(2,1)} %get-tuple-element.63), channel_id=1, source_target_pairs={{0,3},{1,2},{2,5},{3,4},{4,7},{5,6},{6,1},{7,0},{8,11},{9,10},{10,... | collective-permute-start | bytes 2359304 | tf_op jit(solution)/shard_map/ppermute | solution.py:244
  41.8 37.5 %collective-permute-start.5 = (bf16[2,6,256,128]{3,2,1,0:T(8,128)(2,1)}, bf16[2,6,256,128]{3,2,1,0:T(8,128)(2,1)}, u32[]{:S(2)}, u32[]{:S(2)}) collective-permute-start(bf16[2,6,256,128]{3,2,1,0:T(8,128)(2,1)} %get-tuple-element.65), channel_id=1, source_target_pairs={{0,5},{1,4},{2,7},{3,6},{4,1},{5,0},{6,3},{7,2},{8,13},{9,12},{10,... | collective-permute-start | bytes 2359304 | tf_op jit(solution)/shard_map/ppermute | solution.py:244
  45.9 49.9 %collective-permute-start.6 = (bf16[2,6,256,128]{3,2,1,0:T(8,128)(2,1)}, bf16[2,6,256,128]{3,2,1,0:T(8,128)(2,1)}, u32[]{:S(2)}, u32[]{:S(2)}) collective-permute-start(bf16[2,6,256,128]{3,2,1,0:T(8,128)(2,1)} %get-tuple-element.67), channel_id=1, source_target_pairs={{0,7},{1,6},{2,1},{3,0},{4,3},{5,2},{6,5},{7,4},{8,15},{9,14},{10,... | collective-permute-start | bytes 2359304 | tf_op jit(solution)/shard_map/ppermute | solution.py:244
  67.0 31.7 %collective-permute-start.7 = (bf16[1,6,256,128]{3,2,1,0:T(8,128)(2,1)}, bf16[1,6,256,128]{3,2,1,0:T(8,128)(2,1)S(1)}, u32[]{:S(2)}, u32[]{:S(2)}) collective-permute-start(bf16[1,6,256,128]{3,2,1,0:T(8,128)(2,1)} %get-tuple-element.69), channel_id=1, source_target_pairs={{0,1},{1,0},{2,3},{3,2},{4,5},{5,4},{6,7},{7,6},{8,9},{9,8},{10,11... | collective-permute-start | bytes 1179656 | tf_op jit(solution)/shard_map/ppermute | solution.py:244
  67.1 33.8 %collective-permute-start.8 = (bf16[1,6,256,128]{3,2,1,0:T(8,128)(2,1)}, bf16[1,6,256,128]{3,2,1,0:T(8,128)(2,1)S(1)}, u32[]{:S(2)}, u32[]{:S(2)}) collective-permute-start(bf16[1,6,256,128]{3,2,1,0:T(8,128)(2,1)} %get-tuple-element.70), channel_id=1, source_target_pairs={{0,2},{1,3},{2,4},{3,5},{4,6},{5,7},{6,0},{7,1},{8,10},{9,11},{10,... | collective-permute-start | bytes 1179656 | tf_op jit(solution)/shard_map/ppermute | solution.py:244
  77.2 42.1 %collective-permute-start.9 = (bf16[1,6,256,128]{3,2,1,0:T(8,128)(2,1)}, bf16[1,6,256,128]{3,2,1,0:T(8,128)(2,1)}, u32[]{:S(2)}, u32[]{:S(2)}) collective-permute-start(bf16[1,6,256,128]{3,2,1,0:T(8,128)(2,1)} %get-tuple-element.71), channel_id=1, source_target_pairs={{0,3},{1,2},{2,5},{3,4},{4,7},{5,6},{6,1},{7,0},{8,11},{9,10},{10,... | collective-permute-start | bytes 1179656 | tf_op jit(solution)/shard_map/ppermute | solution.py:244
  79.3 40.0 %collective-permute-start.10 = (bf16[1,6,256,128]{3,2,1,0:T(8,128)(2,1)}, bf16[1,6,256,128]{3,2,1,0:T(8,128)(2,1)}, u32[]{:S(2)}, u32[]{:S(2)}) collective-permute-start(bf16[1,6,256,128]{3,2,1,0:T(8,128)(2,1)} %get-tuple-element.72), channel_id=1, source_target_pairs={{0,4},{1,5},{2,6},{3,7},{4,0},{5,1},{6,2},{7,3},{8,12},{9,13},{10,... | collective-permute-start | bytes 1179656 | tf_op jit(solution)/shard_map/ppermute | solution.py:244
  95.9 23.4 %collective-permute-start.11 = (bf16[1,6,256,128]{3,2,1,0:T(8,128)(2,1)}, bf16[1,6,256,128]{3,2,1,0:T(8,128)(2,1)}, u32[]{:S(2)}, u32[]{:S(2)}) collective-permute-start(bf16[1,6,256,128]{3,2,1,0:T(8,128)(2,1)} %get-tuple-element.73), channel_id=1, source_target_pairs={{0,5},{1,4},{2,7},{3,6},{4,1},{5,0},{6,3},{7,2},{8,13},{9,12},{10,... | collective-permute-start | bytes 1179656 | tf_op jit(solution)/shard_map/ppermute | solution.py:244
  98.7 21.9 %collective-permute-start.12 = (bf16[1,6,256,128]{3,2,1,0:T(8,128)(2,1)}, bf16[1,6,256,128]{3,2,1,0:T(8,128)(2,1)}, u32[]{:S(2)}, u32[]{:S(2)}) collective-permute-start(bf16[1,6,256,128]{3,2,1,0:T(8,128)(2,1)} %get-tuple-element.74), channel_id=1, source_target_pairs={{0,6},{1,7},{2,0},{3,1},{4,2},{5,3},{6,4},{7,5},{8,14},{9,15},{10,... | collective-permute-start | bytes 1179656 | tf_op jit(solution)/shard_map/ppermute | solution.py:244
  101.6 27.5 %collective-permute-start.13 = (bf16[1,6,256,128]{3,2,1,0:T(8,128)(2,1)}, bf16[1,6,256,128]{3,2,1,0:T(8,128)(2,1)}, u32[]{:S(2)}, u32[]{:S(2)}) collective-permute-start(bf16[1,6,256,128]{3,2,1,0:T(8,128)(2,1)} %get-tuple-element.75), channel_id=1, source_target_pairs={{0,7},{1,6},{2,1},{3,0},{4,3},{5,2},{6,5},{7,4},{8,15},{9,14},{10,... | collective-permute-start | bytes 1179656 | tf_op jit(solution)/shard_map/ppermute | solution.py:244
  129.1 42.1 %all-to-all-start = ((bf16[8,2,2,256,128]{4,3,2,1,0:T(8,128)(2,1)}), bf16[8,2,2,256,128]{4,3,2,1,0:T(8,128)(2,1)S(1)}, u32[]{:S(2)}, u32[]{:S(2)}) async-start(bf16[8,2,2,256,128]{4,3,2,1,0:T(8,128)(2,1)} %attend.2), calls=%async_computation | async-start | bytes 4194304 | tf_op jit(solution)/shard_map/all_to_all | solution.py:261
  141.4 20.3 %collective-permute-start.15 = (bf16[1,2,256,128]{3,2,1,0:T(8,128)(2,1)S(1)}, bf16[1,2,256,128]{3,2,1,0:T(8,128)(2,1)S(1)}, u32[]{:S(2)}, u32[]{:S(2)}) collective-permute-start(bf16[1,2,256,128]{3,2,1,0:T(8,128)(2,1)S(1)} %get-tuple-element.87), channel_id=1, source_target_pairs={{0,2},{1,3},{2,4},{3,5},{4,6},{5,7},{6,0},{7,1},{8,10},{9,11},{10,... | collective-permute-start | bytes 393224 | tf_op jit(solution)/shard_map/ppermute | solution.py:244
  142.6 22.5 %collective-permute-start.16 = (bf16[1,2,256,128]{3,2,1,0:T(8,128)(2,1)S(1)}, bf16[1,2,256,128]{3,2,1,0:T(8,128)(2,1)S(1)}, u32[]{:S(2)}, u32[]{:S(2)}) collective-permute-start(bf16[1,2,256,128]{3,2,1,0:T(8,128)(2,1)S(1)} %get-tuple-element.88), channel_id=1, source_target_pairs={{0,3},{1,2},{2,5},{3,4},{4,7},{5,6},{6,1},{7,0},{8,11},{9,10},{10,... | collective-permute-start | bytes 393224 | tf_op jit(solution)/shard_map/ppermute | solution.py:244
  143.8 21.3 %collective-permute-start.17 = (bf16[1,2,256,128]{3,2,1,0:T(8,128)(2,1)S(1)}, bf16[1,2,256,128]{3,2,1,0:T(8,128)(2,1)S(1)}, u32[]{:S(2)}, u32[]{:S(2)}) collective-permute-start(bf16[1,2,256,128]{3,2,1,0:T(8,128)(2,1)S(1)} %get-tuple-element.89), channel_id=1, source_target_pairs={{0,4},{1,5},{2,6},{3,7},{4,0},{5,1},{6,2},{7,3},{8,12},{9,13},{10,... | collective-permute-start | bytes 393224 | tf_op jit(solution)/shard_map/ppermute | solution.py:244
  145.0 21.6 %collective-permute-start.18 = (bf16[1,2,256,128]{3,2,1,0:T(8,128)(2,1)S(1)}, bf16[1,2,256,128]{3,2,1,0:T(8,128)(2,1)S(1)}, u32[]{:S(2)}, u32[]{:S(2)}) collective-permute-start(bf16[1,2,256,128]{3,2,1,0:T(8,128)(2,1)S(1)} %get-tuple-element.90), channel_id=1, source_target_pairs={{0,5},{1,4},{2,7},{3,6},{4,1},{5,0},{6,3},{7,2},{8,13},{9,12},{10,... | collective-permute-start | bytes 393224 | tf_op jit(solution)/shard_map/ppermute | solution.py:244
  147.1 21.1 %collective-permute-start.19 = (bf16[1,2,256,128]{3,2,1,0:T(8,128)(2,1)S(1)}, bf16[1,2,256,128]{3,2,1,0:T(8,128)(2,1)S(1)}, u32[]{:S(2)}, u32[]{:S(2)}) collective-permute-start(bf16[1,2,256,128]{3,2,1,0:T(8,128)(2,1)S(1)} %get-tuple-element.91), channel_id=1, source_target_pairs={{0,6},{1,7},{2,0},{3,1},{4,2},{5,3},{6,4},{7,5},{8,14},{9,15},{10,... | collective-permute-start | bytes 393224 | tf_op jit(solution)/shard_map/ppermute | solution.py:244
  161.8 9.4 %collective-permute-start.20 = (bf16[1,2,256,128]{3,2,1,0:T(8,128)(2,1)S(1)}, bf16[1,2,256,128]{3,2,1,0:T(8,128)(2,1)S(1)}, u32[]{:S(2)}, u32[]{:S(2)}) collective-permute-start(bf16[1,2,256,128]{3,2,1,0:T(8,128)(2,1)S(1)} %get-tuple-element.92), channel_id=1, source_target_pairs={{0,7},{1,6},{2,1},{3,0},{4,3},{5,2},{6,5},{7,4},{8,15},{9,14},{10,... | collective-permute-start | bytes 393224 | tf_op jit(solution)/shard_map/ppermute | solution.py:244
  (11 other events, 388.0 us)
Sparse Core Ops, SparseCore 0:
  22.8 124.2 all-gather.1

commit v7 on v6

--- a/solution.py
+++ b/solution.py
@@ -188,34 +188,48 @@
         slot = lax.rem(n, 2)
         return pltpu.make_async_copy(w.at[:, at], tiles.at[slot], tile_sems.at[slot])
 
+    def rows_of(which):
+        copies = []
+        for b in range(members):
+            u = member(b, members, True)
+            for r in range(rounds):
+                source = moved.at[b, r, which] if r < size else last[b].at[r - size, which]
+                head = (b if r < size else u) * rounds + r
+                at = pl.ds(pl.multiple_of(head * HEAD_DIM, HEAD_DIM), HEAD_DIM)
+                to = held.at[which * rows : (which + 1) * rows, at]
+                copies.append(pltpu.make_async_copy(source, to, sems.at[which, len(copies)]))
+        return copies
+
     @pl.when(step == 0)
     def _():
         load(step).start()
-        pairs = []
-        for b in range(members):
-            u = member(b, members, True)
-            for r in range(rounds):
-                for which in range(2):
-                    source = moved.at[b, r, which] if r < size else last[b].at[r - size, which]
-                    head = (b if r < size else u) * rounds + r
-                    at = pl.ds(pl.multiple_of(head * HEAD_DIM, HEAD_DIM), HEAD_DIM)
-                    pairs.append((source, held.at[which * rows : (which + 1) * rows, at]))
-        run_copies(pairs, sems)
+        for which in range(2):
+            for copy in rows_of(which):
+                copy.start()
 
     @pl.when(step + 1 < steps)
     def _():
         load(step + 1).start()
 
+    def product(which):
+        @pl.when(step == 0)
+        def _():
+            for copy in rows_of(which):
+                copy.wait()
+
+        part = held[which * rows : (which + 1) * rows, :]
+        tile = tiles[lax.rem(step, 2)]
+        return jnp.dot(part, tile, preferred_element_type=jnp.float32).astype(BF16)
+
     load(step).wait()
-    product = jnp.dot(held[...], tiles[lax.rem(step, 2)], preferred_element_type=jnp.float32)
-    out[...] = product[:rows].astype(BF16)
-    tangent[...] = product[rows:].astype(BF16)
+    out[...] = product(0)
+    tangent[...] = product(1)
 
 
 def project(moved, last, weight):
     members, size, _, rows, _ = moved.shape
     depth, width = weight.shape
-    tile = 512
+    tile = 768
     given = pl.BlockSpec((rows, tile), lambda step: (0, step))
     return pl.pallas_call(
         functools.partial(project_kernel, members),
@@ -226,7 +240,7 @@
         scratch_shapes=[
             pltpu.VMEM((2 * rows, depth), BF16),
             pltpu.VMEM((2, depth, tile), BF16),
-            pltpu.SemaphoreType.DMA((2 * depth // HEAD_DIM,)),
+            pltpu.SemaphoreType.DMA((2, depth // HEAD_DIM)),
             pltpu.SemaphoreType.DMA((2,)),
         ],
         compiler_params=pltpu.CompilerParams(vmem_limit_bytes=40 * 2**20),

time: 196 us -> 199 us (1.015)
  waiting for transfers between devices: 72.7 us -> 77.8 us
    pallas_call x2, Pallas kernels: 17.4 us -> 12.4 us  [attend(): pl.pallas_call(functools.partial(attend_kernel, members, apart), in_specs...]
    ppermute x25, waiting for transfers between devices: 72.7 us -> 77.8 us  [hop(): return lax.ppermute(value, 'ulysses', pairs)]
    pallas_call x1, Pallas kernels: 14.4 us -> 18.1 us  [project(): pl.pallas_call(functools.partial(project_kernel, members), grid=(width //...]
  transfers between devices with their start and end apart: 27 -> 27, of which waited for: 13 -> 13; matrix products, arithmetic and copies ran while one was open for 1% -> 1% of each run, Pallas kernels for 15% -> 12%
where the time goes in v7:
time: 199 us; the launch traced here: 196 us
  waiting for transfers between devices  77.8 us (39%)
  starting transfers between devices  58.6 us (29%)
  Pallas kernels  41.2 us (21%)
  between operations  14.3 us (7%)
  other arithmetic  2.16 us (1%)
  local copies, waits for them, and re-layouts  2.03 us (1%)
    ppermute x25, waiting for transfers between devices, hop(): return lax.ppermute(value, 'ulysses', pairs)  77.8 us
    ppermute x25, starting transfers between devices, hop(): return lax.ppermute(value, 'ulysses', pairs)  52.6 us
    pallas_call x1, Pallas kernels, project(): pl.pallas_call(functools.partial(project_kernel, members), grid=(width //...  18.1 us
    pallas_call x2, Pallas kernels, attend(): pl.pallas_call(functools.partial(attend_kernel, members, apart), in_specs...  12.4 us
    pallas_call x3, Pallas kernels, pack(): pl.pallas_call(functools.partial(pack_kernel, first, rounds, members, blo...  10.7 us
    all_to_all x1, starting transfers between devices, exchange(): return lax.all_to_all(x, 'ulysses', split_axis=0, concat_axis=0, tiled=True)  6 us
  transfers between devices with their start and end apart: 27, of which 13 were waited for; matrix products, arithmetic and copies ran while one was open for 1% of the time, Pallas kernels for 12%

profile of v7, /device:TPU:19, one launch (start us, length us, event | category | flops | bytes accessed | tf_op | source)
XLA Modules:
  0.0 196.2 jit_solution(11551753651217037960)
XLA Ops:
  7.2 1.9 collective-permute-start.22
  10.6 2.9 %pack.5 = (bf16[2,6,256,128]{3,2,1,0:T(8,128)(2,1)}, bf16[2,6,256,128]{3,2,1,0:T(8,128)(2,1)}, bf16[2,6,256,128]{3,2,1,0:T(8,128)(2,1)}) custom-call(bf16[256,3072]{1,0:T(8,128)(2,1)} %refs_0_.5, bf16[256,3072]{1,0:T(8,128)(2,1)} %refs_1_.5, bf16[256,3072]{1,0:T(8,128)(2,1)} %refs_2_.5, bf16[256,3072]{1,0:T(8,128)(2,1)} %refs_3_.5, ...), custom_call_target="tpu_custom_call" | custom-call | tf_op jit(solution)/shard_map/pack/pallas_call | solution.py:63
  13.5 4.2 %pack.3 = (bf16[2,6,256,128]{3,2,1,0:T(8,128)(2,1)}, bf16[2,6,256,128]{3,2,1,0:T(8,128)(2,1)}, bf16[2,6,256,128]{3,2,1,0:T(8,128)(2,1)}, bf16[2,6,256,128]{3,2,1,0:T(8,128)(2,1)}, bf16[2,6,256,128]{3,2,1,0:T(8,128)(2,1)}) custom-call(bf16[256,3072]{1,0:T(8,128)(2,1)} %refs_0_.5, bf16[256,3072]{1,0:T(8,128)(2,1)} %refs_1_.5, bf16[256,3072]{1,0:T(8,128)(2,1)} %refs_2_.5, ...), custom_call_target="tpu_custom_call" | custom-call | tf_op jit(solution)/shard_map/pack/pallas_call | solution.py:63
  23.0 2.7 %collective-permute-start.2 = (bf16[2,6,256,128]{3,2,1,0:T(8,128)(2,1)}, bf16[2,6,256,128]{3,2,1,0:T(8,128)(2,1)S(1)}, u32[]{:S(2)}, u32[]{:S(2)}) collective-permute-start(bf16[2,6,256,128]{3,2,1,0:T(8,128)(2,1)} %get-tuple-element.60), channel_id=1, source_target_pairs={{0,4},{1,5},{2,6},{3,7},{4,0},{5,1},{6,2},{7,3},{8,12},{9,13},{10,... | collective-permute-start | bytes 2359304 | tf_op jit(solution)/shard_map/ppermute | solution.py:258
  28.4 13.4 %collective-permute-done.1.refs_2_ = bf16[2,6,256,128]{3,2,1,0:T(8,128)(2,1)S(1)} collective-permute-done((bf16[2,6,256,128]{3,2,1,0:T(8,128)(2,1)}, bf16[2,6,256,128]{3,2,1,0:T(8,128)(2,1)S(1)}, u32[]{:S(2)}, u32[]{:S(2)}) %collective-permute-start.1) | collective-permute-done | bytes 786464 | tf_op jit(solution)/shard_map/ppermute | solution.py:258
  41.8 4.1 %collective-permute-start.5 = (bf16[2,6,256,128]{3,2,1,0:T(8,128)(2,1)}, bf16[2,6,256,128]{3,2,1,0:T(8,128)(2,1)}, u32[]{:S(2)}, u32[]{:S(2)}) collective-permute-start(bf16[2,6,256,128]{3,2,1,0:T(8,128)(2,1)} %get-tuple-element.65), channel_id=1, source_target_pairs={{0,5},{1,4},{2,7},{3,6},{4,1},{5,0},{6,3},{7,2},{8,13},{9,12},{10,... | collective-permute-start | bytes 2359304 | tf_op jit(solution)/shard_map/ppermute | solution.py:258
  45.9 17.5 %collective-permute-start.6 = (bf16[2,6,256,128]{3,2,1,0:T(8,128)(2,1)}, bf16[2,6,256,128]{3,2,1,0:T(8,128)(2,1)}, u32[]{:S(2)}, u32[]{:S(2)}) collective-permute-start(bf16[2,6,256,128]{3,2,1,0:T(8,128)(2,1)} %get-tuple-element.67), channel_id=1, source_target_pairs={{0,7},{1,6},{2,1},{3,0},{4,3},{5,2},{6,5},{7,4},{8,15},{9,14},{10,... | collective-permute-start | bytes 2359304 | tf_op jit(solution)/shard_map/ppermute | solution.py:258
  63.4 3.5 %pack.4 = (bf16[1,6,256,128]{3,2,1,0:T(8,128)(2,1)}, bf16[1,6,256,128]{3,2,1,0:T(8,128)(2,1)}, bf16[1,6,256,128]{3,2,1,0:T(8,128)(2,1)}, bf16[1,6,256,128]{3,2,1...) custom-call(bf16[256,3072]{1,0:T(8,128)(2,1)} %refs_0_.5, ...), custom_call_target="tpu_custom_call" | custom-call | tf_op jit(solution)/shard_map/pack/pallas_call | solution.py:63
  67.1 10.0 %collective-permute-done.4.refs_3_ = bf16[2,6,256,128]{3,2,1,0:T(8,128)(2,1)} collective-permute-done((bf16[2,6,256,128]{3,2,1,0:T(8,128)(2,1)}, bf16[2,6,256,128]{3,2,1,0:T(8,128)(2,1)}, u32[]{:S(2)}, u32[]{:S(2)}) %collective-permute-start.4) | collective-permute-done | bytes 786464 | tf_op jit(solution)/shard_map/ppermute | solution.py:258
  79.3 2.4 %collective-permute-start.10 = (bf16[1,6,256,128]{3,2,1,0:T(8,128)(2,1)}, bf16[1,6,256,128]{3,2,1,0:T(8,128)(2,1)}, u32[]{:S(2)}, u32[]{:S(2)}) collective-permute-start(bf16[1,6,256,128]{3,2,1,0:T(8,128)(2,1)} %get-tuple-element.72), channel_id=1, source_target_pairs={{0,4},{1,5},{2,6},{3,7},{4,0},{5,1},{6,2},{7,3},{8,12},{9,13},{10,... | collective-permute-start | bytes 1179656 | tf_op jit(solution)/shard_map/ppermute | solution.py:258
  81.7 14.2 %collective-permute-done.6.refs_7_ = bf16[2,6,256,128]{3,2,1,0:T(8,128)(2,1)} collective-permute-done((bf16[2,6,256,128]{3,2,1,0:T(8,128)(2,1)}, bf16[2,6,256,128]{3,2,1,0:T(8,128)(2,1)}, u32[]{:S(2)}, u32[]{:S(2)}) %collective-permute-start.6) | collective-permute-done | bytes 786464 | tf_op jit(solution)/shard_map/ppermute | solution.py:258
  95.9 2.8 %collective-permute-start.11 = (bf16[1,6,256,128]{3,2,1,0:T(8,128)(2,1)}, bf16[1,6,256,128]{3,2,1,0:T(8,128)(2,1)}, u32[]{:S(2)}, u32[]{:S(2)}) collective-permute-start(bf16[1,6,256,128]{3,2,1,0:T(8,128)(2,1)} %get-tuple-element.73), channel_id=1, source_target_pairs={{0,5},{1,4},{2,7},{3,6},{4,1},{5,0},{6,3},{7,2},{8,13},{9,12},{10,... | collective-permute-start | bytes 1179656 | tf_op jit(solution)/shard_map/ppermute | solution.py:258
  99.0 1.9 collective-permute-done.8.refs_2_
  101.6 4.1 %collective-permute-start.13 = (bf16[1,6,256,128]{3,2,1,0:T(8,128)(2,1)}, bf16[1,6,256,128]{3,2,1,0:T(8,128)(2,1)}, u32[]{:S(2)}, u32[]{:S(2)}) collective-permute-start(bf16[1,6,256,128]{3,2,1,0:T(8,128)(2,1)} %get-tuple-element.75), channel_id=1, source_target_pairs={{0,7},{1,6},{2,1},{3,0},{4,3},{5,2},{6,5},{7,4},{8,15},{9,14},{10,... | collective-permute-start | bytes 1179656 | tf_op jit(solution)/shard_map/ppermute | solution.py:258
  107.7 8.2 %attend.2 = bf16[8,2,2,256,128]{4,3,2,1,0:T(8,128)(2,1)} custom-call(s32[2]{0:T(128)S(1)} %pad_add_fusion.info, bf16[2,6,256,128]{3,2,1,0:T(8,128)(2,1)S(1)} %copy-done, bf16[2,6,256,128]{3,2,1,0:T(8,128)(2,1)} %collective-permute-done.refs_1_, bf16[2,6,256,128]{3,2,1,0:T(8,128)(2,1)S(1)} %collective-permute-done.1.refs_2_, ...), custom_call_target="tpu_custom_call" | custom-call | tf_op jit(solution)/shard_map/attend/pallas_call | solution.py:166
  115.9 4.6 %collective-permute-done.12.refs_6_ = bf16[1,6,256,128]{3,2,1,0:T(8,128)(2,1)} collective-permute-done((bf16[1,6,256,128]{3,2,1,0:T(8,128)(2,1)}, bf16[1,6,256,128]{3,2,1,0:T(8,128)(2,1)}, u32[]{:S(2)}, u32[]{:S(2)}) %collective-permute-start.12) | collective-permute-done | bytes 393248 | tf_op jit(solution)/shard_map/ppermute | solution.py:258
  120.6 8.5 %collective-permute-done.13.refs_7_ = bf16[1,6,256,128]{3,2,1,0:T(8,128)(2,1)} collective-permute-done((bf16[1,6,256,128]{3,2,1,0:T(8,128)(2,1)}, bf16[1,6,256,128]{3,2,1,0:T(8,128)(2,1)}, u32[]{:S(2)}, u32[]{:S(2)}) %collective-permute-start.13) | collective-permute-done | bytes 393248 | tf_op jit(solution)/shard_map/ppermute | solution.py:258
  129.1 6.0 %all-to-all-start = ((bf16[8,2,2,256,128]{4,3,2,1,0:T(8,128)(2,1)}), bf16[8,2,2,256,128]{4,3,2,1,0:T(8,128)(2,1)S(1)}, u32[]{:S(2)}, u32[]{:S(2)}) async-start(bf16[8,2,2,256,128]{4,3,2,1,0:T(8,128)(2,1)} %attend.2), calls=%async_computation | async-start | bytes 4194304 | tf_op jit(solution)/shard_map/all_to_all | solution.py:275
  135.1 4.2 %attend.3 = (bf16[1,2,256,128]{3,2,1,0:T(8,128)(2,1)S(1)}, bf16[1,2,256,128]{3,2,1,0:T(8,128)(2,1)S(1)}, bf16[1,2,256,128]{3,2,1,0:T(8,128)(2,1)S(1)}, bf16[1,2,...) custom-call(s32[2]{0:T(128)S(1)} %pad_add_fusion.info, ...), custom_call_target="tpu_custom_call" | custom-call | tf_op jit(solution)/shard_map/attend/pallas_call | solution.py:166
  143.3 2.0 %collective-permute-start.18 = (bf16[1,2,256,128]{3,2,1,0:T(8,128)(2,1)S(1)}, bf16[1,2,256,128]{3,2,1,0:T(8,128)(2,1)S(1)}, u32[]{:S(2)}, u32[]{:S(2)}) collective-permute-start(bf16[1,2,256,128]{3,2,1,0:T(8,128)(2,1)S(1)} %get-tuple-element.90), channel_id=1, source_target_pairs={{0,5},{1,4},{2,7},{3,6},{4,1},{5,0},{6,3},{7,2},{8,13},{9,12},{10,... | collective-permute-start | bytes 393224 | tf_op jit(solution)/shard_map/ppermute | solution.py:258
  145.9 15.9 %collective-permute-done.15.refs_2_ = bf16[1,2,256,128]{3,2,1,0:T(8,128)(2,1)S(1)} collective-permute-done((bf16[1,2,256,128]{3,2,1,0:T(8,128)(2,1)S(1)}, bf16[1,2,256,128]{3,2,1,0:T(8,128)(2,1)S(1)}, u32[]{:S(2)}, u32[]{:S(2)}) %collective-permute-start.15) | collective-permute-done | bytes 131104 | tf_op jit(solution)/shard_map/ppermute | solution.py:258
  161.8 3.3 %collective-permute-start.20 = (bf16[1,2,256,128]{3,2,1,0:T(8,128)(2,1)S(1)}, bf16[1,2,256,128]{3,2,1,0:T(8,128)(2,1)S(1)}, u32[]{:S(2)}, u32[]{:S(2)}) collective-permute-start(bf16[1,2,256,128]{3,2,1,0:T(8,128)(2,1)S(1)} %get-tuple-element.92), channel_id=1, source_target_pairs={{0,7},{1,6},{2,1},{3,0},{4,3},{5,2},{6,5},{7,4},{8,15},{9,14},{10,... | collective-permute-start | bytes 393224 | tf_op jit(solution)/shard_map/ppermute | solution.py:258
  168.2 3.0 %collective-permute-done.20.refs_7_ = bf16[1,2,256,128]{3,2,1,0:T(8,128)(2,1)S(1)} collective-permute-done((bf16[1,2,256,128]{3,2,1,0:T(8,128)(2,1)S(1)}, bf16[1,2,256,128]{3,2,1,0:T(8,128)(2,1)S(1)}, u32[]{:S(2)}, u32[]{:S(2)}) %collective-permute-start.20) | collective-permute-done | bytes 131104 | tf_op jit(solution)/shard_map/ppermute | solution.py:258
  171.2 18.1 %project.1 = (bf16[256,3072]{1,0:T(8,128)(2,1)}, bf16[256,3072]{1,0:T(8,128)(2,1)}) custom-call(bf16[8,2,2,256,128]{4,3,2,1,0:T(8,128)(2,1)S(1)} %all-to-all-done.moved, bf16[1,2,256,128]{3,2,1,0:T(8,128)(2,1)S(1)} %get-tuple-element.85.refs_0_, bf16[1,2,256,128]{3,2,1,0:T(8,128)(2,1)S(1)} %collective-permute-done.14.refs_1_, ...), custom_call_target="tpu_custom_call" | custom-call | tf_op jit(solution)/shard_map/project/pallas_call | solution.py:234
  (67 shorter events, 22.3 us)
Async XLA Ops:
  7.2 164.0 %all-gather.2.cloned.1.call-start = ((), (), s32[]{:S(2)}) async-start(), calls=%async_computation.1 | async-start | bytes 20054016 | tf_op jit(solution)/shard_map/all_gather | solution.py:297
  7.2 10.6 %collective-permute-start.22 = (bf16[24,3072]{1,0:T(8,128)(2,1)}, bf16[24,3072]{1,0:T(8,128)(2,1)S(1)}, u32[]{:S(2)}, u32[]{:S(2)}) collective-permute-start(bf16[24,3072]{1,0:T(8,128)(2,1)} %param.16), channel_id=1, source_target_pairs={{0,4},{1,5},{2,6},{3,7},{4,0},{5,1},{6,2},{7,3},{8,12},{9,13},{10,... | collective-permute-start | bytes 442376 | tf_op jit(solution)/shard_map/ppermute | solution.py:258
  9.1 8.8 %collective-permute-start.21 = (bf16[24,3072]{1,0:T(8,128)(2,1)}, bf16[24,3072]{1,0:T(8,128)(2,1)S(1)}, u32[]{:S(2)}, u32[]{:S(2)}) collective-permute-start(bf16[24,3072]{1,0:T(8,128)(2,1)} %param.16), channel_id=1, source_target_pairs={{0,6},{1,7},{2,0},{3,1},{4,2},{5,3},{6,4},{7,5},{8,14},{9,15},{10,... | collective-permute-start | bytes 442376 | tf_op jit(solution)/shard_map/ppermute | solution.py:258
  22.7 19.1 %collective-permute-start.1 = (bf16[2,6,256,128]{3,2,1,0:T(8,128)(2,1)}, bf16[2,6,256,128]{3,2,1,0:T(8,128)(2,1)S(1)}, u32[]{:S(2)}, u32[]{:S(2)}) collective-permute-start(bf16[2,6,256,128]{3,2,1,0:T(8,128)(2,1)} %get-tuple-element.59), channel_id=1, source_target_pairs={{0,2},{1,3},{2,4},{3,5},{4,6},{5,7},{6,0},{7,1},{8,10},{9,11},{10,... | collective-permute-start | bytes 2359304 | tf_op jit(solution)/shard_map/ppermute | solution.py:258
  23.0 22.9 %collective-permute-start.2 = (bf16[2,6,256,128]{3,2,1,0:T(8,128)(2,1)}, bf16[2,6,256,128]{3,2,1,0:T(8,128)(2,1)S(1)}, u32[]{:S(2)}, u32[]{:S(2)}) collective-permute-start(bf16[2,6,256,128]{3,2,1,0:T(8,128)(2,1)} %get-tuple-element.60), channel_id=1, source_target_pairs={{0,4},{1,5},{2,6},{3,7},{4,0},{5,1},{6,2},{7,3},{8,12},{9,13},{10,... | collective-permute-start | bytes 2359304 | tf_op jit(solution)/shard_map/ppermute | solution.py:258
  25.7 41.3 %collective-permute-start.3 = (bf16[2,6,256,128]{3,2,1,0:T(8,128)(2,1)}, bf16[2,6,256,128]{3,2,1,0:T(8,128)(2,1)S(1)}, u32[]{:S(2)}, u32[]{:S(2)}) collective-permute-start(bf16[2,6,256,128]{3,2,1,0:T(8,128)(2,1)} %get-tuple-element.61), channel_id=1, source_target_pairs={{0,6},{1,7},{2,0},{3,1},{4,2},{5,3},{6,4},{7,5},{8,14},{9,15},{10,... | collective-permute-start | bytes 2359304 | tf_op jit(solution)/shard_map/ppermute | solution.py:258
  27.2 39.9 %collective-permute-start = (bf16[2,6,256,128]{3,2,1,0:T(8,128)(2,1)}, bf16[2,6,256,128]{3,2,1,0:T(8,128)(2,1)}, u32[]{:S(2)}, u32[]{:S(2)}) collective-permute-start(bf16[2,6,256,128]{3,2,1,0:T(8,128)(2,1)} %get-tuple-element.50), channel_id=1, source_target_pairs={{0,1},{1,0},{2,3},{3,2},{4,5},{5,4},{6,7},{7,6},{8,9},{9,8},{10,11... | collective-permute-start | bytes 2359304 | tf_op jit(solution)/shard_map/ppermute | solution.py:258
  28.4 48.8 %collective-permute-start.4 = (bf16[2,6,256,128]{3,2,1,0:T(8,128)(2,1)}, bf16[2,6,256,128]{3,2,1,0:T(8,128)(2,1)}, u32[]{:S(2)}, u32[]{:S(2)}) collective-permute-start(bf16[2,6,256,128]{3,2,1,0:T(8,128)(2,1)} %get-tuple-element.63), channel_id=1, source_target_pairs={{0,3},{1,2},{2,5},{3,4},{4,7},{5,6},{6,1},{7,0},{8,11},{9,10},{10,... | collective-permute-start | bytes 2359304 | tf_op jit(solution)/shard_map/ppermute | solution.py:258
  41.8 37.5 %collective-permute-start.5 = (bf16[2,6,256,128]{3,2,1,0:T(8,128)(2,1)}, bf16[2,6,256,128]{3,2,1,0:T(8,128)(2,1)}, u32[]{:S(2)}, u32[]{:S(2)}) collective-permute-start(bf16[2,6,256,128]{3,2,1,0:T(8,128)(2,1)} %get-tuple-element.65), channel_id=1, source_target_pairs={{0,5},{1,4},{2,7},{3,6},{4,1},{5,0},{6,3},{7,2},{8,13},{9,12},{10,... | collective-permute-start | bytes 2359304 | tf_op jit(solution)/shard_map/ppermute | solution.py:258
  45.9 49.9 %collective-permute-start.6 = (bf16[2,6,256,128]{3,2,1,0:T(8,128)(2,1)}, bf16[2,6,256,128]{3,2,1,0:T(8,128)(2,1)}, u32[]{:S(2)}, u32[]{:S(2)}) collective-permute-start(bf16[2,6,256,128]{3,2,1,0:T(8,128)(2,1)} %get-tuple-element.67), channel_id=1, source_target_pairs={{0,7},{1,6},{2,1},{3,0},{4,3},{5,2},{6,5},{7,4},{8,15},{9,14},{10,... | collective-permute-start | bytes 2359304 | tf_op jit(solution)/shard_map/ppermute | solution.py:258
  67.0 31.7 %collective-permute-start.7 = (bf16[1,6,256,128]{3,2,1,0:T(8,128)(2,1)}, bf16[1,6,256,128]{3,2,1,0:T(8,128)(2,1)S(1)}, u32[]{:S(2)}, u32[]{:S(2)}) collective-permute-start(bf16[1,6,256,128]{3,2,1,0:T(8,128)(2,1)} %get-tuple-element.69), channel_id=1, source_target_pairs={{0,1},{1,0},{2,3},{3,2},{4,5},{5,4},{6,7},{7,6},{8,9},{9,8},{10,11... | collective-permute-start | bytes 1179656 | tf_op jit(solution)/shard_map/ppermute | solution.py:258
  67.1 33.8 %collective-permute-start.8 = (bf16[1,6,256,128]{3,2,1,0:T(8,128)(2,1)}, bf16[1,6,256,128]{3,2,1,0:T(8,128)(2,1)S(1)}, u32[]{:S(2)}, u32[]{:S(2)}) collective-permute-start(bf16[1,6,256,128]{3,2,1,0:T(8,128)(2,1)} %get-tuple-element.70), channel_id=1, source_target_pairs={{0,2},{1,3},{2,4},{3,5},{4,6},{5,7},{6,0},{7,1},{8,10},{9,11},{10,... | collective-permute-start | bytes 1179656 | tf_op jit(solution)/shard_map/ppermute | solution.py:258
  77.2 38.7 %collective-permute-start.9 = (bf16[1,6,256,128]{3,2,1,0:T(8,128)(2,1)}, bf16[1,6,256,128]{3,2,1,0:T(8,128)(2,1)}, u32[]{:S(2)}, u32[]{:S(2)}) collective-permute-start(bf16[1,6,256,128]{3,2,1,0:T(8,128)(2,1)} %get-tuple-element.71), channel_id=1, source_target_pairs={{0,3},{1,2},{2,5},{3,4},{4,7},{5,6},{6,1},{7,0},{8,11},{9,10},{10,... | collective-permute-start | bytes 1179656 | tf_op jit(solution)/shard_map/ppermute | solution.py:258
  79.3 36.6 %collective-permute-start.10 = (bf16[1,6,256,128]{3,2,1,0:T(8,128)(2,1)}, bf16[1,6,256,128]{3,2,1,0:T(8,128)(2,1)}, u32[]{:S(2)}, u32[]{:S(2)}) collective-permute-start(bf16[1,6,256,128]{3,2,1,0:T(8,128)(2,1)} %get-tuple-element.72), channel_id=1, source_target_pairs={{0,4},{1,5},{2,6},{3,7},{4,0},{5,1},{6,2},{7,3},{8,12},{9,13},{10,... | collective-permute-start | bytes 1179656 | tf_op jit(solution)/shard_map/ppermute | solution.py:258
  95.9 20.0 %collective-permute-start.11 = (bf16[1,6,256,128]{3,2,1,0:T(8,128)(2,1)}, bf16[1,6,256,128]{3,2,1,0:T(8,128)(2,1)}, u32[]{:S(2)}, u32[]{:S(2)}) collective-permute-start(bf16[1,6,256,128]{3,2,1,0:T(8,128)(2,1)} %get-tuple-element.73), channel_id=1, source_target_pairs={{0,5},{1,4},{2,7},{3,6},{4,1},{5,0},{6,3},{7,2},{8,13},{9,12},{10,... | collective-permute-start | bytes 1179656 | tf_op jit(solution)/shard_map/ppermute | solution.py:258
  98.7 21.9 %collective-permute-start.12 = (bf16[1,6,256,128]{3,2,1,0:T(8,128)(2,1)}, bf16[1,6,256,128]{3,2,1,0:T(8,128)(2,1)}, u32[]{:S(2)}, u32[]{:S(2)}) collective-permute-start(bf16[1,6,256,128]{3,2,1,0:T(8,128)(2,1)} %get-tuple-element.74), channel_id=1, source_target_pairs={{0,6},{1,7},{2,0},{3,1},{4,2},{5,3},{6,4},{7,5},{8,14},{9,15},{10,... | collective-permute-start | bytes 1179656 | tf_op jit(solution)/shard_map/ppermute | solution.py:258
  101.6 27.5 %collective-permute-start.13 = (bf16[1,6,256,128]{3,2,1,0:T(8,128)(2,1)}, bf16[1,6,256,128]{3,2,1,0:T(8,128)(2,1)}, u32[]{:S(2)}, u32[]{:S(2)}) collective-permute-start(bf16[1,6,256,128]{3,2,1,0:T(8,128)(2,1)} %get-tuple-element.75), channel_id=1, source_target_pairs={{0,7},{1,6},{2,1},{3,0},{4,3},{5,2},{6,5},{7,4},{8,15},{9,14},{10,... | collective-permute-start | bytes 1179656 | tf_op jit(solution)/shard_map/ppermute | solution.py:258
  129.1 42.1 %all-to-all-start = ((bf16[8,2,2,256,128]{4,3,2,1,0:T(8,128)(2,1)}), bf16[8,2,2,256,128]{4,3,2,1,0:T(8,128)(2,1)S(1)}, u32[]{:S(2)}, u32[]{:S(2)}) async-start(bf16[8,2,2,256,128]{4,3,2,1,0:T(8,128)(2,1)} %attend.2), calls=%async_computation | async-start | bytes 4194304 | tf_op jit(solution)/shard_map/all_to_all | solution.py:275
  139.7 22.0 %collective-permute-start.15 = (bf16[1,2,256,128]{3,2,1,0:T(8,128)(2,1)S(1)}, bf16[1,2,256,128]{3,2,1,0:T(8,128)(2,1)S(1)}, u32[]{:S(2)}, u32[]{:S(2)}) collective-permute-start(bf16[1,2,256,128]{3,2,1,0:T(8,128)(2,1)S(1)} %get-tuple-element.87), channel_id=1, source_target_pairs={{0,2},{1,3},{2,4},{3,5},{4,6},{5,7},{6,0},{7,1},{8,10},{9,11},{10,... | collective-permute-start | bytes 393224 | tf_op jit(solution)/shard_map/ppermute | solution.py:258
  140.9 24.2 %collective-permute-start.16 = (bf16[1,2,256,128]{3,2,1,0:T(8,128)(2,1)S(1)}, bf16[1,2,256,128]{3,2,1,0:T(8,128)(2,1)S(1)}, u32[]{:S(2)}, u32[]{:S(2)}) collective-permute-start(bf16[1,2,256,128]{3,2,1,0:T(8,128)(2,1)S(1)} %get-tuple-element.88), channel_id=1, source_target_pairs={{0,3},{1,2},{2,5},{3,4},{4,7},{5,6},{6,1},{7,0},{8,11},{9,10},{10,... | collective-permute-start | bytes 393224 | tf_op jit(solution)/shard_map/ppermute | solution.py:258
  142.1 23.0 %collective-permute-start.17 = (bf16[1,2,256,128]{3,2,1,0:T(8,128)(2,1)S(1)}, bf16[1,2,256,128]{3,2,1,0:T(8,128)(2,1)S(1)}, u32[]{:S(2)}, u32[]{:S(2)}) collective-permute-start(bf16[1,2,256,128]{3,2,1,0:T(8,128)(2,1)S(1)} %get-tuple-element.89), channel_id=1, source_target_pairs={{0,4},{1,5},{2,6},{3,7},{4,0},{5,1},{6,2},{7,3},{8,12},{9,13},{10,... | collective-permute-start | bytes 393224 | tf_op jit(solution)/shard_map/ppermute | solution.py:258
  143.3 23.3 %collective-permute-start.18 = (bf16[1,2,256,128]{3,2,1,0:T(8,128)(2,1)S(1)}, bf16[1,2,256,128]{3,2,1,0:T(8,128)(2,1)S(1)}, u32[]{:S(2)}, u32[]{:S(2)}) collective-permute-start(bf16[1,2,256,128]{3,2,1,0:T(8,128)(2,1)S(1)} %get-tuple-element.90), channel_id=1, source_target_pairs={{0,5},{1,4},{2,7},{3,6},{4,1},{5,0},{6,3},{7,2},{8,13},{9,12},{10,... | collective-permute-start | bytes 393224 | tf_op jit(solution)/shard_map/ppermute | solution.py:258
  145.3 22.8 %collective-permute-start.19 = (bf16[1,2,256,128]{3,2,1,0:T(8,128)(2,1)S(1)}, bf16[1,2,256,128]{3,2,1,0:T(8,128)(2,1)S(1)}, u32[]{:S(2)}, u32[]{:S(2)}) collective-permute-start(bf16[1,2,256,128]{3,2,1,0:T(8,128)(2,1)S(1)} %get-tuple-element.91), channel_id=1, source_target_pairs={{0,6},{1,7},{2,0},{3,1},{4,2},{5,3},{6,4},{7,5},{8,14},{9,15},{10,... | collective-permute-start | bytes 393224 | tf_op jit(solution)/shard_map/ppermute | solution.py:258
  161.8 9.4 %collective-permute-start.20 = (bf16[1,2,256,128]{3,2,1,0:T(8,128)(2,1)S(1)}, bf16[1,2,256,128]{3,2,1,0:T(8,128)(2,1)S(1)}, u32[]{:S(2)}, u32[]{:S(2)}) collective-permute-start(bf16[1,2,256,128]{3,2,1,0:T(8,128)(2,1)S(1)} %get-tuple-element.92), channel_id=1, source_target_pairs={{0,7},{1,6},{2,1},{3,0},{4,3},{5,2},{6,5},{7,4},{8,15},{9,14},{10,... | collective-permute-start | bytes 393224 | tf_op jit(solution)/shard_map/ppermute | solution.py:258
  (11 other events, 394.7 us)
Sparse Core Ops, SparseCore 0:
  22.8 124.2 all-gather.1
